TPU v7x, 256 devices: a whole 4x4x8 slice. The times are simulated.
256 devices in a mesh: seq: 32 (over y, z), head: 8 (over x, core).
Axes of the slice: x: 4, y: 4, z: 8, core: 2. Of those that a mesh axis runs over, the one named last changes fastest.
Arguments:
- inputs: bfloat16 [65536, 32, 64], P('seq', 'head'), may hold values from -0.3984375 to 0.3984375
- log_decay: float32 [65536, 32], P('seq', 'head'), may hold values from -1.1 to 0, as said below
- in_proj: bfloat16 [65536, 2, 128], P('seq'), may hold values from -0.5 to 0.5
- out_proj: bfloat16 [65536, 2, 128], P('seq'), may hold values from -6 to 6
- upstream: bfloat16 [65536, 32, 64], P('seq', 'head'), may hold values from -0.15917969 to 0.15917969
Outputs:
- grad_inputs: bfloat16 [65536, 32, 64], P('seq', 'head')
- grad_log_decay: float32 [65536, 32], P('seq', 'head')
- grad_in_proj: float32 [65536, 2, 128], P(('seq', 'head'))
- grad_out_proj: float32 [65536, 2, 128], P(('seq', 'head'))
Inputs may be any that keep to these rules, and one draw needn't show every extreme that they name: `log_decay`: each entry is negative.
All inputs are finite; a program needn't handle non-finite values.
Results may differ from a plain program's by a relative error of at most 0.0012.
Values sent between devices are 32-bit elements; how exact they have to be, the bound alone decides.
No kernel may reach another device: no remote copies, remote signals or barrier semaphores. Data moves between devices by JAX's collectives and lax.ppermute only.
A program may use at most 128 MiB of HBM per device.

v0:
```python
import jax
import jax.numpy as jnp
from jax import lax
from jax.sharding import PartitionSpec as P

HEAD_PER_GROUP = 16
SPAN = 128


finest = lax.Precision.HIGHEST


def split_blocks(values, log_rates, in_group, out_group):
    blocks = values.shape[0] // SPAN
    blocked = values.reshape(blocks, SPAN, values.shape[1], values.shape[2])
    cumulative = jnp.cumsum(log_rates.reshape(blocks, SPAN, log_rates.shape[1]), axis=1)
    return (
        blocked,
        cumulative,
        in_group.reshape(blocks, SPAN, in_group.shape[1]),
        out_group.reshape(blocks, SPAN, out_group.shape[1]),
    )


def block_states(blocked, cumulative, incoming_segments):
    tail = jnp.exp(cumulative[:, -1:, :] - cumulative)
    states = jnp.einsum(
        "kjn,kjhp->khnp", incoming_segments, blocked * tail[..., None], precision=finest
    )
    return (states, jnp.exp(cumulative[:, -1, :]))


def run_chain(start, totals, states):

    def advance(carried, item):
        return (item[0][:, None, None] * carried + item[1], carried)

    return lax.scan(advance, start, (totals, states))


def block_output(values, log_rates, in_group, out_group, start):
    blocked, cumulative, incoming_segments, out_blocks = split_blocks(
        values, log_rates, in_group, out_group
    )
    states, totals = block_states(blocked, cumulative, incoming_segments)
    final, initial = run_chain(start, totals, states)
    scores = jnp.einsum("kin,kjn->kij", out_blocks, incoming_segments, precision=finest)
    across = jnp.transpose(cumulative, (0, 2, 1))
    spread = across[:, :, :, None] - across[:, :, None, :]
    lower = lax.broadcasted_iota(jnp.int32, (SPAN, SPAN), 0) >= lax.broadcasted_iota(
        jnp.int32, (SPAN, SPAN), 1
    )
    decay = jnp.where(lower, jnp.exp(jnp.where(lower, spread, 0.0)), 0.0)
    within = jnp.einsum("khij,kjhp->kihp", scores[:, None] * decay, blocked, precision=finest)
    carried = (
        jnp.einsum("kin,khnp->kihp", out_blocks, initial, precision=finest)
        * jnp.exp(cumulative)[..., None]
    )
    return ((within + carried).reshape(values.shape), final)


def local(inputs, log_decay, in_proj, out_proj, upstream):
    heads_here = inputs.shape[1]
    group = lax.axis_index("head") * heads_here // HEAD_PER_GROUP
    in_group = lax.dynamic_index_in_dim(in_proj, group, 1, keepdims=False).astype(jnp.float32)
    out_group = lax.dynamic_index_in_dim(out_proj, group, 1, keepdims=False).astype(jnp.float32)
    values = inputs.astype(jnp.float32)
    grads_out = upstream.astype(jnp.float32)
    blocked, cumulative, incoming_segments, out_blocks = split_blocks(
        values, log_decay, in_group, out_group
    )
    states, totals = block_states(blocked, cumulative, incoming_segments)
    empty = jnp.zeros((heads_here, in_proj.shape[2], inputs.shape[2]), jnp.float32)
    own_state, unused = run_chain(empty, totals, states)
    own_log = jnp.sum(log_decay, axis=0)
    running = jnp.exp(jnp.cumsum(log_decay, axis=0))
    own_grad = jnp.einsum(
        "tn,thp->hnp", out_group, grads_out * running[..., None], precision=finest
    )
    logs_all, states_all = (
        lax.all_gather(own_log[None], "seq", axis=0, tiled=True),
        lax.all_gather(own_state[None], "seq", axis=0, tiled=True),
    )
    grad_logs, grads_all = (
        lax.all_gather(own_log[None], "seq", axis=0, tiled=True),
        lax.all_gather(own_grad[None], "seq", axis=0, tiled=True),
    )
    position = lax.axis_index("seq")
    order = lax.broadcasted_iota(jnp.int32, logs_all.shape, 0)
    earlier = order < position
    later = order > position
    before = jnp.sum(jnp.where(earlier, logs_all, 0.0), axis=0)
    inclusive = jnp.cumsum(logs_all, axis=0)
    forward_weight = jnp.where(
        earlier, jnp.exp(jnp.where(earlier, before[None] - inclusive, 0.0)), 0.0
    )
    entering = jnp.einsum("eh,ehnp->hnp", forward_weight, states_all, precision=finest)
    through = before + own_log
    exclusive = jnp.cumsum(grad_logs, axis=0) - grad_logs
    backward_weight = jnp.where(
        later, jnp.exp(jnp.where(later, exclusive - through[None], 0.0)), 0.0
    )
    leaving = jnp.einsum("eh,ehnp->hnp", backward_weight, grads_all, precision=finest)

    def closed(first, second, third, fourth):
        return block_output(first, second, third, fourth, entering)

    outputs, pullback = jax.vjp(closed, values, log_decay, in_group, out_group)
    grad_values, rate_gradient, grad_in, grad_out = pullback((grads_out, leaving))
    onehot = (jnp.arange(in_proj.shape[1]) == group).astype(jnp.float32)
    partial_in = onehot[None, :, None] * grad_in[:, None, :]
    partial_out = onehot[None, :, None] * grad_out[:, None, :]
    summed_in, summed_out = (
        lax.psum_scatter(partial_in, "head", scatter_dimension=0, tiled=True),
        lax.psum_scatter(partial_out, "head", scatter_dimension=0, tiled=True),
    )
    return (grad_values.astype(jnp.bfloat16), rate_gradient, summed_in, summed_out)


def solution(mesh):
    in_specs = (
        P("seq", "head", None),
        P("seq", "head"),
        P("seq", None, None),
        P("seq", None, None),
        P("seq", "head", None),
    )
    out_specs = (
        P("seq", "head", None),
        P("seq", "head"),
        P(("seq", "head"), None, None),
        P(("seq", "head"), None, None),
    )
    return jax.shard_map(local, mesh=mesh, in_specs=in_specs, out_specs=out_specs, check_vma=False)
```

profile of v0, /device:TPU:32, one launch (start us, length us, event | category | flops | bytes accessed | tf_op | source)
XLA Modules:
  0.0 377.3 jit_solution(6580400537287853477)
XLA Ops:
  9.7 4.3 %constant_dynamic-slice_fusion.5 = (bf16[2048,1,128]{2,1,0:T(2,128)(2,1)}, bf16[2048,1,128]{2,1,0:T(2,128)(2,1)S(1)}) fusion(bf16[2048,2,128]{2,1,0:T(2,128)(2,1)} %param.13, s32[]{:T(128)S(6)} %select_n.41, bf16[2048,2,128]{2,1,0:T(2,128)(2,1)} %param.14), kind=kLoop, calls=%fused_computation.102 | loop fusion | bytes 2097156 | tf_op jit(solution)/shard_map/jit(dynamic_index_in_dim)/dynamic_slice | solution.py:65
  14.1 1.8 fusion.43
  16.0 1.4 copy.98
  17.4 1.4 fusion.65
  19.5 1.3 copy.161
  20.8 2.6 fusion.28
  23.4 3.8 copy.109
  27.1 17.4 %while.45 = (s32[]{:T(128)}, f32[4,128,64]{2,1,0:T(8,128)S(1)}, f32[16,4]{1,0:T(8,128)S(1)}, f32[16,4,128,64]{3,2,1,0:T(8,128)}, s32[]{:T(128)}, /*index=5*/s32[]{:T(128)}) while((s32[]{:T(128)}, f32[4,128,64]{2,1,0:T(8,128)S(1)}, f32[16,4]{1,0:T(8,128)S(1)}, f32[16,4,128,64]{3,2,1,0:T(8,128)}, s32[]{:T(128)}, ...), condition=%wide.region_7.8_spmd.clone, body=%wide.region_6.7_spmd.clone.sunk | while | flops 98307 | bytes 393359 | solution.py:38
  47.7 74.1 %all-reduce.2 = f32[128]{0:T(128)S(1)} all-reduce(f32[128]{0:T(128)S(1)} %dynamic-update-slice), channel_id=2, replica_groups=mesh['seq'=32,'head'=8] {'seq'}, use_global_device_ids=true, to_apply=%add.2 | all-reduce | flops 128 | bytes 1024
  122.6 2.9 convert_bitcast_fusion
  126.6 1.4 copy-done.1
  128.1 2.9 fusion.29
  131.0 4.9 %fusion.13 = (f32[16,4,128]{2,1,0:T(4,128)S(1)}, f32[16,4,128]{2,1,0:T(4,128)S(1)}, f32[16,128,128]{2,1,0:T(8,128)}) fusion(f32[16,4,128]{2,1,0:T(4,128)S(1)} %copy.99, f32[16,128,128]{2,1,0:T(8,128)S(1)} %fusion.67, pred[128,128]{1,0:T(8,128)(4,1)S(1)} %iota_compare_fusion, bf16[2048,4,64]{0,2,1:T(8,128)(2,1)S(1)} %copy-done, ...), kind=kOutput, calls=%fused_computation.31 | convolution fusion | flops 145473536 | bytes 4308992 | tf_op jit(solution)/shard_map/transpose(jvp(khij,kjhp->kihp))/dot_general | solution.py:54
  136.0 2.5 multiply_reduce_fusion.1
  138.6 44.3 %all-gather.8.cloned.1.call-done = f32[128,128,64]{1,2,0:T(8,128)} async-done(((f32[4,128,64]{1,2,0:T(8,128)}), f32[128,128,64]{1,2,0:T(8,128)}) %all-gather.8.cloned.1.call-update) | async-done | bytes 4194320 | tf_op jit(solution)/shard_map/all_gather | solution.py:82
  182.9 2.5 multiply_reduce_fusion
  185.6 2.5 broadcast.30.clone
  188.1 29.6 %while.43 = (s32[]{:T(128)}, f32[4,128,64]{2,1,0:T(8,128)S(1)}, f32[16,4,128,64]{3,2,1,0:T(8,128)}, f32[16,4,1,1]{1,3,2,0:T(1,128)S(1)}, f32[16,4]{1,0:T(8,128)S(1)}, /*index=5*/f32[16,4,128,64]{3,2,1,0:T(8,128)}, s32[]{:T(128)}) while((s32[]{:T(128)}, f32[4,128,64]{2,1,0:T(8,128)S(1)}, f32[16,4,128,64]{3,2,1,0:T(8,128)}, ...), condition=%wide.region_9.10_spmd, body=%wide.region_8.9_spmd.sunk | while | flops 65538 | bytes 787605 | solution.py:38
  217.7 11.2 %fusion.34 = f32[16,128,128]{2,1,0:T(8,128)} fusion(f32[16,4,128,64]{3,2,1,0:T(8,128)} %get-tuple-element.500, f32[16,128,4,64]{1,0,3,2:T(8,128)} %copy-done.1), kind=kOutput, calls=%fused_computation.50 | convolution fusion | flops 805306368 | bytes 5242880 | tf_op jit(solution)/shard_map/transpose(jvp(kin,khnp->kihp))/dot_general | solution.py:56
  228.9 2.4 broadcast.30
  231.3 47.2 %while.44 = (s32[]{:T(128)}, f32[4,128,64]{2,1,0:T(8,128)S(1)}, f32[16,4]{1,0:T(8,128)S(1)}, f32[16,4,128,64]{3,2,1,0:T(8,128)}, f32[16,4,128,64]{2,3,1,0:T(8,12...) while((s32[]{:T(128)}, f32[4,128,64]{2,1,0:T(8,128)S(1)}, ...), condition=%wide.region_12.13_spmd, body=%wide.region_10.12_spmd.sunk | while | flops 131071 | bytes 1442021 | solution.py:38
  278.6 9.1 %fusion.40 = f32[16,128,128]{2,1,0:T(8,128)S(1)} fusion(f32[16,4,128,64]{3,2,1,0:T(8,128)} %get-tuple-element.204, f32[16,128,4]{1,2,0:T(4,128)S(1)} %copy.107, bf16[2048,4,64]{0,2,1:T(8,128)(2,1)S(1)} %copy-done), kind=kOutput, calls=%fused_computation.52 | convolution fusion | flops 806354944 | bytes 4227072 | tf_op jit(solution)/shard_map/transpose(jvp(kjn,kjhp->khnp))/dot_general | solution.py:27
  289.4 3.0 broadcast_multiply_fusion
  294.3 3.8 %copy.116 = f32[16,4,128,64]{2,3,1,0:T(8,128)} copy(f32[16,4,128,64]{3,2,1,0:T(8,128)} %get-tuple-element.530) | data formatting | bytes 4194304 | tf_op jit(solution)/shard_map/jvp()/while | solution.py:38
  298.3 6.0 %fusion.14 = (f32[16,128,4]{1,2,0:T(4,128)S(1)}, f32[16,128,4,64]{1,3,2,0:T(8,128)S(1)}) fusion(bf16[16,128,128,1]{2,1,3,0:T(8,128)(2,1)S(1)} %bitcast.227, f32[16,4,128,64]{3,2,1,0:T(8,128)} %get-tuple-element.204, bf16[2048,4,64]{0,2,1:T(8,128)(2,1)S(1)} %copy-done), kind=kOutput, calls=%fused_computation.32 | convolution fusion | flops 806871040 | bytes 5799936 | tf_op jit(solution)/shard_map/transpose(jvp(kjn,kjhp->khnp))/dot_general | solution.py:27
  304.4 3.6 fusion.37
  308.0 1.2 copy.224
  309.7 3.5 fusion.15
  313.8 23.3 %fusion.66 = f32[16,128,4]{2,0,1:T(8,128)S(1)} fusion(f32[16,128,4]{2,0,1:T(8,128)S(1)} %copy.128), kind=kOutput, calls=%fused_computation.107 | output fusion | flops 1040384 | bytes 65536 | tf_op jit(solution)/shard_map/transpose(jvp(jit(cumsum)))/reduce_window_sum | solution.py:16
  338.2 29.3 %all-reduce.8.cloned.1.call-done = (f32[2048,2,128]{2,1,0:T(2,128)}, f32[2048,2,128]{2,1,0:T(2,128)}) async-done(((f32[2048,2,128]{2,1,0:T(2,128)}, f32[2048,2,128]{2,1,0:T(2,128)}), (f32[2048,2,128]{2,1,0:T(2,128)}, f32[2048,2,128]{2,1,0:T(2,128)})) %all-reduce.8.cloned.1.call-update) | async-done | bytes 4194320
  367.4 1.7 constant_dynamic-slice_fusion.4
  369.1 1.7 constant_dynamic-slice_fusion.3
  (269 shorter events, 105.7 us)
Async XLA Ops:
  7.2 13.6 %copy-start = (bf16[2048,4,64]{0,2,1:T(8,128)(2,1)S(1)}, bf16[2048,4,64]{0,2,1:T(8,128)(2,1)}, u32[]{:S(2)}) copy-start(bf16[2048,4,64]{0,2,1:T(8,128)(2,1)} %param.11) | copy-start | bytes 3145732
  7.2 128.8 %all-gather.6.cloned.1.call-start = ((), (), s32[]{:S(2)}) async-start(), calls=%async_computation | async-start | bytes 4325376 | tf_op jit(solution)/shard_map/all_gather | solution.py:86
  9.7 4.4 %copy-start.4 = (bf16[2048,4,64]{0,2,1:T(8,128)(2,1)S(1)}, bf16[2048,4,64]{0,2,1:T(8,128)(2,1)}, u32[]{:S(2)}) copy-start(bf16[2048,4,64]{0,2,1:T(8,128)(2,1)} %param.15) | copy-start | bytes 3145732
  15.9 167.0 %all-gather.8.cloned.1.call-start = ((), (), s32[]{:S(2)}) async-start(), calls=%async_computation.1 | async-start | bytes 4325376 | tf_op jit(solution)/shard_map/all_gather | solution.py:82
  27.1 19.1 %copy-start.10 = (u32[256]{0:T(256)S(1)}, u32[256]{0:T(256)}, u32[]{:S(2)}) copy-start(u32[256]{0:T(256)} %constant.135) | copy-start | bytes 3076
  45.3 322.1 %all-reduce.8.cloned.1.call-start = ((), (), s32[]{:S(2)}) async-start(), calls=%async_computation.2 | async-start | bytes 8388608
  126.5 4.6 %copy-start.7 = (f32[16,128,128]{2,1,0:T(8,128)}, f32[16,128,128]{2,1,0:T(8,128)S(1)}, u32[]{:S(2)}) copy-start(f32[16,128,128]{2,1,0:T(8,128)S(1)} %fusion.67) | copy-start | bytes 3145732
  126.6 1.5 copy-start.1
  128.1 2.9 copy-start.5
  278.5 9.1 %copy-start.2 = (f32[16,128,128]{2,1,0:T(8,128)S(1)}, f32[16,128,128]{2,1,0:T(8,128)}, u32[]{:S(2)}) copy-start(f32[16,128,128]{2,1,0:T(8,128)} %get-tuple-element.291) | copy-start | bytes 3145732
  278.5 9.1 %copy-start.3 = (f32[16,128,128]{2,1,0:T(8,128)S(1)}, f32[16,128,128]{2,1,0:T(8,128)}, u32[]{:S(2)}) copy-start(f32[16,128,128]{2,1,0:T(8,128)} %fusion.34) | copy-start | bytes 3145732
  292.4 0.7 copy-start.9
  298.3 6.1 %copy-start.6 = (bf16[2048,4,64]{0,2,1:T(8,128)(2,1)S(1)}, bf16[2048,4,64]{0,2,1:T(8,128)(2,1)}, u32[]{:S(2)}) copy-start(bf16[2048,4,64]{0,2,1:T(8,128)(2,1)} %param.15) | copy-start | bytes 3145732
  298.3 6.1 %copy-start.8 = (f32[16,128,128]{2,1,0:T(8,128)S(1)}, f32[16,128,128]{2,1,0:T(8,128)}, u32[]{:S(2)}) copy-start(f32[16,128,128]{2,1,0:T(8,128)} %copy-done.7) | copy-start | bytes 3145732
Sparse Core Ops, SparseCore 0:
  16.0 84.7 all-gather.5
  104.0 78.8 all-gather.7
  292.5 74.8 all-reduce.7
where the time goes:
time: 380 us; the launch traced here: 377 us
  other arithmetic  89.5 us (24%)
  local copies, waits for them, and re-layouts  74.9 us (20%)
  blocking collectives  74.1 us (19%)
  waiting for transfers between devices  73.6 us (19%)
  matrix products  47.9 us (13%)
  between operations  15.4 us (4%)
    unnamed x1, blocking collectives  74.1 us
    all_gather x1, waiting for transfers between devices, local(): lax.all_gather(own_state[None], 'seq', axis=0, tiled=True)  44.3 us
    add x32, other arithmetic, advance(): return (item[0][:, None, None] * carried + item[1], carried)  33.6 us
    unnamed x4, waiting for transfers between devices  29.3 us
    another operation x2, other arithmetic, split_blocks(): jnp.cumsum(log_rates.reshape(blocks, SPAN, log_rates.shape[1]), axis=1)  24.7 us
    dynamic_update_slice x64, local copies, waits for them, and re-layouts, run_chain(): return lax.scan(advance, start, (totals, states))  24.3 us
    dot_general x3, matrix products, block_states(): jnp.einsum('kjn,kjhp->khnp', incoming_segments, blocked * tail[..., None]...  17.7 us
    reduce_sum x16, other arithmetic, advance(): return (item[0][:, None, None] * carried + item[1], carried)  17.3 us
  transfers between devices with their start and end apart: 3, of which 2 were waited for; matrix products, arithmetic and copies ran while one was open for 24% of the time, Pallas kernels for 0%

commit v1 on v0

v1 whole, which is shorter than its diff:
```python
import functools

import jax
import jax.numpy as jnp
from jax import lax
from jax.experimental import pallas as pl
from jax.experimental.pallas import tpu as pltpu
from jax.sharding import PartitionSpec as P

HEADS_HERE = 4
WIDTH = 64
STATE = 128
SPAN = 128
TOK = 2048
CHUNKS = TOK // SPAN
ROWS = HEADS_HERE * WIDTH
SEQ = 32
SLICE = ROWS // SEQ
F32 = jnp.float32
BF16 = jnp.bfloat16
FIRST_LIMIT = 60 * 1024 * 1024
PART_LIMIT = 40 * 1024 * 1024
LAST_LIMIT = 40 * 1024 * 1024
CHUNK_LIMIT = 60 * 1024 * 1024
VMEM_LIMIT = 24 * 1024 * 1024


def dot_nn(a, b):
    return lax.dot_general(a, b, (((1,), (0,)), ((), ())), preferred_element_type=F32)


def dot_nt(a, b):
    return lax.dot_general(a, b, (((1,), (1,)), ((), ())), preferred_element_type=F32)


def split2(x):
    hi = x.astype(BF16)
    return hi, (x - hi.astype(F32)).astype(BF16)


def split3(x):
    a = x.astype(BF16)
    rest = x - a.astype(F32)
    b = rest.astype(BF16)
    return a, b, (rest - b.astype(F32)).astype(BF16)


def cat(parts, axis):
    return jnp.concatenate(parts, axis=axis)


def wide(x):
    hi, lo = split2(x)
    return cat([hi, lo], 1)


def iotas(shape):
    return lax.broadcasted_iota(jnp.int32, shape, 0), lax.broadcasted_iota(jnp.int32, shape, 1)


def ones_where(mask):
    return jnp.where(mask, 1.0, 0.0).astype(BF16)


def pad_heads(x):
    return cat([x, jnp.zeros((8 - HEADS_HERE, x.shape[1]), F32)], 0)


def spread_rows(rows):
    return cat(
        [jnp.broadcast_to(rows[h : h + 1, :], (WIDTH, SPAN)) for h in range(HEADS_HERE)], 0
    )


def head_sums(x):
    return cat(
        [
            jnp.sum(x[h * WIDTH : (h + 1) * WIDTH, :], axis=0, keepdims=True)
            for h in range(HEADS_HERE)
        ],
        0,
    )


def by_head(rows):
    lane = lax.broadcasted_iota(jnp.int32, (1, 2 * WIDTH), 1)
    return cat(
        [
            jnp.where(lane < WIDTH, rows[2 * q : 2 * q + 1, :], rows[2 * q + 1 : 2 * q + 2, :])
            for q in range(HEADS_HERE // 2)
        ],
        1,
    )


def to_slices(x, ref, place):
    for a in range(STATE // SLICE):
        for q in range(2):
            ref[2 * a + q, place : place + SLICE, :] = x[
                a * SLICE : (a + 1) * SLICE, q * STATE : (q + 1) * STATE
            ]


def from_slices(ref, place):
    return cat(
        [
            cat([ref[2 * a + q, place : place + SLICE, :] for q in range(2)], 1)
            for a in range(STATE // SLICE)
        ],
        0,
    )


ROWSET = 32


def choose(x, ref, group):
    ref[...] = x.astype(F32)
    return ref[pl.ds(group, SPAN, stride=2), :].astype(BF16)


def row_tables(log_ref, rows_ref, edge_ref, lanes_ref, msg_ref):
    r, c = iotas((SPAN, SPAN))
    tri = cat([ones_where(r <= c), ones_where(r > c), jnp.ones((SPAN, SPAN), BF16)], 1)
    tri = cat([tri] * 3, 0)
    stacked = cat(
        [
            cat(list(split3(pad_heads(log_ref[:, k * SPAN : (k + 1) * SPAN]))), 1)
            for k in range(CHUNKS)
        ],
        0,
    )
    sums = dot_nn(stacked, tri)
    tot = [sums[8 * k : 8 * k + 8, 2 * SPAN :] for k in range(CHUNKS)]
    before = jnp.zeros((8, SPAN), F32)
    for k in range(CHUNKS):
        cin = sums[8 * k : 8 * k + 8, :SPAN]
        rows_ref[k, 0:8, :] = cin
        rows_ref[k, 8:16, :] = jnp.exp(cin)
        rows_ref[k, 16:24, :] = jnp.exp(sums[8 * k : 8 * k + 8, SPAN : 2 * SPAN])
        whole = jnp.exp(tot[k])
        rows_ref[k, 24:32, :] = whole
        edge_ref[k, 0:8, :] = jnp.exp(before + cin)
        lanes_ref[k, 0:1, :] = by_head(whole)
        lanes_ref[k, 1:2, :] = by_head(jnp.exp(before))
        before = before + tot[k]
    after = jnp.zeros((8, SPAN), F32)
    for k in reversed(range(CHUNKS)):
        edge_ref[k, 8:16, :] = jnp.exp(after + sums[8 * k : 8 * k + 8, SPAN : 2 * SPAN])
        lanes_ref[k, 2:3, :] = by_head(jnp.exp(after))
        lanes_ref[k, 3:8, :] = jnp.zeros((5, ROWS), F32)
        after = after + tot[k]
    to_slices(jnp.broadcast_to(by_head(jnp.exp(before)), (STATE, ROWS)), msg_ref, 2 * SLICE)


def first_kernel(
    x_hbm, y_hbm, b_hbm, c_hbm, log_hbm, msg_hbm, rows_hbm, edge_hbm, lanes_hbm, bs_hbm, cs_hbm,
    x_ref, y_ref, b_ref, c_ref, log_ref, msg_ref, rows_ref, edge_ref, lanes_ref, bs_ref, cs_ref, wide_ref,
    get_sem, put_sem
):
    top, low = pl.ds(0, ROWS // 2), pl.ds(ROWS // 2, ROWS // 2)
    gets = [
        pltpu.make_async_copy(src, dst, get_sem.at[n])
        for n, (src, dst) in enumerate(
            (
                (log_hbm, log_ref),
                (b_hbm, b_ref),
                (x_hbm, x_ref),
                (c_hbm, c_ref),
                (y_hbm.at[top, :], y_ref.at[top, :]),
                (y_hbm.at[low, :], y_ref.at[low, :]),
            )
        )
    ]
    for copy in gets:
        copy.start()
    puts = []

    def put(src, dst):
        copy = pltpu.make_async_copy(src, dst, put_sem.at[len(puts)])
        copy.start()
        puts.append(copy)

    def put_message(place):
        part = pl.ds(place, SLICE)
        put(msg_ref.at[:, part, :], msg_hbm.at[:, part, :])

    group = lax.axis_index("head") // 4
    gets[0].wait()
    row_tables(log_ref, rows_ref, edge_ref, lanes_ref, msg_ref)
    put(rows_ref, rows_hbm)
    put(edge_ref, edge_hbm)
    put(lanes_ref, lanes_hbm)
    put_message(2 * SLICE)

    def select(src, dst, base):
        out = []
        for k in range(CHUNKS):
            got = choose(src[2 * k * SPAN : 2 * (k + 1) * SPAN, :], wide_ref.at[base + k], group)
            dst[k * SPAN : (k + 1) * SPAN, :] = got
            turned = got.T
            out.append(cat([turned, turned], 1))
        return out

    def gather(turned, src, row, first, heads):
        total = jnp.zeros((STATE, heads * WIDTH), F32)
        for k in range(CHUNKS):
            scale = edge_ref[k, row : row + 8, :]
            scale = cat(
                [
                    jnp.broadcast_to(scale[h : h + 1, :], (WIDTH, SPAN))
                    for h in range(first, first + heads)
                ],
                0,
            )
            part = src[first * WIDTH : (first + heads) * WIDTH, k * SPAN : (k + 1) * SPAN]
            total = total + dot_nt(turned[k], wide(part.astype(F32) * scale))
        return total

    gets[1].wait()
    turned = select(b_ref, bs_ref, 0)
    put(bs_ref, bs_hbm)
    gets[2].wait()
    to_slices(gather(turned, x_ref, 8, 0, HEADS_HERE), msg_ref, 0)
    put_message(0)
    gets[3].wait()
    turned = select(c_ref, cs_ref, CHUNKS)
    put(cs_ref, cs_hbm)
    halves = []
    for q in range(2):
        gets[4 + q].wait()
        halves.append(gather(turned, y_ref, 0, 2 * q, 2))
    to_slices(cat(halves, 1), msg_ref, SLICE)
    put_message(SLICE)
    for copy in puts:
        copy.wait()


def first_pass(x, y, b, c, log):
    hbm = pl.BlockSpec(memory_space=pltpu.HBM)
    return pl.pallas_call(
        first_kernel,
        in_specs=[hbm] * 5,
        out_specs=[hbm] * 6,
        out_shape=[
            jax.ShapeDtypeStruct((SEQ, 3 * SLICE, STATE), F32),
            jax.ShapeDtypeStruct((CHUNKS, ROWSET, SPAN), F32),
            jax.ShapeDtypeStruct((CHUNKS, 16, SPAN), F32),
            jax.ShapeDtypeStruct((CHUNKS, 8, ROWS), F32),
            jax.ShapeDtypeStruct((TOK, STATE), BF16),
            jax.ShapeDtypeStruct((TOK, STATE), BF16),
        ],
        scratch_shapes=[
            pltpu.VMEM((ROWS, TOK), BF16),
            pltpu.VMEM((ROWS, TOK), BF16),
            pltpu.VMEM((2 * TOK, STATE), BF16),
            pltpu.VMEM((2 * TOK, STATE), BF16),
            pltpu.VMEM((HEADS_HERE, TOK), F32),
            pltpu.VMEM((SEQ, 3 * SLICE, STATE), F32),
            pltpu.VMEM((CHUNKS, ROWSET, SPAN), F32),
            pltpu.VMEM((CHUNKS, 16, SPAN), F32),
            pltpu.VMEM((CHUNKS, 8, ROWS), F32),
            pltpu.VMEM((TOK, STATE), BF16),
            pltpu.VMEM((TOK, STATE), BF16),
            pltpu.VMEM((2 * CHUNKS, 2 * SPAN, STATE), F32),
            pltpu.SemaphoreType.DMA((6,)),
            pltpu.SemaphoreType.DMA((8,)),
        ],
        compiler_params=pltpu.CompilerParams(vmem_limit_bytes=FIRST_LIMIT),
        cost_estimate=pl.CostEstimate(flops=800_000_000, bytes_accessed=6_000_000, transcendentals=20_000),
        name="own_states",
    )(x, y, b, c, log)


def scan_kernel(got_ref, out_ref):
    carry = jnp.zeros((SLICE, STATE), F32)
    for k in range(SEQ):
        out_ref[k, :SLICE, :] = carry
        if k < SEQ - 1:
            carry = carry * got_ref[k, 2 * SLICE :, :] + got_ref[k, :SLICE, :]
    carry = jnp.zeros((SLICE, STATE), F32)
    for k in reversed(range(SEQ)):
        out_ref[k, SLICE:, :] = carry
        if k > 0:
            carry = carry * got_ref[k, 2 * SLICE :, :] + got_ref[k, SLICE : 2 * SLICE, :]


def scan_blocks(got):
    return pl.pallas_call(
        scan_kernel,
        in_specs=[pl.BlockSpec(memory_space=pltpu.VMEM)],
        out_shape=jax.ShapeDtypeStruct((SEQ, 2 * SLICE, STATE), F32),
        compiler_params=pltpu.CompilerParams(vmem_limit_bytes=VMEM_LIMIT),
        name="scan_blocks",
    )(got)


def decays(rows_ref, k, mask):
    cin = rows_ref[k, 0:8, :]
    cols = cin.T
    out = []
    for h in range(HEADS_HERE):
        gap = jnp.broadcast_to(cin[h : h + 1, :], (SPAN, SPAN)) - jnp.broadcast_to(
            cols[:, h : h + 1], (SPAN, SPAN)
        )
        out.append(jnp.exp(jnp.where(mask, gap, -1e30)))
    return out


def crosses(xt, y):
    zero = jnp.zeros((WIDTH, SPAN), BF16)
    out = []
    for q in range(HEADS_HERE // 2):
        top = y[2 * q * WIDTH : (2 * q + 1) * WIDTH, :]
        low = y[(2 * q + 1) * WIDTH : (2 * q + 2) * WIDTH, :]
        both = cat([cat([top, zero], 1), cat([zero, low], 1)], 0)
        pair = dot_nn(xt[:, 2 * q * WIDTH : 2 * (q + 1) * WIDTH], both)
        out += [pair[:, :SPAN], pair[:, SPAN:]]
    return out


def inter(near_hi, near_lo, state):
    hi, lo = split2(state)
    return dot_nn(cat([hi, hi, lo], 1), cat([near_hi, near_lo, near_hi], 0))


PER2 = 8


def ascend_kernel(x_ref, y_ref, b_ref, c_ref, rows_ref, lanes_ref, db_ref, dc_ref, s_ref, state):
    @pl.when(pl.program_id(0) == 0)
    def _():
        state[...] = jnp.zeros((STATE, ROWS), F32)

    r, l = iotas((SPAN, SPAN))
    mask = l >= r
    own = state[...]
    for k in range(PER2):
        here = slice(k * SPAN, (k + 1) * SPAN)
        x = x_ref[:, here]
        bt, ct = b_ref[here, :].T, c_ref[here, :].T
        twice = cat([bt, bt], 1)
        total = jnp.zeros((SPAN, SPAN), F32)
        for cross, decay in zip(crosses(x.T, y_ref[:, here]), decays(rows_ref, k, mask)):
            total = total + cross * decay
        hi, lo = split2(total)
        db_ref[:, here] = dot_nt(cat([ct, ct], 1), cat([hi, lo], 1))
        yhi, ylo = split2(y_ref[:, here].astype(F32) * spread_rows(rows_ref[k, 8:16, :]))
        dc_ref[:, here] = dot_nn(twice, cat([hi, lo], 0)) + inter(yhi, ylo, own)
        s_ref[k * STATE : (k + 1) * STATE, :] = own
        own = own * lanes_ref[k, 0:1, :] + dot_nt(
            twice, wide(x.astype(F32) * spread_rows(rows_ref[k, 16:24, :]))
        )
    state[...] = own


def chunk_specs(per, order):
    return [
        pl.BlockSpec((ROWS, per * SPAN), lambda i: (0, order(i))),
        pl.BlockSpec((ROWS, per * SPAN), lambda i: (0, order(i))),
        pl.BlockSpec((per * SPAN, STATE), lambda i: (order(i), 0)),
        pl.BlockSpec((per * SPAN, STATE), lambda i: (order(i), 0)),
        pl.BlockSpec((per, ROWSET, SPAN), lambda i: (order(i), 0, 0)),
        pl.BlockSpec((per, 8, ROWS), lambda i: (order(i), 0, 0)),
    ]


def ascend(x, y, b, c, rows, lanes):
    tokens = pl.BlockSpec((STATE, PER2 * SPAN), lambda i: (0, i))
    return pl.pallas_call(
        ascend_kernel,
        grid=(CHUNKS // PER2,),
        in_specs=chunk_specs(PER2, lambda i: i),
        out_specs=[
            tokens,
            tokens,
            pl.BlockSpec((PER2 * STATE, ROWS), lambda i: (i, 0)),
        ],
        out_shape=[jax.ShapeDtypeStruct((STATE, TOK), F32)] * 2
        + [
            jax.ShapeDtypeStruct((CHUNKS * STATE, ROWS), F32),
        ],
        scratch_shapes=[pltpu.VMEM((STATE, ROWS), F32)],
        compiler_params=pltpu.CompilerParams(vmem_limit_bytes=CHUNK_LIMIT),
        cost_estimate=pl.CostEstimate(flops=3_000_000_000, bytes_accessed=8_000_000, transcendentals=1_000_000),
        name="chunks_ascending",
    )(x, y, b, c, rows, lanes)


PER3 = 8


def descend_kernel(x_ref, y_ref, c_ref, rows_ref, lanes_ref, dbp_ref, db_ref, d_ref, grad):
    @pl.when(pl.program_id(0) == 0)
    def _():
        grad[...] = jnp.zeros((STATE, ROWS), F32)

    back = grad[...]
    for k in reversed(range(PER3)):
        here = slice(k * SPAN, (k + 1) * SPAN)
        xhi, xlo = split2(x_ref[:, here].astype(F32) * spread_rows(rows_ref[k, 16:24, :]))
        db_ref[:, here] = dbp_ref[:, here] + inter(xhi, xlo, back)
        d_ref[k * STATE : (k + 1) * STATE, :] = back
        ct = c_ref[here, :].T
        back = back * lanes_ref[k, 0:1, :] + dot_nt(
            cat([ct, ct], 1), wide(y_ref[:, here].astype(F32) * spread_rows(rows_ref[k, 8:16, :]))
        )
    grad[...] = back


def descend(x, y, c, rows, lanes, dbp):
    steps = CHUNKS // PER3
    order = lambda i: steps - 1 - i
    specs = chunk_specs(PER3, order)
    tokens = pl.BlockSpec((STATE, PER3 * SPAN), lambda i: (0, order(i)))
    states = pl.BlockSpec((PER3 * STATE, ROWS), lambda i: (order(i), 0))
    return pl.pallas_call(
        descend_kernel,
        grid=(steps,),
        in_specs=specs[:2] + specs[3:] + [tokens],
        out_specs=[tokens, states],
        out_shape=[
            jax.ShapeDtypeStruct((STATE, TOK), F32),
            jax.ShapeDtypeStruct((CHUNKS * STATE, ROWS), F32),
        ],
        scratch_shapes=[pltpu.VMEM((STATE, ROWS), F32)],
        compiler_params=pltpu.CompilerParams(vmem_limit_bytes=CHUNK_LIMIT),
        cost_estimate=pl.CostEstimate(flops=3_000_000_000, bytes_accessed=8_000_000, transcendentals=0),
        name="chunks_descending",
    )(x, y, c, rows, lanes, dbp)


HALF = 256


def part_kernel(
    side, bound_ref, edge_hbm, x_hbm, y_hbm, db_hbm, dc_hbm, out_hbm,
    edge_ref, x_ref, y_ref, both_ref, out_ref, get_sem, put_sem
):
    place = lax.axis_index("head")
    chip, core = place // 2, place % 2
    gets = []
    for i in range(4):
        block = 2 * jnp.bitwise_xor(chip, i) + jnp.bitwise_xor(core, side)
        cols = pl.ds(pl.multiple_of(block * HALF, HALF), HALF)
        gets.append(
            [
                pltpu.make_async_copy(
                    edge_hbm.at[pl.ds(2 * block, 2)], edge_ref.at[i], get_sem.at[i, 0]
                ),
                pltpu.make_async_copy(x_hbm.at[:, cols], x_ref.at[i], get_sem.at[i, 1]),
                pltpu.make_async_copy(y_hbm.at[:, cols], y_ref.at[i], get_sem.at[i, 2]),
                pltpu.make_async_copy(db_hbm.at[:, cols], both_ref.at[i, 0], get_sem.at[i, 3]),
                pltpu.make_async_copy(dc_hbm.at[:, cols], both_ref.at[i, 1], get_sem.at[i, 4]),
            ]
        )
        for copy in gets[i]:
            copy.start()
    edges = [split2(from_slices(bound_ref, place)) for place in (SLICE, 0)]
    stacks = [cat(list(edge), 0) for edge in edges]
    puts = []
    for i in range(4):
        for copy in gets[i]:
            copy.wait()
        for t, (row, src) in enumerate(((8, x_ref), (0, y_ref))):
            scale = cat(
                [spread_rows(edge_ref[i, k, row : row + 8, :]) for k in range(HALF // SPAN)], 1
            )
            near_hi, near_lo = split2(src[i].astype(F32) * scale)
            first = dot_nn(stacks[t], near_hi)
            out_ref[i, t] = both_ref[i, t] + (
                first[:STATE] + (first[STATE:] + dot_nn(edges[t][0], near_lo))
            )
        copy = pltpu.make_async_copy(out_ref.at[i], out_hbm.at[i], put_sem.at[i])
        copy.start()
        puts.append(copy)
    for copy in puts:
        copy.wait()


def part_pass(name, side, bound, edge, x, y, db, dc):
    hbm = pl.BlockSpec(memory_space=pltpu.HBM)
    return pl.pallas_call(
        functools.partial(part_kernel, side),
        in_specs=[pl.BlockSpec(memory_space=pltpu.VMEM)] + [hbm] * 5,
        out_specs=hbm,
        out_shape=jax.ShapeDtypeStruct((4, 2, STATE, HALF), F32),
        scratch_shapes=[
            pltpu.VMEM((4, 2, 16, SPAN), F32),
            pltpu.VMEM((4, ROWS, HALF), BF16),
            pltpu.VMEM((4, ROWS, HALF), BF16),
            pltpu.VMEM((4, 2, STATE, HALF), F32),
            pltpu.VMEM((4, 2, STATE, HALF), F32),
            pltpu.SemaphoreType.DMA((4, 5)),
            pltpu.SemaphoreType.DMA((4,)),
        ],
        compiler_params=pltpu.CompilerParams(vmem_limit_bytes=PART_LIMIT),
        cost_estimate=pl.CostEstimate(flops=500_000_000, bytes_accessed=3_000_000, transcendentals=0),
        name=name,
    )(bound, edge, x, y, db, dc)


def sum_kernel(kept_ref, got_ref, *outs):
    for m in range(4):
        outs[m][...] = kept_ref[m] + got_ref[m]


def sum_pass(kept, got):
    vmem = pl.BlockSpec(memory_space=pltpu.VMEM)
    return pl.pallas_call(
        sum_kernel,
        in_specs=[vmem, vmem],
        out_specs=[vmem] * 4,
        out_shape=[jax.ShapeDtypeStruct((2, STATE, HALF), F32)] * 4,
        compiler_params=pltpu.CompilerParams(vmem_limit_bytes=VMEM_LIMIT),
        name="sum_cores",
    )(kept, got)


PER5 = 4


def last_kernel(x_ref, y_ref, b_ref, c_ref, rows_ref, lanes_ref, bound_ref, s_ref, d_ref, dx_ref, dl_ref):
    entering = from_slices(bound_ref, 0)
    leaving = from_slices(bound_ref, SLICE)
    r, l = iotas((SPAN, SPAN))
    mask = l >= r
    later = cat([ones_where(r >= l)] * 3, 0)
    every = jnp.ones((3 * (SPAN + ROWS), SPAN), BF16)
    owner_row, owner_lane = iotas((HEADS_HERE, ROWS))
    owned = owner_lane // WIDTH == owner_row
    for k in range(PER5):
        here = slice(k * SPAN, (k + 1) * SPAN)
        states = slice(k * STATE, (k + 1) * STATE)
        x, y, b, c = x_ref[:, here], y_ref[:, here], b_ref[here, :], c_ref[here, :]
        scores = dot_nt(b, c)
        s = s_ref[states, :] + lanes_ref[k, 1:2, :] * entering
        d = d_ref[states, :] + lanes_ref[k, 2:3, :] * leaving
        dhi, dlo = split2(d)
        shi, slo = split2(s)
        u = dot_nt(cat([dhi.T, dlo.T], 1), cat([b, b], 1)) * spread_rows(rows_ref[k, 16:24, :])
        z = dot_nt(cat([shi.T, slo.T], 1), cat([c, c], 1))
        row, inner = [], []
        for h, (cross, decay) in enumerate(zip(crosses(x.T, y), decays(rows_ref, k, mask))):
            weight = scores * decay
            yh = y[h * WIDTH : (h + 1) * WIDTH, :]
            inner.append(dot_nt(cat([yh, yh], 1), wide(weight)))
            row.append(jnp.sum(weight * cross, axis=0, keepdims=True))
        dx = cat(inner, 0) + u
        dx_ref[:, here] = dx.astype(BF16)
        xf = x.astype(F32)
        pending = (
            cat(row, 0)
            + rows_ref[k, 8 : 8 + HEADS_HERE, :] * head_sums(z * y.astype(F32))
            - head_sums(xf * dx)
        )
        meet = jnp.where(owned, jnp.sum(s * d, axis=0, keepdims=True), 0.0) * cat(
            [rows_ref[k, 24 : 24 + HEADS_HERE, :]] * 2, 1
        )
        through = cat([head_sums(xf * u), meet], 1)
        dl_ref[:, here] = dot_nn(cat(list(split3(pending)), 1), later) + dot_nn(
            cat(list(split3(through)), 1), every
        )


def last_pass(x, y, b, c, rows, lanes, bound, s, d):
    states = pl.BlockSpec((PER5 * STATE, ROWS), lambda i: (i, 0))
    return pl.pallas_call(
        last_kernel,
        grid=(CHUNKS // PER5,),
        in_specs=chunk_specs(PER5, lambda i: i)
        + [
            pl.BlockSpec((SEQ, 2 * SLICE, STATE), lambda i: (0, 0, 0)),
            states,
            states,
        ],
        out_specs=[
            pl.BlockSpec((ROWS, PER5 * SPAN), lambda i: (0, i)),
            pl.BlockSpec((HEADS_HERE, PER5 * SPAN), lambda i: (0, i)),
        ],
        out_shape=[
            jax.ShapeDtypeStruct((ROWS, TOK), BF16),
            jax.ShapeDtypeStruct((HEADS_HERE, TOK), F32),
        ],
        compiler_params=pltpu.CompilerParams(vmem_limit_bytes=LAST_LIMIT),
        cost_estimate=pl.CostEstimate(flops=6_000_000_000, bytes_accessed=12_000_000, transcendentals=1_000_000),
        name="inputs_and_decay",
    )(x, y, b, c, rows, lanes, bound, s, d)


def merge_kernel(own_ref, near_ref, far_ref, side_ref, in_ref, out_ref):
    group = lax.axis_index("head") // 4
    for t, ref in enumerate((in_ref, out_ref)):
        ref[pl.ds(group, HALF, stride=2), :] = (own_ref[t] + near_ref[t]).T
        ref[pl.ds(1 - group, HALF, stride=2), :] = (far_ref[t] + side_ref[t]).T


def merge(own, near, far, side):
    spec = pl.BlockSpec(memory_space=pltpu.VMEM)
    return pl.pallas_call(
        merge_kernel,
        in_specs=[spec] * 4,
        out_specs=[spec] * 2,
        out_shape=[jax.ShapeDtypeStruct((2 * HALF, STATE), F32)] * 2,
        compiler_params=pltpu.CompilerParams(vmem_limit_bytes=VMEM_LIMIT),
        name="merge",
    )(own, near, far, side)


def local(inputs, log_decay, in_proj, out_proj, upstream):
    x = jnp.transpose(inputs, (1, 2, 0)).reshape(ROWS, TOK)
    y = jnp.transpose(upstream, (1, 2, 0)).reshape(ROWS, TOK)
    log = jnp.transpose(log_decay)
    b2 = in_proj.reshape(2 * TOK, STATE)
    c2 = out_proj.reshape(2 * TOK, STATE)
    message, rows, edge, lanes, b, c = first_pass(x, y, b2, c2, log)
    got = lax.all_to_all(message, "seq", 0, 0)
    dbp, dc, s = ascend(x, y, b, c, rows, lanes)
    got, dbp = lax.optimization_barrier((got, dbp))
    bound = lax.all_to_all(scan_blocks(got), "seq", 0, 0)
    db, d = descend(x, y, c, rows, lanes, dbp)
    sent = part_pass("projections_send", 1, bound, edge, x, y, db, dc)
    other = lax.ppermute(sent, "head", [(i, i ^ 1) for i in range(8)])
    kept = part_pass("projections_keep", 0, bound, edge, x, y, db, dc)
    parts = sum_pass(kept, other)
    moved = [
        lax.ppermute(parts[m], "head", [(i, i ^ (2 * m)) for i in range(8)]) for m in (1, 2, 3)
    ]
    grad_x, grad_log = last_pass(x, y, b, c, rows, lanes, bound, s, d)
    grad_in, grad_out = merge(parts[0], *moved)
    return (
        jnp.transpose(grad_x.reshape(HEADS_HERE, WIDTH, TOK), (2, 0, 1)),
        jnp.transpose(grad_log),
        grad_in.reshape(HALF, 2, STATE),
        grad_out.reshape(HALF, 2, STATE),
    )


def solution(mesh):
    in_specs = (
        P("seq", "head", None),
        P("seq", "head"),
        P("seq", None, None),
        P("seq", None, None),
        P("seq", "head", None),
    )
    out_specs = (
        P("seq", "head", None),
        P("seq", "head"),
        P(("seq", "head"), None, None),
        P(("seq", "head"), None, None),
    )
    return jax.shard_map(local, mesh=mesh, in_specs=in_specs, out_specs=out_specs, check_vma=False)
```

time: 380 us -> 75.8 us (0.20)
  other arithmetic: 89.5 us -> 0 us
  blocking collectives: 74.1 us -> 0 us
  local copies, waits for them, and re-layouts: 74.9 us -> 1.27 us
  waiting for transfers between devices: 73.6 us -> 18 us
  matrix products: 47.9 us -> 0 us
  Pallas kernels: 0 us -> 34.5 us
  starting transfers between devices: 0.12 us -> 21 us
  between operations: 15.4 us -> 0.82 us
    unnamed x1 -> x0, blocking collectives: 74.1 us -> none
    dot_general x11 -> x0, matrix products: 44.4 us -> none  [the longest x3 17.7 us: block_states(): jnp.einsum('kjn,kjhp->khnp', incoming_segments, blocked * tail[..., None]...]
    all_gather x2 -> x0, waiting for transfers between devices: 44.3 us -> none  [the longest x1 44.3 us: local(): lax.all_gather(own_state[None], 'seq', axis=0, tiled=True)]
    pallas_call x0 -> x9, Pallas kernels: none -> 34.5 us  [the longest x1 8.4 us: ascend(): pl.pallas_call(ascend_kernel, grid=(CHUNKS // PER2,), in_specs=chunk_spec...]
    add x33 -> x0, other arithmetic: 33.6 us -> none  [the longest x32 33.6 us: advance(): return (item[0][:, None, None] * carried + item[1], carried)]
    unnamed x4 -> x0, waiting for transfers between devices: 29.3 us -> none
    another operation x5 -> x0, other arithmetic: 26 us -> none  [the longest x2 24.7 us: split_blocks(): jnp.cumsum(log_rates.reshape(blocks, SPAN, log_rates.shape[1]), axis=1)]
    dynamic_update_slice x64 -> x0, local copies, waits for them, and re-layouts: 24.3 us -> none  [run_chain(): return lax.scan(advance, start, (totals, states))]
  transfers between devices with their start and end apart: 3 -> 6, of which waited for: 2 -> 5; matrix products, arithmetic and copies ran while one was open for 24% -> 0% of each run, Pallas kernels for 0% -> 33%
where the time goes in v1:
time: 75.8 us; the launch traced here: 75.5 us
  Pallas kernels  34.5 us (46%)
  starting transfers between devices  21 us (28%)
  waiting for transfers between devices  18 us (24%)
  local copies, waits for them, and re-layouts  1.27 us (2%)
  between operations  0.82 us (1%)
    all_to_all x1, starting transfers between devices, local(): got = lax.all_to_all(message, 'seq', 0, 0)  11.4 us
    pallas_call x1, Pallas kernels, ascend(): pl.pallas_call(ascend_kernel, grid=(CHUNKS // PER2,), in_specs=chunk_spec...  8.4 us
    pallas_call x1, Pallas kernels, last_pass(): pl.pallas_call(last_kernel, grid=(CHUNKS // PER5,), in_specs=chunk_specs(...  8.26 us
    pallas_call x1, Pallas kernels, descend(): pl.pallas_call(descend_kernel, grid=(steps,), in_specs=specs[:2] + specs[...  6.61 us
    all_to_all x1, waiting for transfers between devices, local(): got = lax.all_to_all(message, 'seq', 0, 0)  6.48 us
    ppermute x3, waiting for transfers between devices, local(): lax.ppermute(parts[m], 'head', [(i, i ^ 2 * m) for i in range(8)])  5.84 us
    pallas_call x1, Pallas kernels, first_pass(): pl.pallas_call(first_kernel, in_specs=[hbm] * 5, out_specs=[hbm] * 6, out...  5.4 us
    all_to_all x1, waiting for transfers between devices, local(): bound = lax.all_to_all(scan_blocks(got), 'seq', 0, 0)  5.09 us
  transfers between devices with their start and end apart: 6, of which 5 were waited for; matrix products, arithmetic and copies ran while one was open for 0% of the time, Pallas kernels for 33%

profile of v1, /device:TPU:32, one launch (start us, length us, event | category | flops | bytes accessed | tf_op | source)
XLA Modules:
  0.0 75.5 jit_solution(6017907675898343831)
XLA Ops:
  0.6 5.4 %own_states.1 = (f32[32,24,128]{2,1,0:T(8,128)}, f32[16,32,128]{2,1,0:T(8,128)}, f32[16,16,128]{2,1,0:T(8,128)}, f32[16,8,256]{2,1,0:T(8,128)}, bf16[2048,128]{1,0:T(8,128)(2,1)}, /*index=5*/bf16[2048,128]{1,0:T(8,128)(2,1)}) custom-call(bf16[256,2048]{1,0:T(8,128)(2,1)} %bitcast.15, bf16[256,2048]{1,0:T(8,128)(2,1)} %bitcast.21, ...), custom_call_target="tpu_custom_call" | custom-call | flops 800000000 | bytes 6000000 | tf_op jit(solution)/shard_map/own_states/pallas_call | solution.py:241
  6.0 11.4 %all-to-all-start = ((f32[32,24,128]{2,1,0:T(8,128)}), f32[32,24,128]{2,1,0:T(8,128)S(1)}, u32[]{:S(2)}, u32[]{:S(2)}) async-start(f32[32,24,128]{2,1,0:T(8,128)} %get-tuple-element.29), calls=%async_computation | async-start | bytes 786432 | tf_op jit(solution)/shard_map/all_to_all | solution.py:617
  17.4 8.4 %chunks_ascending.1 = (f32[128,2048]{1,0:T(8,128)}, f32[128,2048]{1,0:T(8,128)}, f32[2048,256]{1,0:T(8,128)}) custom-call(bf16[256,2048]{1,0:T(8,128)(2,1)} %bitcast.16, bf16[256,2048]{1,0:T(8,128)(2,1)} %bitcast.22, bf16[2048,128]{1,0:T(8,128)(2,1)} %get-tuple-element.25.b_ref, bf16[2048,128]{1,0:T(8,128)(2,1)} %get-tuple-element.26.c_ref, ...), custom_call_target="tpu_custom_call" | custom-call | flops 3000000000 | bytes 8000000 | tf_op jit(solution)/shard_map/chunks_ascending/pallas_call | solution.py:370
  25.8 6.5 %all-to-all-done.got_ref = f32[32,24,128]{2,1,0:T(8,128)S(1)} async-done(((f32[32,24,128]{2,1,0:T(8,128)}), f32[32,24,128]{2,1,0:T(8,128)S(1)}, u32[]{:S(2)}, u32[]{:S(2)}) %all-to-all-start) | async-done | bytes 393248 | tf_op jit(solution)/shard_map/all_to_all | solution.py:617
  32.3 0.8 %scan_blocks.1 = f32[32,16,128]{2,1,0:T(8,128)} custom-call(f32[32,24,128]{2,1,0:T(8,128)S(1)} %all-to-all-done.got_ref), custom_call_target="tpu_custom_call" | custom-call | tf_op jit(solution)/shard_map/scan_blocks/pallas_call | solution.py:289
  33.1 4.8 %all-to-all-start.1 = ((f32[32,16,128]{2,1,0:T(8,128)}), f32[32,16,128]{2,1,0:T(8,128)S(1)}, u32[]{:S(2)}, u32[]{:S(2)}) async-start(f32[32,16,128]{2,1,0:T(8,128)} %scan_blocks.1), calls=%async_computation.1 | async-start | bytes 524288 | tf_op jit(solution)/shard_map/all_to_all | solution.py:620
  37.9 0.0 copy-start
  37.9 0.0 copy-start.1
  37.9 0.0 copy-start.2
  37.9 0.0 copy-start.5
  37.9 6.6 %chunks_descending.1 = (f32[128,2048]{1,0:T(8,128)}, f32[2048,256]{1,0:T(8,128)}) custom-call(bf16[256,2048]{1,0:T(8,128)(2,1)} %bitcast.17, bf16[256,2048]{1,0:T(8,128)(2,1)} %bitcast.23, bf16[2048,128]{1,0:T(8,128)(2,1)} %get-tuple-element.26.c_ref, f32[16,32,128]{2,1,0:T(8,128)} %get-tuple-element.27.rows_ref, f32[16,8,256]{2,1,0:T(8,128)} %get-tuple-element.28.lanes_ref, ...), custom_call_target="tpu_custom_call" | custom-call | flops 3000000000 | bytes 8000000 | tf_op jit(solution)/shard_map/chunks_descending/pallas_call | solution.py:417
  44.5 5.1 %all-to-all-done.1.bound_ref = f32[32,16,128]{2,1,0:T(8,128)S(1)} async-done(((f32[32,16,128]{2,1,0:T(8,128)}), f32[32,16,128]{2,1,0:T(8,128)S(1)}, u32[]{:S(2)}, u32[]{:S(2)}) %all-to-all-start.1) | async-done | bytes 262176 | tf_op jit(solution)/shard_map/all_to_all | solution.py:620
  49.6 0.0 copy-done
  49.6 0.0 copy-done.1
  49.6 0.0 copy-done.2
  49.6 0.0 copy-done.5
  49.6 0.0 copy-start.3
  49.6 1.2 %copy-done.3 = f32[128,2048]{1,0:T(8,128)S(1)} copy-done((f32[128,2048]{1,0:T(8,128)S(1)}, f32[128,2048]{1,0:T(8,128)}, u32[]{:S(2)}) %copy-start.3) | copy-done | bytes 1048600
  50.9 2.0 %projections_send.1 = f32[4,2,128,256]{3,2,1,0:T(8,128)S(1)} custom-call(f32[32,16,128]{2,1,0:T(8,128)S(1)} %all-to-all-done.1.bound_ref, f32[16,16,128]{2,1,0:T(8,128)S(1)} %copy-done.5, bf16[256,2048]{1,0:T(8,128)(2,1)S(1)} %bitcast.18, bf16[256,2048]{1,0:T(8,128)(2,1)S(1)} %bitcast.24, f32[128,2048]{1,0:T(8,128)S(1)} %copy-done.3, f32[128,2048]{1,0:T(8,128)S(1)} %copy-done.2), custom_call_target="tpu_custom_call" | custom-call | flops 500000000 | bytes 3000000 | tf_op jit(solution)/shard_map/projections_send/pallas_call | solution.py:483
  52.8 0.1 collective-permute-start
  53.0 2.0 %projections_keep.1.kept_ref = f32[4,2,128,256]{3,2,1,0:T(8,128)S(1)} custom-call(f32[32,16,128]{2,1,0:T(8,128)S(1)} %all-to-all-done.1.bound_ref, f32[16,16,128]{2,1,0:T(8,128)S(1)} %copy-done.5, bf16[256,2048]{1,0:T(8,128)(2,1)S(1)} %bitcast.19, bf16[256,2048]{1,0:T(8,128)(2,1)S(1)} %bitcast.25, f32[128,2048]{1,0:T(8,128)S(1)} %copy-done.4, ...), custom_call_target="tpu_custom_call" | custom-call | flops 500000000 | bytes 3000000 | tf_op jit(solution)/shard_map/projections_keep/pallas_call | solution.py:483
  55.0 0.0 copy-start.8
  55.0 0.6 collective-permute-done.got_ref
  55.6 0.1 sum_cores.1
  55.7 1.6 %collective-permute-start.1 = (f32[2,128,256]{2,1,0:T(8,128)S(1)}, f32[2,128,256]{2,1,0:T(8,128)S(1)}, u32[]{:S(2)}, u32[]{:S(2)}) collective-permute-start(f32[2,128,256]{2,1,0:T(8,128)S(1)} %get-tuple-element.41), channel_id=1, source_target_pairs={{0,2},{1,3},{2,0},{3,1},{4,6},{5,7},{6,4},{7,5},{8,10},{9,11},{10,... | collective-permute-start | bytes 786440 | tf_op jit(solution)/shard_map/ppermute | solution.py:627
  57.2 2.8 %collective-permute-start.2 = (f32[2,128,256]{2,1,0:T(8,128)S(1)}, f32[2,128,256]{2,1,0:T(8,128)S(1)}, u32[]{:S(2)}, u32[]{:S(2)}) collective-permute-start(f32[2,128,256]{2,1,0:T(8,128)S(1)} %get-tuple-element.42), channel_id=1, source_target_pairs={{0,4},{1,5},{2,6},{3,7},{4,0},{5,1},{6,2},{7,3},{8,12},{9,13},{10,... | collective-permute-start | bytes 786440 | tf_op jit(solution)/shard_map/ppermute | solution.py:627
  60.0 0.5 collective-permute-start.3
  60.5 8.3 %inputs_and_decay.1 = (bf16[256,2048]{1,0:T(8,128)(2,1)}, f32[4,2048]{1,0:T(4,128)}) custom-call(bf16[256,2048]{1,0:T(8,128)(2,1)S(1)} %bitcast.20, bf16[256,2048]{1,0:T(8,128)(2,1)S(1)} %bitcast.26, bf16[2048,128]{1,0:T(8,128)(2,1)S(1)} %copy-done.6, bf16[2048,128]{1,0:T(8,128)(2,1)S(1)} %copy-done.7, f32[16,32,128]{2,1,0:T(8,128)S(1)} %copy-done.8, ...), custom_call_target="tpu_custom_call" | custom-call | flops 6000000000 | bytes 12000000 | tf_op jit(solution)/shard_map/inputs_and_decay/pallas_call | solution.py:568
  68.8 0.0 collective-permute-done.1.near_ref
  68.8 3.3 %collective-permute-done.2.far_ref = f32[2,128,256]{2,1,0:T(8,128)S(1)} collective-permute-done((f32[2,128,256]{2,1,0:T(8,128)S(1)}, f32[2,128,256]{2,1,0:T(8,128)S(1)}, u32[]{:S(2)}, u32[]{:S(2)}) %collective-permute-start.2) | collective-permute-done | bytes 262176 | tf_op jit(solution)/shard_map/ppermute | solution.py:627
  72.0 2.6 %collective-permute-done.3.side_ref = f32[2,128,256]{2,1,0:T(8,128)S(1)} collective-permute-done((f32[2,128,256]{2,1,0:T(8,128)S(1)}, f32[2,128,256]{2,1,0:T(8,128)S(1)}, u32[]{:S(2)}, u32[]{:S(2)}) %collective-permute-start.3) | collective-permute-done | bytes 262176 | tf_op jit(solution)/shard_map/ppermute | solution.py:627
  74.6 0.9 %merge.1 = (f32[512,128]{1,0:T(8,128)}, f32[512,128]{1,0:T(8,128)}) custom-call(f32[2,128,256]{2,1,0:T(8,128)S(1)} %get-tuple-element.40.own_ref, f32[2,128,256]{2,1,0:T(8,128)S(1)} %collective-permute-done.1.near_ref, f32[2,128,256]{2,1,0:T(8,128)S(1)} %collective-permute-done.2.far_ref, f32[2,128,256]{2,1,0:T(8,128)S(1)} %collective-permute-done.3.side_ref), custom_call_target="tpu_custom_call" | custom-call | tf_op jit(solution)/shard_map/merge/pallas_call | solution.py:600
  (13 shorter events, 0.0 us)
Async XLA Ops:
  6.0 26.3 %all-to-all-start = ((f32[32,24,128]{2,1,0:T(8,128)}), f32[32,24,128]{2,1,0:T(8,128)S(1)}, u32[]{:S(2)}, u32[]{:S(2)}) async-start(f32[32,24,128]{2,1,0:T(8,128)} %get-tuple-element.29), calls=%async_computation | async-start | bytes 786432 | tf_op jit(solution)/shard_map/all_to_all | solution.py:617
  33.1 16.5 %all-to-all-start.1 = ((f32[32,16,128]{2,1,0:T(8,128)}), f32[32,16,128]{2,1,0:T(8,128)S(1)}, u32[]{:S(2)}, u32[]{:S(2)}) async-start(f32[32,16,128]{2,1,0:T(8,128)} %scan_blocks.1), calls=%async_computation.1 | async-start | bytes 524288 | tf_op jit(solution)/shard_map/all_to_all | solution.py:620
  37.9 11.7 %copy-start = (bf16[2048,4,64]{0,2,1:T(8,128)(2,1)S(1)}, bf16[2048,4,64]{0,2,1:T(8,128)(2,1)}, u32[]{:S(2)}) copy-start(bf16[2048,4,64]{0,2,1:T(8,128)(2,1)} %param.5) | copy-start | bytes 3145732
  37.9 11.7 %copy-start.1 = (bf16[2048,4,64]{0,2,1:T(8,128)(2,1)S(1)}, bf16[2048,4,64]{0,2,1:T(8,128)(2,1)}, u32[]{:S(2)}) copy-start(bf16[2048,4,64]{0,2,1:T(8,128)(2,1)} %param.9) | copy-start | bytes 3145732
  37.9 11.7 %copy-start.2 = (f32[128,2048]{1,0:T(8,128)S(1)}, f32[128,2048]{1,0:T(8,128)}, u32[]{:S(2)}) copy-start(f32[128,2048]{1,0:T(8,128)} %get-tuple-element.39.dc_hbm) | copy-start | bytes 3145732
  37.9 11.7 %copy-start.5 = (f32[16,16,128]{2,1,0:T(8,128)S(1)}, f32[16,16,128]{2,1,0:T(8,128)}, u32[]{:S(2)}) copy-start(f32[16,16,128]{2,1,0:T(8,128)} %get-tuple-element.37.edge_hbm) | copy-start | bytes 393220
  49.6 1.2 %copy-start.3 = (f32[128,2048]{1,0:T(8,128)S(1)}, f32[128,2048]{1,0:T(8,128)}, u32[]{:S(2)}) copy-start(f32[128,2048]{1,0:T(8,128)} %get-tuple-element.38.db_hbm) | copy-start | bytes 3145732
  50.9 2.1 %copy-start.4 = (f32[128,2048]{1,0:T(8,128)S(1)}, f32[128,2048]{1,0:T(8,128)}, u32[]{:S(2)}) copy-start(f32[128,2048]{1,0:T(8,128)} %get-tuple-element.38.db_hbm) | copy-start | bytes 3145732
  52.8 2.7 %collective-permute-start = (f32[4,2,128,256]{3,2,1,0:T(8,128)S(1)}, f32[4,2,128,256]{3,2,1,0:T(8,128)S(1)}, u32[]{:S(2)}, u32[]{:S(2)}) collective-permute-start(f32[4,2,128,256]{3,2,1,0:T(8,128)S(1)} %projections_send.1), channel_id=1, source_target_pairs={{0,1},{1,0},{2,3},{3,2},{4,5},{5,4},{6,7},{7,6},{8,9},{9,8},{10,11... | collective-permute-start | bytes 3145736 | tf_op jit(solution)/shard_map/ppermute | solution.py:623
  52.9 7.5 %copy-start.10 = (f32[2048,256]{1,0:T(8,128)S(1)}, f32[2048,256]{1,0:T(8,128)}, u32[]{:S(2)}) copy-start(f32[2048,256]{1,0:T(8,128)} %get-tuple-element.34.d_ref) | copy-start | bytes 6291460
  52.9 7.5 %copy-start.11 = (f32[2048,256]{1,0:T(8,128)S(1)}, f32[2048,256]{1,0:T(8,128)}, u32[]{:S(2)}) copy-start(f32[2048,256]{1,0:T(8,128)} %get-tuple-element.32.s_ref) | copy-start | bytes 6291460
  55.0 5.5 %copy-start.6 = (bf16[2048,128]{1,0:T(8,128)(2,1)S(1)}, bf16[2048,128]{1,0:T(8,128)(2,1)}, u32[]{:S(2)}) copy-start(bf16[2048,128]{1,0:T(8,128)(2,1)} %get-tuple-element.25.b_ref) | copy-start | bytes 1572868
  55.0 5.5 %copy-start.7 = (bf16[2048,128]{1,0:T(8,128)(2,1)S(1)}, bf16[2048,128]{1,0:T(8,128)(2,1)}, u32[]{:S(2)}) copy-start(bf16[2048,128]{1,0:T(8,128)(2,1)} %get-tuple-element.26.c_ref) | copy-start | bytes 1572868
  55.0 5.5 %copy-start.8 = (f32[16,32,128]{2,1,0:T(8,128)S(1)}, f32[16,32,128]{2,1,0:T(8,128)}, u32[]{:S(2)}) copy-start(f32[16,32,128]{2,1,0:T(8,128)} %get-tuple-element.27.rows_ref) | copy-start | bytes 786436
  55.0 5.5 %copy-start.9 = (f32[16,8,256]{2,1,0:T(8,128)S(1)}, f32[16,8,256]{2,1,0:T(8,128)}, u32[]{:S(2)}) copy-start(f32[16,8,256]{2,1,0:T(8,128)} %get-tuple-element.28.lanes_ref) | copy-start | bytes 393220
  55.7 13.1 %collective-permute-start.1 = (f32[2,128,256]{2,1,0:T(8,128)S(1)}, f32[2,128,256]{2,1,0:T(8,128)S(1)}, u32[]{:S(2)}, u32[]{:S(2)}) collective-permute-start(f32[2,128,256]{2,1,0:T(8,128)S(1)} %get-tuple-element.41), channel_id=1, source_target_pairs={{0,2},{1,3},{2,0},{3,1},{4,6},{5,7},{6,4},{7,5},{8,10},{9,11},{10,... | collective-permute-start | bytes 786440 | tf_op jit(solution)/shard_map/ppermute | solution.py:627
  57.2 14.8 %collective-permute-start.2 = (f32[2,128,256]{2,1,0:T(8,128)S(1)}, f32[2,128,256]{2,1,0:T(8,128)S(1)}, u32[]{:S(2)}, u32[]{:S(2)}) collective-permute-start(f32[2,128,256]{2,1,0:T(8,128)S(1)} %get-tuple-element.42), channel_id=1, source_target_pairs={{0,4},{1,5},{2,6},{3,7},{4,0},{5,1},{6,2},{7,3},{8,12},{9,13},{10,... | collective-permute-start | bytes 786440 | tf_op jit(solution)/shard_map/ppermute | solution.py:627
  60.0 14.6 %collective-permute-start.3 = (f32[2,128,256]{2,1,0:T(8,128)S(1)}, f32[2,128,256]{2,1,0:T(8,128)S(1)}, u32[]{:S(2)}, u32[]{:S(2)}) collective-permute-start(f32[2,128,256]{2,1,0:T(8,128)S(1)} %get-tuple-element.43), channel_id=1, source_target_pairs={{0,6},{1,7},{2,4},{3,5},{4,2},{5,3},{6,0},{7,1},{8,14},{9,15},{10,... | collective-permute-start | bytes 786440 | tf_op jit(solution)/shard_map/ppermute | solution.py:627

commit v2 on v1

--- a/solution.py
+++ b/solution.py
@@ -22,6 +22,7 @@
 PART_LIMIT = 40 * 1024 * 1024
 LAST_LIMIT = 40 * 1024 * 1024
 CHUNK_LIMIT = 60 * 1024 * 1024
+DOWN_LIMIT = 60 * 1024 * 1024
 VMEM_LIMIT = 24 * 1024 * 1024
 
 
@@ -140,13 +141,15 @@
         rows_ref[k, 16:24, :] = jnp.exp(sums[8 * k : 8 * k + 8, SPAN : 2 * SPAN])
         whole = jnp.exp(tot[k])
         rows_ref[k, 24:32, :] = whole
-        edge_ref[k, 0:8, :] = jnp.exp(before + cin)
+        edge_ref[k, :HEADS_HERE, :] = jnp.exp(before + cin)[:HEADS_HERE]
         lanes_ref[k, 0:1, :] = by_head(whole)
         lanes_ref[k, 1:2, :] = by_head(jnp.exp(before))
         before = before + tot[k]
     after = jnp.zeros((8, SPAN), F32)
     for k in reversed(range(CHUNKS)):
-        edge_ref[k, 8:16, :] = jnp.exp(after + sums[8 * k : 8 * k + 8, SPAN : 2 * SPAN])
+        edge_ref[k, HEADS_HERE:, :] = jnp.exp(after + sums[8 * k : 8 * k + 8, SPAN : 2 * SPAN])[
+            :HEADS_HERE
+        ]
         lanes_ref[k, 2:3, :] = by_head(jnp.exp(after))
         lanes_ref[k, 3:8, :] = jnp.zeros((5, ROWS), F32)
         after = after + tot[k]
@@ -158,20 +161,18 @@
     x_ref, y_ref, b_ref, c_ref, log_ref, msg_ref, rows_ref, edge_ref, lanes_ref, bs_ref, cs_ref, wide_ref,
     get_sem, put_sem
 ):
-    top, low = pl.ds(0, ROWS // 2), pl.ds(ROWS // 2, ROWS // 2)
-    gets = [
-        pltpu.make_async_copy(src, dst, get_sem.at[n])
-        for n, (src, dst) in enumerate(
-            (
-                (log_hbm, log_ref),
-                (b_hbm, b_ref),
-                (x_hbm, x_ref),
-                (c_hbm, c_ref),
-                (y_hbm.at[top, :], y_ref.at[top, :]),
-                (y_hbm.at[low, :], y_ref.at[low, :]),
+    gets = [pltpu.make_async_copy(log_hbm, log_ref, get_sem.at[0])]
+    for q in range(2):
+        rows, cols = pl.ds(q * TOK, TOK), pl.ds(q * TOK // 2, TOK // 2)
+        for src, dst, part in (
+            (b_hbm, b_ref, (rows, slice(None))),
+            (x_hbm, x_ref, (slice(None), cols)),
+            (c_hbm, c_ref, (rows, slice(None))),
+            (y_hbm, y_ref, (slice(None), cols)),
+        ):
+            gets.append(
+                pltpu.make_async_copy(src.at[part], dst.at[part], get_sem.at[len(gets)])
             )
-        )
-    ]
     for copy in gets:
         copy.start()
     puts = []
@@ -193,44 +194,33 @@
     put(lanes_ref, lanes_hbm)
     put_message(2 * SLICE)
 
-    def select(src, dst, base):
-        out = []
-        for k in range(CHUNKS):
-            got = choose(src[2 * k * SPAN : 2 * (k + 1) * SPAN, :], wide_ref.at[base + k], group)
-            dst[k * SPAN : (k + 1) * SPAN, :] = got
-            turned = got.T
-            out.append(cat([turned, turned], 1))
-        return out
-
-    def gather(turned, src, row, first, heads):
-        total = jnp.zeros((STATE, heads * WIDTH), F32)
-        for k in range(CHUNKS):
-            scale = edge_ref[k, row : row + 8, :]
-            scale = cat(
-                [
-                    jnp.broadcast_to(scale[h : h + 1, :], (WIDTH, SPAN))
-                    for h in range(first, first + heads)
-                ],
-                0,
-            )
-            part = src[first * WIDTH : (first + heads) * WIDTH, k * SPAN : (k + 1) * SPAN]
-            total = total + dot_nt(turned[k], wide(part.astype(F32) * scale))
-        return total
-
-    gets[1].wait()
-    turned = select(b_ref, bs_ref, 0)
-    put(bs_ref, bs_hbm)
-    gets[2].wait()
-    to_slices(gather(turned, x_ref, 8, 0, HEADS_HERE), msg_ref, 0)
-    put_message(0)
-    gets[3].wait()
-    turned = select(c_ref, cs_ref, CHUNKS)
+    def gather(total, base, k, pairs_ref, chosen_ref, src, row):
+        got = choose(pairs_ref[2 * k * SPAN : 2 * (k + 1) * SPAN, :], wide_ref.at[base + k], group)
+        chosen_ref[k * SPAN : (k + 1) * SPAN, :] = got
+        turned = got.T
+        near = src[:, k * SPAN : (k + 1) * SPAN].astype(F32) * spread_rows(
+            edge_ref[k, row : row + HEADS_HERE, :]
+        )
+        return total + dot_nt(cat([turned, turned], 1), wide(near))
+
+    own = jnp.zeros((STATE, ROWS), F32)
+    back = jnp.zeros((STATE, ROWS), F32)
+    for q in range(2):
+        chunks = range(q * CHUNKS // 2, (q + 1) * CHUNKS // 2)
+        gets[4 * q + 1].wait()
+        gets[4 * q + 2].wait()
+        for k in chunks:
+            own = gather(own, 0, k, b_ref, bs_ref, x_ref, HEADS_HERE)
+        if q == 1:
+            put(bs_ref, bs_hbm)
+            to_slices(own, msg_ref, 0)
+            put_message(0)
+        gets[4 * q + 3].wait()
+        gets[4 * q + 4].wait()
+        for k in chunks:
+            back = gather(back, CHUNKS, k, c_ref, cs_ref, y_ref, 0)
     put(cs_ref, cs_hbm)
-    halves = []
-    for q in range(2):
-        gets[4 + q].wait()
-        halves.append(gather(turned, y_ref, 0, 2 * q, 2))
-    to_slices(cat(halves, 1), msg_ref, SLICE)
+    to_slices(back, msg_ref, SLICE)
     put_message(SLICE)
     for copy in puts:
         copy.wait()
@@ -245,7 +235,7 @@
         out_shape=[
             jax.ShapeDtypeStruct((SEQ, 3 * SLICE, STATE), F32),
             jax.ShapeDtypeStruct((CHUNKS, ROWSET, SPAN), F32),
-            jax.ShapeDtypeStruct((CHUNKS, 16, SPAN), F32),
+            jax.ShapeDtypeStruct((CHUNKS, 8, SPAN), F32),
             jax.ShapeDtypeStruct((CHUNKS, 8, ROWS), F32),
             jax.ShapeDtypeStruct((TOK, STATE), BF16),
             jax.ShapeDtypeStruct((TOK, STATE), BF16),
@@ -258,12 +248,12 @@
             pltpu.VMEM((HEADS_HERE, TOK), F32),
             pltpu.VMEM((SEQ, 3 * SLICE, STATE), F32),
             pltpu.VMEM((CHUNKS, ROWSET, SPAN), F32),
-            pltpu.VMEM((CHUNKS, 16, SPAN), F32),
+            pltpu.VMEM((CHUNKS, 8, SPAN), F32),
             pltpu.VMEM((CHUNKS, 8, ROWS), F32),
             pltpu.VMEM((TOK, STATE), BF16),
             pltpu.VMEM((TOK, STATE), BF16),
             pltpu.VMEM((2 * CHUNKS, 2 * SPAN, STATE), F32),
-            pltpu.SemaphoreType.DMA((6,)),
+            pltpu.SemaphoreType.DMA((9,)),
             pltpu.SemaphoreType.DMA((8,)),
         ],
         compiler_params=pltpu.CompilerParams(vmem_limit_bytes=FIRST_LIMIT),
@@ -327,7 +317,22 @@
 PER2 = 8
 
 
-def ascend_kernel(x_ref, y_ref, b_ref, c_ref, rows_ref, lanes_ref, db_ref, dc_ref, s_ref, state):
+HALF = 256
+
+
+def by_side(blocks, send_ref, keep_ref):
+    second = lax.axis_index("head") % 2 == 1
+    for a in range(len(blocks) // 2):
+        even, odd = blocks[2 * a], blocks[2 * a + 1]
+        send_ref[a] = jnp.where(second, even, odd)
+        keep_ref[a] = jnp.where(second, odd, even)
+
+
+def halves(chunks):
+    return [cat([chunks[2 * j], chunks[2 * j + 1]], 1) for j in range(len(chunks) // 2)]
+
+
+def ascend_kernel(x_ref, y_ref, b_ref, c_ref, rows_ref, lanes_ref, db_ref, send_ref, keep_ref, s_ref, state):
     @pl.when(pl.program_id(0) == 0)
     def _():
         state[...] = jnp.zeros((STATE, ROWS), F32)
@@ -335,6 +340,7 @@
     r, l = iotas((SPAN, SPAN))
     mask = l >= r
     own = state[...]
+    chunks = []
     for k in range(PER2):
         here = slice(k * SPAN, (k + 1) * SPAN)
         x = x_ref[:, here]
@@ -346,12 +352,13 @@
         hi, lo = split2(total)
         db_ref[:, here] = dot_nt(cat([ct, ct], 1), cat([hi, lo], 1))
         yhi, ylo = split2(y_ref[:, here].astype(F32) * spread_rows(rows_ref[k, 8:16, :]))
-        dc_ref[:, here] = dot_nn(twice, cat([hi, lo], 0)) + inter(yhi, ylo, own)
+        chunks.append(dot_nn(twice, cat([hi, lo], 0)) + inter(yhi, ylo, own))
         s_ref[k * STATE : (k + 1) * STATE, :] = own
         own = own * lanes_ref[k, 0:1, :] + dot_nt(
             twice, wide(x.astype(F32) * spread_rows(rows_ref[k, 16:24, :]))
         )
     state[...] = own
+    by_side(halves(chunks), send_ref, keep_ref)
 
 
 def chunk_specs(per, order):
@@ -365,21 +372,21 @@
     ]
 
 
+def side_specs(per, order):
+    return [pl.BlockSpec((per // 4, STATE, HALF), lambda i: (order(i), 0, 0))] * 2
+
+
 def ascend(x, y, b, c, rows, lanes):
-    tokens = pl.BlockSpec((STATE, PER2 * SPAN), lambda i: (0, i))
     return pl.pallas_call(
         ascend_kernel,
         grid=(CHUNKS // PER2,),
         in_specs=chunk_specs(PER2, lambda i: i),
-        out_specs=[
-            tokens,
-            tokens,
-            pl.BlockSpec((PER2 * STATE, ROWS), lambda i: (i, 0)),
-        ],
-        out_shape=[jax.ShapeDtypeStruct((STATE, TOK), F32)] * 2
-        + [
-            jax.ShapeDtypeStruct((CHUNKS * STATE, ROWS), F32),
-        ],
+        out_specs=[pl.BlockSpec((STATE, PER2 * SPAN), lambda i: (0, i))]
+        + side_specs(PER2, lambda i: i)
+        + [pl.BlockSpec((PER2 * STATE, ROWS), lambda i: (i, 0))],
+        out_shape=[jax.ShapeDtypeStruct((STATE, TOK), F32)]
+        + [jax.ShapeDtypeStruct((4, STATE, HALF), F32)] * 2
+        + [jax.ShapeDtypeStruct((CHUNKS * STATE, ROWS), F32)],
         scratch_shapes=[pltpu.VMEM((STATE, ROWS), F32)],
         compiler_params=pltpu.CompilerParams(vmem_limit_bytes=CHUNK_LIMIT),
         cost_estimate=pl.CostEstimate(flops=3_000_000_000, bytes_accessed=8_000_000, transcendentals=1_000_000),
@@ -390,22 +397,24 @@
 PER3 = 8
 
 
-def descend_kernel(x_ref, y_ref, c_ref, rows_ref, lanes_ref, dbp_ref, db_ref, d_ref, grad):
+def descend_kernel(x_ref, y_ref, c_ref, rows_ref, lanes_ref, dbp_ref, send_ref, keep_ref, d_ref, grad):
     @pl.when(pl.program_id(0) == 0)
     def _():
         grad[...] = jnp.zeros((STATE, ROWS), F32)
 
     back = grad[...]
+    chunks = [None] * PER3
     for k in reversed(range(PER3)):
         here = slice(k * SPAN, (k + 1) * SPAN)
         xhi, xlo = split2(x_ref[:, here].astype(F32) * spread_rows(rows_ref[k, 16:24, :]))
-        db_ref[:, here] = dbp_ref[:, here] + inter(xhi, xlo, back)
+        chunks[k] = dbp_ref[:, here] + inter(xhi, xlo, back)
         d_ref[k * STATE : (k + 1) * STATE, :] = back
         ct = c_ref[here, :].T
         back = back * lanes_ref[k, 0:1, :] + dot_nt(
             cat([ct, ct], 1), wide(y_ref[:, here].astype(F32) * spread_rows(rows_ref[k, 8:16, :]))
         )
     grad[...] = back
+    by_side(halves(chunks), send_ref, keep_ref)
 
 
 def descend(x, y, c, rows, lanes, dbp):
@@ -418,82 +427,46 @@
         descend_kernel,
         grid=(steps,),
         in_specs=specs[:2] + specs[3:] + [tokens],
-        out_specs=[tokens, states],
+        out_specs=side_specs(PER3, order) + [states],
         out_shape=[
-            jax.ShapeDtypeStruct((STATE, TOK), F32),
+            jax.ShapeDtypeStruct((4, STATE, HALF), F32),
+            jax.ShapeDtypeStruct((4, STATE, HALF), F32),
             jax.ShapeDtypeStruct((CHUNKS * STATE, ROWS), F32),
         ],
         scratch_shapes=[pltpu.VMEM((STATE, ROWS), F32)],
-        compiler_params=pltpu.CompilerParams(vmem_limit_bytes=CHUNK_LIMIT),
+        compiler_params=pltpu.CompilerParams(vmem_limit_bytes=DOWN_LIMIT),
         cost_estimate=pl.CostEstimate(flops=3_000_000_000, bytes_accessed=8_000_000, transcendentals=0),
         name="chunks_descending",
     )(x, y, c, rows, lanes, dbp)
 
 
-HALF = 256
-
-
-def part_kernel(
-    side, bound_ref, edge_hbm, x_hbm, y_hbm, db_hbm, dc_hbm, out_hbm,
-    edge_ref, x_ref, y_ref, both_ref, out_ref, get_sem, put_sem
-):
-    place = lax.axis_index("head")
-    chip, core = place // 2, place % 2
-    gets = []
-    for i in range(4):
-        block = 2 * jnp.bitwise_xor(chip, i) + jnp.bitwise_xor(core, side)
-        cols = pl.ds(pl.multiple_of(block * HALF, HALF), HALF)
-        gets.append(
-            [
-                pltpu.make_async_copy(
-                    edge_hbm.at[pl.ds(2 * block, 2)], edge_ref.at[i], get_sem.at[i, 0]
-                ),
-                pltpu.make_async_copy(x_hbm.at[:, cols], x_ref.at[i], get_sem.at[i, 1]),
-                pltpu.make_async_copy(y_hbm.at[:, cols], y_ref.at[i], get_sem.at[i, 2]),
-                pltpu.make_async_copy(db_hbm.at[:, cols], both_ref.at[i, 0], get_sem.at[i, 3]),
-                pltpu.make_async_copy(dc_hbm.at[:, cols], both_ref.at[i, 1], get_sem.at[i, 4]),
-            ]
-        )
-        for copy in gets[i]:
-            copy.start()
-    edges = [split2(from_slices(bound_ref, place)) for place in (SLICE, 0)]
-    stacks = [cat(list(edge), 0) for edge in edges]
-    puts = []
-    for i in range(4):
-        for copy in gets[i]:
-            copy.wait()
-        for t, (row, src) in enumerate(((8, x_ref), (0, y_ref))):
+def part_kernel(side, bound_ref, edge_ref, x_ref, y_ref, db_ref, dc_ref, out_ref):
+    index = lax.axis_index("head")
+    chip, core = index // 2, index % 2
+    for t, (place, row, src, held) in enumerate(
+        ((SLICE, HEADS_HERE, x_ref, db_ref), (0, 0, y_ref, dc_ref))
+    ):
+        edge = split2(from_slices(bound_ref, place))
+        stack = cat(list(edge), 0)
+        for i in range(4):
+            to = jnp.bitwise_xor(chip, i)
+            block = 2 * to + jnp.bitwise_xor(core, side)
+            cols = pl.ds(pl.multiple_of(block * HALF, HALF), HALF)
             scale = cat(
-                [spread_rows(edge_ref[i, k, row : row + 8, :]) for k in range(HALF // SPAN)], 1
+                [spread_rows(edge_ref[2 * block + k, row : row + HEADS_HERE, :]) for k in range(2)], 1
             )
-            near_hi, near_lo = split2(src[i].astype(F32) * scale)
-            first = dot_nn(stacks[t], near_hi)
-            out_ref[i, t] = both_ref[i, t] + (
-                first[:STATE] + (first[STATE:] + dot_nn(edges[t][0], near_lo))
-            )
-        copy = pltpu.make_async_copy(out_ref.at[i], out_hbm.at[i], put_sem.at[i])
-        copy.start()
-        puts.append(copy)
-    for copy in puts:
-        copy.wait()
+            near_hi, near_lo = split2(src[:, cols].astype(F32) * scale)
+            first = dot_nn(stack, near_hi)
+            out_ref[i, t] = held[to] + (first[:STATE] + (first[STATE:] + dot_nn(edge[0], near_lo)))
 
 
 def part_pass(name, side, bound, edge, x, y, db, dc):
-    hbm = pl.BlockSpec(memory_space=pltpu.HBM)
+    vmem = pl.BlockSpec(memory_space=pltpu.VMEM)
     return pl.pallas_call(
         functools.partial(part_kernel, side),
-        in_specs=[pl.BlockSpec(memory_space=pltpu.VMEM)] + [hbm] * 5,
-        out_specs=hbm,
+        in_specs=[vmem] * 6,
+        out_specs=vmem,
         out_shape=jax.ShapeDtypeStruct((4, 2, STATE, HALF), F32),
-        scratch_shapes=[
-            pltpu.VMEM((4, 2, 16, SPAN), F32),
-            pltpu.VMEM((4, ROWS, HALF), BF16),
-            pltpu.VMEM((4, ROWS, HALF), BF16),
-            pltpu.VMEM((4, 2, STATE, HALF), F32),
-            pltpu.VMEM((4, 2, STATE, HALF), F32),
-            pltpu.SemaphoreType.DMA((4, 5)),
-            pltpu.SemaphoreType.DMA((4,)),
-        ],
         compiler_params=pltpu.CompilerParams(vmem_limit_bytes=PART_LIMIT),
         cost_estimate=pl.CostEstimate(flops=500_000_000, bytes_accessed=3_000_000, transcendentals=0),
         name=name,
@@ -615,13 +588,13 @@
     c2 = out_proj.reshape(2 * TOK, STATE)
     message, rows, edge, lanes, b, c = first_pass(x, y, b2, c2, log)
     got = lax.all_to_all(message, "seq", 0, 0)
-    dbp, dc, s = ascend(x, y, b, c, rows, lanes)
+    dbp, dc_send, dc_keep, s = ascend(x, y, b, c, rows, lanes)
     got, dbp = lax.optimization_barrier((got, dbp))
     bound = lax.all_to_all(scan_blocks(got), "seq", 0, 0)
-    db, d = descend(x, y, c, rows, lanes, dbp)
-    sent = part_pass("projections_send", 1, bound, edge, x, y, db, dc)
+    db_send, db_keep, d = descend(x, y, c, rows, lanes, dbp)
+    sent = part_pass("projections_send", 1, bound, edge, x, y, db_send, dc_send)
     other = lax.ppermute(sent, "head", [(i, i ^ 1) for i in range(8)])
-    kept = part_pass("projections_keep", 0, bound, edge, x, y, db, dc)
+    kept = part_pass("projections_keep", 0, bound, edge, x, y, db_keep, dc_keep)
     parts = sum_pass(kept, other)
     moved = [
         lax.ppermute(parts[m], "head", [(i, i ^ (2 * m)) for i in range(8)]) for m in (1, 2, 3)

time: 75.8 us -> 73.7 us (0.972)
  Pallas kernels: 34.5 us -> 31.1 us
  waiting for transfers between devices: 18 us -> 19 us
    pallas_call x2, Pallas kernels: 3.97 us -> 1.33 us  [part_pass(): pl.pallas_call(functools.partial(part_kernel, side), in_specs=[vmem] * 6,...]
    ppermute x1, waiting for transfers between devices: 0.56 us -> 1.52 us  [local(): other = lax.ppermute(sent, 'head', [(i, i ^ 1) for i in range(8)])]
where the time goes in v2:
time: 73.7 us; the launch traced here: 73.4 us
  Pallas kernels  31.1 us (42%)
  starting transfers between devices  21 us (28%)
  waiting for transfers between devices  19 us (26%)
  local copies, waits for them, and re-layouts  1.5 us (2%)
  between operations  0.79 us (1%)
    all_to_all x1, starting transfers between devices, local(): got = lax.all_to_all(message, 'seq', 0, 0)  11.4 us
    pallas_call x1, Pallas kernels, last_pass(): pl.pallas_call(last_kernel, grid=(CHUNKS // PER5,), in_specs=chunk_specs(...  8.26 us
    pallas_call x1, Pallas kernels, ascend(): pl.pallas_call(ascend_kernel, grid=(CHUNKS // PER2,), in_specs=chunk_spec...  8.2 us
    pallas_call x1, Pallas kernels, descend(): pl.pallas_call(descend_kernel, grid=(steps,), in_specs=specs[:2] + specs[...  6.74 us
    all_to_all x1, waiting for transfers between devices, local(): got = lax.all_to_all(message, 'seq', 0, 0)  6.68 us
    ppermute x3, waiting for transfers between devices, local(): lax.ppermute(parts[m], 'head', [(i, i ^ 2 * m) for i in range(8)])  5.84 us
    all_to_all x1, waiting for transfers between devices, local(): bound = lax.all_to_all(scan_blocks(got), 'seq', 0, 0)  4.96 us
    ppermute x3, starting transfers between devices, local(): lax.ppermute(parts[m], 'head', [(i, i ^ 2 * m) for i in range(8)])  4.79 us
  transfers between devices with their start and end apart: 6, of which 5 were waited for; matrix products, arithmetic and copies ran while one was open for 0% of the time, Pallas kernels for 33%

profile of v2, /device:TPU:32, one launch (start us, length us, event | category | flops | bytes accessed | tf_op | source)
XLA Modules:
  0.0 73.4 jit_solution(9962990250286673992)
XLA Ops:
  0.6 4.7 %own_states.1 = (f32[32,24,128]{2,1,0:T(8,128)}, f32[16,32,128]{2,1,0:T(8,128)}, f32[16,8,128]{2,1,0:T(8,128)}, f32[16,8,256]{2,1,0:T(8,128)}, bf16[2048,128]{1,0:T(8,128)(2,1)}, /*index=5*/bf16[2048,128]{1,0:T(8,128)(2,1)}) custom-call(bf16[256,2048]{1,0:T(8,128)(2,1)} %bitcast.15, bf16[256,2048]{1,0:T(8,128)(2,1)} %bitcast.21, bf16[4096,128]{1,0:T(8,128)(2,1)} %bitcast.27, ...), custom_call_target="tpu_custom_call" | custom-call | flops 800000000 | bytes 6000000 | tf_op jit(solution)/shard_map/own_states/pallas_call | solution.py:231
  5.4 11.4 %all-to-all-start = ((f32[32,24,128]{2,1,0:T(8,128)}), f32[32,24,128]{2,1,0:T(8,128)S(1)}, u32[]{:S(2)}, u32[]{:S(2)}) async-start(f32[32,24,128]{2,1,0:T(8,128)} %get-tuple-element.31), calls=%async_computation | async-start | bytes 786432 | tf_op jit(solution)/shard_map/all_to_all | solution.py:590
  16.7 8.2 %chunks_ascending.1 = (f32[128,2048]{1,0:T(8,128)}, f32[4,128,256]{2,1,0:T(8,128)}, f32[4,128,256]{2,1,0:T(8,128)}, f32[2048,256]{1,0:T(8,128)}) custom-call(bf16[256,2048]{1,0:T(8,128)(2,1)} %bitcast.16, bf16[256,2048]{1,0:T(8,128)(2,1)} %bitcast.22, bf16[2048,128]{1,0:T(8,128)(2,1)} %get-tuple-element.27.b_ref, bf16[2048,128]{1,0:T(8,128)(2,1)} %get-tuple-element.28.c_ref, ...), custom_call_target="tpu_custom_call" | custom-call | flops 3000000000 | bytes 8000000 | tf_op jit(solution)/shard_map/chunks_ascending/pallas_call | solution.py:380
  24.9 6.7 %all-to-all-done.got_ref = f32[32,24,128]{2,1,0:T(8,128)S(1)} async-done(((f32[32,24,128]{2,1,0:T(8,128)}), f32[32,24,128]{2,1,0:T(8,128)S(1)}, u32[]{:S(2)}, u32[]{:S(2)}) %all-to-all-start) | async-done | bytes 393248 | tf_op jit(solution)/shard_map/all_to_all | solution.py:590
  31.6 0.8 %scan_blocks.1 = f32[32,16,128]{2,1,0:T(8,128)} custom-call(f32[32,24,128]{2,1,0:T(8,128)S(1)} %all-to-all-done.got_ref), custom_call_target="tpu_custom_call" | custom-call | tf_op jit(solution)/shard_map/scan_blocks/pallas_call | solution.py:279
  32.4 4.8 %all-to-all-start.1 = ((f32[32,16,128]{2,1,0:T(8,128)}), f32[32,16,128]{2,1,0:T(8,128)S(1)}, u32[]{:S(2)}, u32[]{:S(2)}) async-start(f32[32,16,128]{2,1,0:T(8,128)} %scan_blocks.1), calls=%async_computation.1 | async-start | bytes 524288 | tf_op jit(solution)/shard_map/all_to_all | solution.py:593
  37.2 0.0 copy-start
  37.2 0.0 copy-start.1
  37.2 0.0 copy-start.3
  37.2 0.0 copy-start.6
  37.2 6.7 %chunks_descending.1 = (f32[4,128,256]{2,1,0:T(8,128)}, f32[4,128,256]{2,1,0:T(8,128)}, f32[2048,256]{1,0:T(8,128)}) custom-call(bf16[256,2048]{1,0:T(8,128)(2,1)} %bitcast.17, bf16[256,2048]{1,0:T(8,128)(2,1)} %bitcast.23, bf16[2048,128]{1,0:T(8,128)(2,1)} %get-tuple-element.28.c_ref, f32[16,32,128]{2,1,0:T(8,128)} %get-tuple-element.29.rows_ref, ...), custom_call_target="tpu_custom_call" | custom-call | flops 3000000000 | bytes 8000000 | tf_op jit(solution)/shard_map/chunks_descending/pallas_call | solution.py:426
  44.0 5.0 %all-to-all-done.1.bound_ref = f32[32,16,128]{2,1,0:T(8,128)S(1)} async-done(((f32[32,16,128]{2,1,0:T(8,128)}), f32[32,16,128]{2,1,0:T(8,128)S(1)}, u32[]{:S(2)}, u32[]{:S(2)}) %all-to-all-start.1) | async-done | bytes 262176 | tf_op jit(solution)/shard_map/all_to_all | solution.py:593
  48.9 0.0 copy-done
  49.0 1.0 %copy-done.5 = f32[4,128,256]{2,1,0:T(8,128)S(1)} copy-done((f32[4,128,256]{2,1,0:T(8,128)S(1)}, f32[4,128,256]{2,1,0:T(8,128)}, u32[]{:S(2)}) %copy-start.5) | copy-done | bytes 524312
  50.0 0.7 projections_send.1
  50.7 0.1 collective-permute-start
  50.8 0.3 copy-done.2
  51.0 0.2 copy-done.4
  51.2 0.7 projections_keep.1.kept_ref
  51.9 0.0 copy-start.9
  51.9 0.0 copy-start.10
  51.9 1.5 %collective-permute-done.got_ref = f32[4,2,128,256]{3,2,1,0:T(8,128)S(1)} collective-permute-done((f32[4,2,128,256]{3,2,1,0:T(8,128)S(1)}, f32[4,2,128,256]{3,2,1,0:T(8,128)S(1)}, u32[]{:S(2)}, u32[]{:S(2)}) %collective-permute-start) | collective-permute-done | bytes 1048608 | tf_op jit(solution)/shard_map/ppermute | solution.py:596
  53.4 0.1 sum_cores.1
  53.5 1.6 %collective-permute-start.1 = (f32[2,128,256]{2,1,0:T(8,128)S(1)}, f32[2,128,256]{2,1,0:T(8,128)S(1)}, u32[]{:S(2)}, u32[]{:S(2)}) collective-permute-start(f32[2,128,256]{2,1,0:T(8,128)S(1)} %get-tuple-element.45), channel_id=1, source_target_pairs={{0,2},{1,3},{2,0},{3,1},{4,6},{5,7},{6,4},{7,5},{8,10},{9,11},{10,... | collective-permute-start | bytes 786440 | tf_op jit(solution)/shard_map/ppermute | solution.py:600
  55.1 2.7 %collective-permute-start.2 = (f32[2,128,256]{2,1,0:T(8,128)S(1)}, f32[2,128,256]{2,1,0:T(8,128)S(1)}, u32[]{:S(2)}, u32[]{:S(2)}) collective-permute-start(f32[2,128,256]{2,1,0:T(8,128)S(1)} %get-tuple-element.46), channel_id=1, source_target_pairs={{0,4},{1,5},{2,6},{3,7},{4,0},{5,1},{6,2},{7,3},{8,12},{9,13},{10,... | collective-permute-start | bytes 786440 | tf_op jit(solution)/shard_map/ppermute | solution.py:600
  57.8 0.5 collective-permute-start.3
  58.3 0.0 copy-done.8
  58.4 8.3 %inputs_and_decay.1 = (bf16[256,2048]{1,0:T(8,128)(2,1)}, f32[4,2048]{1,0:T(4,128)}) custom-call(bf16[256,2048]{1,0:T(8,128)(2,1)S(1)} %bitcast.20, bf16[256,2048]{1,0:T(8,128)(2,1)S(1)} %bitcast.26, bf16[2048,128]{1,0:T(8,128)(2,1)S(1)} %copy-done.7, bf16[2048,128]{1,0:T(8,128)(2,1)S(1)} %copy-done.8, f32[16,32,128]{2,1,0:T(8,128)S(1)} %copy-done.9, ...), custom_call_target="tpu_custom_call" | custom-call | flops 6000000000 | bytes 12000000 | tf_op jit(solution)/shard_map/inputs_and_decay/pallas_call | solution.py:541
  66.6 0.0 collective-permute-done.1.near_ref
  66.6 3.3 %collective-permute-done.2.far_ref = f32[2,128,256]{2,1,0:T(8,128)S(1)} collective-permute-done((f32[2,128,256]{2,1,0:T(8,128)S(1)}, f32[2,128,256]{2,1,0:T(8,128)S(1)}, u32[]{:S(2)}, u32[]{:S(2)}) %collective-permute-start.2) | collective-permute-done | bytes 262176 | tf_op jit(solution)/shard_map/ppermute | solution.py:600
  69.9 2.6 %collective-permute-done.3.side_ref = f32[2,128,256]{2,1,0:T(8,128)S(1)} collective-permute-done((f32[2,128,256]{2,1,0:T(8,128)S(1)}, f32[2,128,256]{2,1,0:T(8,128)S(1)}, u32[]{:S(2)}, u32[]{:S(2)}) %collective-permute-start.3) | collective-permute-done | bytes 262176 | tf_op jit(solution)/shard_map/ppermute | solution.py:600
  72.5 0.9 %merge.1 = (f32[512,128]{1,0:T(8,128)}, f32[512,128]{1,0:T(8,128)}) custom-call(f32[2,128,256]{2,1,0:T(8,128)S(1)} %get-tuple-element.44.own_ref, f32[2,128,256]{2,1,0:T(8,128)S(1)} %collective-permute-done.1.near_ref, f32[2,128,256]{2,1,0:T(8,128)S(1)} %collective-permute-done.2.far_ref, f32[2,128,256]{2,1,0:T(8,128)S(1)} %collective-permute-done.3.side_ref), custom_call_target="tpu_custom_call" | custom-call | tf_op jit(solution)/shard_map/merge/pallas_call | solution.py:573
  (15 shorter events, 0.0 us)
Async XLA Ops:
  5.4 26.3 %all-to-all-start = ((f32[32,24,128]{2,1,0:T(8,128)}), f32[32,24,128]{2,1,0:T(8,128)S(1)}, u32[]{:S(2)}, u32[]{:S(2)}) async-start(f32[32,24,128]{2,1,0:T(8,128)} %get-tuple-element.31), calls=%async_computation | async-start | bytes 786432 | tf_op jit(solution)/shard_map/all_to_all | solution.py:590
  32.4 16.5 %all-to-all-start.1 = ((f32[32,16,128]{2,1,0:T(8,128)}), f32[32,16,128]{2,1,0:T(8,128)S(1)}, u32[]{:S(2)}, u32[]{:S(2)}) async-start(f32[32,16,128]{2,1,0:T(8,128)} %scan_blocks.1), calls=%async_computation.1 | async-start | bytes 524288 | tf_op jit(solution)/shard_map/all_to_all | solution.py:593
  37.2 11.7 %copy-start = (bf16[2048,4,64]{0,2,1:T(8,128)(2,1)S(1)}, bf16[2048,4,64]{0,2,1:T(8,128)(2,1)}, u32[]{:S(2)}) copy-start(bf16[2048,4,64]{0,2,1:T(8,128)(2,1)} %param.5) | copy-start | bytes 3145732
  37.2 11.7 %copy-start.1 = (bf16[2048,4,64]{0,2,1:T(8,128)(2,1)S(1)}, bf16[2048,4,64]{0,2,1:T(8,128)(2,1)}, u32[]{:S(2)}) copy-start(bf16[2048,4,64]{0,2,1:T(8,128)(2,1)} %param.9) | copy-start | bytes 3145732
  37.2 11.7 %copy-start.3 = (f32[4,128,256]{2,1,0:T(8,128)S(1)}, f32[4,128,256]{2,1,0:T(8,128)}, u32[]{:S(2)}) copy-start(f32[4,128,256]{2,1,0:T(8,128)} %get-tuple-element.43.dc_ref) | copy-start | bytes 1572868
  37.2 11.7 %copy-start.6 = (f32[16,8,128]{2,1,0:T(8,128)S(1)}, f32[16,8,128]{2,1,0:T(8,128)}, u32[]{:S(2)}) copy-start(f32[16,8,128]{2,1,0:T(8,128)} %get-tuple-element.39.edge_ref) | copy-start | bytes 196612
  49.0 1.0 %copy-start.5 = (f32[4,128,256]{2,1,0:T(8,128)S(1)}, f32[4,128,256]{2,1,0:T(8,128)}, u32[]{:S(2)}) copy-start(f32[4,128,256]{2,1,0:T(8,128)} %get-tuple-element.42.db_ref) | copy-start | bytes 1572868
  50.0 1.0 %copy-start.2 = (f32[4,128,256]{2,1,0:T(8,128)S(1)}, f32[4,128,256]{2,1,0:T(8,128)}, u32[]{:S(2)}) copy-start(f32[4,128,256]{2,1,0:T(8,128)} %get-tuple-element.41.dc_ref) | copy-start | bytes 1572868
  50.0 1.2 %copy-start.4 = (f32[4,128,256]{2,1,0:T(8,128)S(1)}, f32[4,128,256]{2,1,0:T(8,128)}, u32[]{:S(2)}) copy-start(f32[4,128,256]{2,1,0:T(8,128)} %get-tuple-element.40.db_ref) | copy-start | bytes 1572868
  50.7 2.7 %collective-permute-start = (f32[4,2,128,256]{3,2,1,0:T(8,128)S(1)}, f32[4,2,128,256]{3,2,1,0:T(8,128)S(1)}, u32[]{:S(2)}, u32[]{:S(2)}) collective-permute-start(f32[4,2,128,256]{3,2,1,0:T(8,128)S(1)} %projections_send.1), channel_id=1, source_target_pairs={{0,1},{1,0},{2,3},{3,2},{4,5},{5,4},{6,7},{7,6},{8,9},{9,8},{10,11... | collective-permute-start | bytes 3145736 | tf_op jit(solution)/shard_map/ppermute | solution.py:596
  51.2 7.1 %copy-start.11 = (f32[2048,256]{1,0:T(8,128)S(1)}, f32[2048,256]{1,0:T(8,128)}, u32[]{:S(2)}) copy-start(f32[2048,256]{1,0:T(8,128)} %get-tuple-element.36.d_ref) | copy-start | bytes 6291460
  51.2 7.1 %copy-start.12 = (f32[2048,256]{1,0:T(8,128)S(1)}, f32[2048,256]{1,0:T(8,128)}, u32[]{:S(2)}) copy-start(f32[2048,256]{1,0:T(8,128)} %get-tuple-element.34.s_ref) | copy-start | bytes 6291460
  51.9 6.5 %copy-start.7 = (bf16[2048,128]{1,0:T(8,128)(2,1)S(1)}, bf16[2048,128]{1,0:T(8,128)(2,1)}, u32[]{:S(2)}) copy-start(bf16[2048,128]{1,0:T(8,128)(2,1)} %get-tuple-element.27.b_ref) | copy-start | bytes 1572868
  51.9 6.5 %copy-start.8 = (bf16[2048,128]{1,0:T(8,128)(2,1)S(1)}, bf16[2048,128]{1,0:T(8,128)(2,1)}, u32[]{:S(2)}) copy-start(bf16[2048,128]{1,0:T(8,128)(2,1)} %get-tuple-element.28.c_ref) | copy-start | bytes 1572868
  51.9 6.5 %copy-start.9 = (f32[16,32,128]{2,1,0:T(8,128)S(1)}, f32[16,32,128]{2,1,0:T(8,128)}, u32[]{:S(2)}) copy-start(f32[16,32,128]{2,1,0:T(8,128)} %get-tuple-element.29.rows_ref) | copy-start | bytes 786436
  51.9 6.4 %copy-start.10 = (f32[16,8,256]{2,1,0:T(8,128)S(1)}, f32[16,8,256]{2,1,0:T(8,128)}, u32[]{:S(2)}) copy-start(f32[16,8,256]{2,1,0:T(8,128)} %get-tuple-element.30.lanes_ref) | copy-start | bytes 393220
  53.5 13.1 %collective-permute-start.1 = (f32[2,128,256]{2,1,0:T(8,128)S(1)}, f32[2,128,256]{2,1,0:T(8,128)S(1)}, u32[]{:S(2)}, u32[]{:S(2)}) collective-permute-start(f32[2,128,256]{2,1,0:T(8,128)S(1)} %get-tuple-element.45), channel_id=1, source_target_pairs={{0,2},{1,3},{2,0},{3,1},{4,6},{5,7},{6,4},{7,5},{8,10},{9,11},{10,... | collective-permute-start | bytes 786440 | tf_op jit(solution)/shard_map/ppermute | solution.py:600
  55.1 14.8 %collective-permute-start.2 = (f32[2,128,256]{2,1,0:T(8,128)S(1)}, f32[2,128,256]{2,1,0:T(8,128)S(1)}, u32[]{:S(2)}, u32[]{:S(2)}) collective-permute-start(f32[2,128,256]{2,1,0:T(8,128)S(1)} %get-tuple-element.46), channel_id=1, source_target_pairs={{0,4},{1,5},{2,6},{3,7},{4,0},{5,1},{6,2},{7,3},{8,12},{9,13},{10,... | collective-permute-start | bytes 786440 | tf_op jit(solution)/shard_map/ppermute | solution.py:600
  57.8 14.6 %collective-permute-start.3 = (f32[2,128,256]{2,1,0:T(8,128)S(1)}, f32[2,128,256]{2,1,0:T(8,128)S(1)}, u32[]{:S(2)}, u32[]{:S(2)}) collective-permute-start(f32[2,128,256]{2,1,0:T(8,128)S(1)} %get-tuple-element.47), channel_id=1, source_target_pairs={{0,6},{1,7},{2,4},{3,5},{4,2},{5,3},{6,0},{7,1},{8,14},{9,15},{10,... | collective-permute-start | bytes 786440 | tf_op jit(solution)/shard_map/ppermute | solution.py:600

commit v3 on v2

--- a/solution.py
+++ b/solution.py
@@ -440,54 +440,60 @@
     )(x, y, c, rows, lanes, dbp)
 
 
-def part_kernel(side, bound_ref, edge_ref, x_ref, y_ref, db_ref, dc_ref, out_ref):
+def blocks_of(side, place, row, bound_ref, edge_ref, src, held):
     index = lax.axis_index("head")
     chip, core = index // 2, index % 2
-    for t, (place, row, src, held) in enumerate(
-        ((SLICE, HEADS_HERE, x_ref, db_ref), (0, 0, y_ref, dc_ref))
-    ):
-        edge = split2(from_slices(bound_ref, place))
-        stack = cat(list(edge), 0)
-        for i in range(4):
-            to = jnp.bitwise_xor(chip, i)
-            block = 2 * to + jnp.bitwise_xor(core, side)
-            cols = pl.ds(pl.multiple_of(block * HALF, HALF), HALF)
-            scale = cat(
-                [spread_rows(edge_ref[2 * block + k, row : row + HEADS_HERE, :]) for k in range(2)], 1
-            )
-            near_hi, near_lo = split2(src[:, cols].astype(F32) * scale)
-            first = dot_nn(stack, near_hi)
-            out_ref[i, t] = held[to] + (first[:STATE] + (first[STATE:] + dot_nn(edge[0], near_lo)))
-
-
-def part_pass(name, side, bound, edge, x, y, db, dc):
+    edge = split2(from_slices(bound_ref, place))
+    stack = cat(list(edge), 0)
+    for i in range(4):
+        to = jnp.bitwise_xor(chip, i)
+        block = 2 * to + jnp.bitwise_xor(core, side)
+        cols = pl.ds(pl.multiple_of(block * HALF, HALF), HALF)
+        scale = cat(
+            [spread_rows(edge_ref[2 * block + k, row : row + HEADS_HERE, :]) for k in range(2)], 1
+        )
+        near_hi, near_lo = split2(src[:, cols].astype(F32) * scale)
+        first = dot_nn(stack, near_hi)
+        yield i, held[to] + (first[:STATE] + (first[STATE:] + dot_nn(edge[0], near_lo)))
+
+
+def send_out_kernel(bound_ref, edge_ref, y_ref, held_ref, out_ref):
+    for i, block in blocks_of(1, 0, 0, bound_ref, edge_ref, y_ref, held_ref):
+        out_ref[i] = block
+
+
+def send_in_kernel(bound_ref, edge_ref, x_ref, held_ref, far_ref, own_ref):
+    for i, block in blocks_of(1, SLICE, HEADS_HERE, bound_ref, edge_ref, x_ref, held_ref):
+        if i == 0:
+            own_ref[...] = block
+        else:
+            far_ref[i - 1] = block
+
+
+def keep_kernel(bound_ref, edge_ref, x_ref, y_ref, in_ref, out_ref, kept_ref):
+    for i, block in blocks_of(0, SLICE, HEADS_HERE, bound_ref, edge_ref, x_ref, in_ref):
+        kept_ref[i, 0] = block
+    for i, block in blocks_of(0, 0, 0, bound_ref, edge_ref, y_ref, out_ref):
+        kept_ref[i, 1] = block
+
+
+def sum_kernel(kept_ref, out_ref, in_ref, *outs):
+    for m in range(4):
+        outs[m][0] = kept_ref[m, 0] + in_ref[m - 1] if m else kept_ref[m, 0]
+        outs[m][1] = kept_ref[m, 1] + out_ref[m]
+
+
+def in_vmem(name, kernel, shapes, *operands):
     vmem = pl.BlockSpec(memory_space=pltpu.VMEM)
     return pl.pallas_call(
-        functools.partial(part_kernel, side),
-        in_specs=[vmem] * 6,
-        out_specs=vmem,
-        out_shape=jax.ShapeDtypeStruct((4, 2, STATE, HALF), F32),
+        kernel,
+        in_specs=[vmem] * len(operands),
+        out_specs=[vmem] * len(shapes),
+        out_shape=[jax.ShapeDtypeStruct(shape, F32) for shape in shapes],
         compiler_params=pltpu.CompilerParams(vmem_limit_bytes=PART_LIMIT),
         cost_estimate=pl.CostEstimate(flops=500_000_000, bytes_accessed=3_000_000, transcendentals=0),
         name=name,
-    )(bound, edge, x, y, db, dc)
-
-
-def sum_kernel(kept_ref, got_ref, *outs):
-    for m in range(4):
-        outs[m][...] = kept_ref[m] + got_ref[m]
-
-
-def sum_pass(kept, got):
-    vmem = pl.BlockSpec(memory_space=pltpu.VMEM)
-    return pl.pallas_call(
-        sum_kernel,
-        in_specs=[vmem, vmem],
-        out_specs=[vmem] * 4,
-        out_shape=[jax.ShapeDtypeStruct((2, STATE, HALF), F32)] * 4,
-        compiler_params=pltpu.CompilerParams(vmem_limit_bytes=VMEM_LIMIT),
-        name="sum_cores",
-    )(kept, got)
+    )(*operands)
 
 
 PER5 = 4
@@ -561,23 +567,14 @@
     )(x, y, b, c, rows, lanes, bound, s, d)
 
 
-def merge_kernel(own_ref, near_ref, far_ref, side_ref, in_ref, out_ref):
+def merge_kernel(own_ref, late_ref, near_ref, far_ref, side_ref, in_ref, out_ref):
     group = lax.axis_index("head") // 4
     for t, ref in enumerate((in_ref, out_ref)):
-        ref[pl.ds(group, HALF, stride=2), :] = (own_ref[t] + near_ref[t]).T
+        own = own_ref[t] + near_ref[t]
+        if t == 0:
+            own = own + late_ref[...]
+        ref[pl.ds(group, HALF, stride=2), :] = own.T
         ref[pl.ds(1 - group, HALF, stride=2), :] = (far_ref[t] + side_ref[t]).T
-
-
-def merge(own, near, far, side):
-    spec = pl.BlockSpec(memory_space=pltpu.VMEM)
-    return pl.pallas_call(
-        merge_kernel,
-        in_specs=[spec] * 4,
-        out_specs=[spec] * 2,
-        out_shape=[jax.ShapeDtypeStruct((2 * HALF, STATE), F32)] * 2,
-        compiler_params=pltpu.CompilerParams(vmem_limit_bytes=VMEM_LIMIT),
-        name="merge",
-    )(own, near, far, side)
 
 
 def local(inputs, log_decay, in_proj, out_proj, upstream):
@@ -592,15 +589,29 @@
     got, dbp = lax.optimization_barrier((got, dbp))
     bound = lax.all_to_all(scan_blocks(got), "seq", 0, 0)
     db_send, db_keep, d = descend(x, y, c, rows, lanes, dbp)
-    sent = part_pass("projections_send", 1, bound, edge, x, y, db_send, dc_send)
-    other = lax.ppermute(sent, "head", [(i, i ^ 1) for i in range(8)])
-    kept = part_pass("projections_keep", 0, bound, edge, x, y, db_keep, dc_keep)
-    parts = sum_pass(kept, other)
+    bound, d = lax.optimization_barrier((bound, d))
+    pair = [(i, i ^ 1) for i in range(8)]
+    block = (STATE, HALF)
+    (sent_out,) = in_vmem("out_send", send_out_kernel, [(4, *block)], bound, edge, y, dc_send)
+    got_out = lax.ppermute(sent_out, "head", pair)
+    db_send, sent_out = lax.optimization_barrier((db_send, sent_out))
+    sent_in, sent_own = in_vmem(
+        "in_send", send_in_kernel, [(3, *block), block], bound, edge, x, db_send
+    )
+    got_in = lax.ppermute(sent_in, "head", pair)
+    late = lax.ppermute(sent_own, "head", pair)
+    dc_keep, sent_in = lax.optimization_barrier((dc_keep, sent_in))
+    (kept,) = in_vmem(
+        "keep", keep_kernel, [(4, 2, *block)], bound, edge, x, y, db_keep, dc_keep
+    )
+    parts = in_vmem("sum_cores", sum_kernel, [(2, *block)] * 4, kept, got_out, got_in)
     moved = [
         lax.ppermute(parts[m], "head", [(i, i ^ (2 * m)) for i in range(8)]) for m in (1, 2, 3)
     ]
     grad_x, grad_log = last_pass(x, y, b, c, rows, lanes, bound, s, d)
-    grad_in, grad_out = merge(parts[0], *moved)
+    grad_in, grad_out = in_vmem(
+        "merge", merge_kernel, [(2 * HALF, STATE)] * 2, parts[0], late, *moved
+    )
     return (
         jnp.transpose(grad_x.reshape(HEADS_HERE, WIDTH, TOK), (2, 0, 1)),
         jnp.transpose(grad_log),

time: 73.7 us -> 72.4 us (0.982)
  local copies, waits for them, and re-layouts: 1.5 us -> 0.06 us
    unnamed x26, local copies, waits for them, and re-layouts: 1.5 us -> 0.06 us
    ppermute x1 -> x3, waiting for transfers between devices: 1.52 us -> 0.62 us  [the longest x1 0.61 us: local(): got_in = lax.ppermute(sent_in, 'head', pair)]
    pallas_call x4 -> x5, Pallas kernels: 2.36 us -> 2.56 us  [in_vmem(): pl.pallas_call(kernel, in_specs=[vmem] * len(operands), out_specs=[vmem]...]
  transfers between devices with their start and end apart: 6 -> 8, of which waited for: 5 -> 5; matrix products, arithmetic and copies ran while one was open for 0% -> 0% of each run, Pallas kernels for 33% -> 34%
where the time goes in v3:
time: 72.4 us; the launch traced here: 72.1 us
  Pallas kernels  31.2 us (43%)
  starting transfers between devices  21.7 us (30%)
  waiting for transfers between devices  18.3 us (25%)
  between operations  0.82 us (1%)
    all_to_all x1, starting transfers between devices, local(): got = lax.all_to_all(message, 'seq', 0, 0)  11.4 us
    pallas_call x1, Pallas kernels, last_pass(): pl.pallas_call(last_kernel, grid=(CHUNKS // PER5,), in_specs=chunk_specs(...  8.26 us
    pallas_call x1, Pallas kernels, ascend(): pl.pallas_call(ascend_kernel, grid=(CHUNKS // PER2,), in_specs=chunk_spec...  8.21 us
    pallas_call x1, Pallas kernels, descend(): pl.pallas_call(descend_kernel, grid=(steps,), in_specs=specs[:2] + specs[...  6.69 us
    all_to_all x1, waiting for transfers between devices, local(): got = lax.all_to_all(message, 'seq', 0, 0)  6.67 us
    ppermute x3, waiting for transfers between devices, local(): lax.ppermute(parts[m], 'head', [(i, i ^ 2 * m) for i in range(8)])  5.98 us
    all_to_all x1, waiting for transfers between devices, local(): bound = lax.all_to_all(scan_blocks(got), 'seq', 0, 0)  5.01 us
    ppermute x3, starting transfers between devices, local(): lax.ppermute(parts[m], 'head', [(i, i ^ 2 * m) for i in range(8)])  4.79 us
  transfers between devices with their start and end apart: 8, of which 5 were waited for; matrix products, arithmetic and copies ran while one was open for 0% of the time, Pallas kernels for 34%

profile of v3, /device:TPU:32, one launch (start us, length us, event | category | flops | bytes accessed | tf_op | source)
XLA Modules:
  0.0 72.1 jit_solution(7380830363893028103)
XLA Ops:
  0.6 4.7 %own_states.1 = (f32[32,24,128]{2,1,0:T(8,128)}, f32[16,32,128]{2,1,0:T(8,128)}, f32[16,8,128]{2,1,0:T(8,128)}, f32[16,8,256]{2,1,0:T(8,128)}, bf16[2048,128]{1,0:T(8,128)(2,1)}, /*index=5*/bf16[2048,128]{1,0:T(8,128)(2,1)}) custom-call(bf16[256,2048]{1,0:T(8,128)(2,1)} %bitcast.21, bf16[256,2048]{1,0:T(8,128)(2,1)} %bitcast.15, bf16[4096,128]{1,0:T(8,128)(2,1)} %bitcast.27, ...), custom_call_target="tpu_custom_call" | custom-call | flops 800000000 | bytes 6000000 | tf_op jit(solution)/shard_map/own_states/pallas_call | solution.py:231
  5.4 11.4 %all-to-all-start = ((f32[32,24,128]{2,1,0:T(8,128)}), f32[32,24,128]{2,1,0:T(8,128)S(1)}, u32[]{:S(2)}, u32[]{:S(2)}) async-start(f32[32,24,128]{2,1,0:T(8,128)} %get-tuple-element.37), calls=%async_computation | async-start | bytes 786432 | tf_op jit(solution)/shard_map/all_to_all | solution.py:587
  16.7 8.2 %chunks_ascending.1 = (f32[128,2048]{1,0:T(8,128)}, f32[4,128,256]{2,1,0:T(8,128)}, f32[4,128,256]{2,1,0:T(8,128)}, f32[2048,256]{1,0:T(8,128)}) custom-call(bf16[256,2048]{1,0:T(8,128)(2,1)} %bitcast.22, bf16[256,2048]{1,0:T(8,128)(2,1)} %bitcast.16, bf16[2048,128]{1,0:T(8,128)(2,1)} %get-tuple-element.33.b_ref, bf16[2048,128]{1,0:T(8,128)(2,1)} %get-tuple-element.34.c_ref, ...), custom_call_target="tpu_custom_call" | custom-call | flops 3000000000 | bytes 8000000 | tf_op jit(solution)/shard_map/chunks_ascending/pallas_call | solution.py:380
  24.9 6.7 %all-to-all-done.got_ref = f32[32,24,128]{2,1,0:T(8,128)S(1)} async-done(((f32[32,24,128]{2,1,0:T(8,128)}), f32[32,24,128]{2,1,0:T(8,128)S(1)}, u32[]{:S(2)}, u32[]{:S(2)}) %all-to-all-start) | async-done | bytes 393248 | tf_op jit(solution)/shard_map/all_to_all | solution.py:587
  31.6 0.8 %scan_blocks.1 = f32[32,16,128]{2,1,0:T(8,128)} custom-call(f32[32,24,128]{2,1,0:T(8,128)S(1)} %all-to-all-done.got_ref), custom_call_target="tpu_custom_call" | custom-call | tf_op jit(solution)/shard_map/scan_blocks/pallas_call | solution.py:279
  32.4 4.8 %all-to-all-start.1 = ((f32[32,16,128]{2,1,0:T(8,128)}), f32[32,16,128]{2,1,0:T(8,128)S(1)}, u32[]{:S(2)}, u32[]{:S(2)}) async-start(f32[32,16,128]{2,1,0:T(8,128)} %scan_blocks.1), calls=%async_computation.1 | async-start | bytes 524288 | tf_op jit(solution)/shard_map/all_to_all | solution.py:590
  37.2 0.0 copy-start
  37.2 6.7 %chunks_descending.1 = (f32[4,128,256]{2,1,0:T(8,128)}, f32[4,128,256]{2,1,0:T(8,128)}, f32[2048,256]{1,0:T(8,128)}) custom-call(bf16[256,2048]{1,0:T(8,128)(2,1)} %bitcast.23, bf16[256,2048]{1,0:T(8,128)(2,1)} %bitcast.17, bf16[2048,128]{1,0:T(8,128)(2,1)} %get-tuple-element.34.c_ref, f32[16,32,128]{2,1,0:T(8,128)} %get-tuple-element.35.rows_ref, ...), custom_call_target="tpu_custom_call" | custom-call | flops 3000000000 | bytes 8000000 | tf_op jit(solution)/shard_map/chunks_descending/pallas_call | solution.py:426
  43.9 5.0 %all-to-all-done.1.bound_ref = f32[32,16,128]{2,1,0:T(8,128)S(1)} async-done(((f32[32,16,128]{2,1,0:T(8,128)}), f32[32,16,128]{2,1,0:T(8,128)S(1)}, u32[]{:S(2)}, u32[]{:S(2)}) %all-to-all-start.1) | async-done | bytes 262176 | tf_op jit(solution)/shard_map/all_to_all | solution.py:590
  48.9 0.0 copy-start.3
  49.0 0.0 copy-start.4
  49.0 0.4 out_send.1
  49.4 0.1 collective-permute-start
  49.5 0.4 in_send.1
  50.0 0.6 collective-permute-start.1
  50.5 0.1 collective-permute-start.2
  50.6 0.0 copy-done.4
  50.6 0.0 copy-start.9
  50.7 0.7 keep.1.kept_ref
  51.4 0.6 collective-permute-done.1.in_ref
  52.0 0.0 collective-permute-done.out_ref
  52.0 0.1 sum_cores.1
  52.1 1.6 %collective-permute-start.3 = (f32[2,128,256]{2,1,0:T(8,128)S(1)}, f32[2,128,256]{2,1,0:T(8,128)S(1)}, u32[]{:S(2)}, u32[]{:S(2)}) collective-permute-start(f32[2,128,256]{2,1,0:T(8,128)S(1)} %get-tuple-element.57), channel_id=1, source_target_pairs={{0,2},{1,3},{2,0},{3,1},{4,6},{5,7},{6,4},{7,5},{8,10},{9,11},{10,... | collective-permute-start | bytes 786440 | tf_op jit(solution)/shard_map/ppermute | solution.py:609
  53.7 2.7 %collective-permute-start.4 = (f32[2,128,256]{2,1,0:T(8,128)S(1)}, f32[2,128,256]{2,1,0:T(8,128)S(1)}, u32[]{:S(2)}, u32[]{:S(2)}) collective-permute-start(f32[2,128,256]{2,1,0:T(8,128)S(1)} %get-tuple-element.58), channel_id=1, source_target_pairs={{0,4},{1,5},{2,6},{3,7},{4,0},{5,1},{6,2},{7,3},{8,12},{9,13},{10,... | collective-permute-start | bytes 786440 | tf_op jit(solution)/shard_map/ppermute | solution.py:609
  56.4 0.5 collective-permute-start.5
  56.9 0.0 copy-done.10
  56.9 8.3 %inputs_and_decay.1 = (bf16[256,2048]{1,0:T(8,128)(2,1)}, f32[4,2048]{1,0:T(4,128)}) custom-call(bf16[256,2048]{1,0:T(8,128)(2,1)S(1)} %bitcast.26, bf16[256,2048]{1,0:T(8,128)(2,1)S(1)} %bitcast.20, bf16[2048,128]{1,0:T(8,128)(2,1)S(1)} %copy-done.7, bf16[2048,128]{1,0:T(8,128)(2,1)S(1)} %copy-done.8, f32[16,32,128]{2,1,0:T(8,128)S(1)} %copy-done.9, ...), custom_call_target="tpu_custom_call" | custom-call | flops 6000000000 | bytes 12000000 | tf_op jit(solution)/shard_map/inputs_and_decay/pallas_call | solution.py:547
  65.2 0.0 collective-permute-done.2.late_ref
  65.2 0.0 collective-permute-done.3.near_ref
  65.2 3.4 %collective-permute-done.4.far_ref = f32[2,128,256]{2,1,0:T(8,128)S(1)} collective-permute-done((f32[2,128,256]{2,1,0:T(8,128)S(1)}, f32[2,128,256]{2,1,0:T(8,128)S(1)}, u32[]{:S(2)}, u32[]{:S(2)}) %collective-permute-start.4) | collective-permute-done | bytes 262176 | tf_op jit(solution)/shard_map/ppermute | solution.py:609
  68.6 2.6 %collective-permute-done.5.side_ref = f32[2,128,256]{2,1,0:T(8,128)S(1)} collective-permute-done((f32[2,128,256]{2,1,0:T(8,128)S(1)}, f32[2,128,256]{2,1,0:T(8,128)S(1)}, u32[]{:S(2)}, u32[]{:S(2)}) %collective-permute-start.5) | collective-permute-done | bytes 262176 | tf_op jit(solution)/shard_map/ppermute | solution.py:609
  71.1 0.9 %merge.1 = (f32[512,128]{1,0:T(8,128)}, f32[512,128]{1,0:T(8,128)}) custom-call(f32[2,128,256]{2,1,0:T(8,128)S(1)} %get-tuple-element.55.own_ref, f32[128,256]{1,0:T(8,128)S(1)} %collective-permute-done.2.late_ref, f32[2,128,256]{2,1,0:T(8,128)S(1)} %collective-permute-done.3.near_ref, f32[2,128,256]{2,1,0:T(8,128)S(1)} %collective-permute-done.4.far_ref, ...), custom_call_target="tpu_custom_call" | custom-call | flops 500000000 | bytes 3000000 | tf_op jit(solution)/shard_map/merge/pallas_call | solution.py:488
  (20 shorter events, 0.0 us)
Async XLA Ops:
  5.4 26.3 %all-to-all-start = ((f32[32,24,128]{2,1,0:T(8,128)}), f32[32,24,128]{2,1,0:T(8,128)S(1)}, u32[]{:S(2)}, u32[]{:S(2)}) async-start(f32[32,24,128]{2,1,0:T(8,128)} %get-tuple-element.37), calls=%async_computation | async-start | bytes 786432 | tf_op jit(solution)/shard_map/all_to_all | solution.py:587
  32.4 16.5 %all-to-all-start.1 = ((f32[32,16,128]{2,1,0:T(8,128)}), f32[32,16,128]{2,1,0:T(8,128)S(1)}, u32[]{:S(2)}, u32[]{:S(2)}) async-start(f32[32,16,128]{2,1,0:T(8,128)} %scan_blocks.1), calls=%async_computation.1 | async-start | bytes 524288 | tf_op jit(solution)/shard_map/all_to_all | solution.py:590
  37.2 11.7 %copy-start = (bf16[2048,4,64]{0,2,1:T(8,128)(2,1)S(1)}, bf16[2048,4,64]{0,2,1:T(8,128)(2,1)}, u32[]{:S(2)}) copy-start(bf16[2048,4,64]{0,2,1:T(8,128)(2,1)} %param.9) | copy-start | bytes 3145732
  37.2 11.7 %copy-start.2 = (f32[16,8,128]{2,1,0:T(8,128)S(1)}, f32[16,8,128]{2,1,0:T(8,128)}, u32[]{:S(2)}) copy-start(f32[16,8,128]{2,1,0:T(8,128)} %get-tuple-element.47.edge_ref) | copy-start | bytes 196612
  37.2 11.7 %copy-start.5 = (f32[4,128,256]{2,1,0:T(8,128)S(1)}, f32[4,128,256]{2,1,0:T(8,128)}, u32[]{:S(2)}) copy-start(f32[4,128,256]{2,1,0:T(8,128)} %get-tuple-element.51.held_ref) | copy-start | bytes 1572868
  43.9 5.6 %copy-start.1 = (bf16[2048,4,64]{0,2,1:T(8,128)(2,1)S(1)}, bf16[2048,4,64]{0,2,1:T(8,128)(2,1)}, u32[]{:S(2)}) copy-start(bf16[2048,4,64]{0,2,1:T(8,128)(2,1)} %param.5) | copy-start | bytes 3145732
  43.9 5.6 %copy-start.6 = (f32[4,128,256]{2,1,0:T(8,128)S(1)}, f32[4,128,256]{2,1,0:T(8,128)}, u32[]{:S(2)}) copy-start(f32[4,128,256]{2,1,0:T(8,128)} %get-tuple-element.52.held_ref) | copy-start | bytes 1572868
  48.9 1.7 %copy-start.3 = (f32[4,128,256]{2,1,0:T(8,128)S(1)}, f32[4,128,256]{2,1,0:T(8,128)}, u32[]{:S(2)}) copy-start(f32[4,128,256]{2,1,0:T(8,128)} %get-tuple-element.54.out_ref) | copy-start | bytes 1572868
  49.0 1.7 %copy-start.4 = (f32[4,128,256]{2,1,0:T(8,128)S(1)}, f32[4,128,256]{2,1,0:T(8,128)}, u32[]{:S(2)}) copy-start(f32[4,128,256]{2,1,0:T(8,128)} %get-tuple-element.48.in_ref) | copy-start | bytes 1572868
  49.4 2.6 %collective-permute-start = (f32[4,128,256]{2,1,0:T(8,128)S(1)}, f32[4,128,256]{2,1,0:T(8,128)S(1)}, u32[]{:S(2)}, u32[]{:S(2)}) collective-permute-start(f32[4,128,256]{2,1,0:T(8,128)S(1)} %out_send.1), channel_id=1, source_target_pairs={{0,1},{1,0},{2,3},{3,2},{4,5},{5,4},{6,7},{7,6},{8,9},{9,8},{10,11... | collective-permute-start | bytes 1572872 | tf_op jit(solution)/shard_map/ppermute | solution.py:596
  50.0 2.0 %collective-permute-start.1 = (f32[3,128,256]{2,1,0:T(8,128)S(1)}, f32[3,128,256]{2,1,0:T(8,128)S(1)}, u32[]{:S(2)}, u32[]{:S(2)}) collective-permute-start(f32[3,128,256]{2,1,0:T(8,128)S(1)} %get-tuple-element.53), channel_id=1, source_target_pairs={{0,1},{1,0},{2,3},{3,2},{4,5},{5,4},{6,7},{7,6},{8,9},{9,8},{10,11... | collective-permute-start | bytes 1179656 | tf_op jit(solution)/shard_map/ppermute | solution.py:601
  50.5 14.6 %collective-permute-start.2 = (f32[128,256]{1,0:T(8,128)S(1)}, f32[128,256]{1,0:T(8,128)S(1)}, u32[]{:S(2)}, u32[]{:S(2)}) collective-permute-start(f32[128,256]{1,0:T(8,128)S(1)} %get-tuple-element.56), channel_id=1, source_target_pairs={{0,1},{1,0},{2,3},{3,2},{4,5},{5,4},{6,7},{7,6},{8,9},{9,8},{10,11... | collective-permute-start | bytes 393224 | tf_op jit(solution)/shard_map/ppermute | solution.py:602
  50.6 6.2 %copy-start.7 = (bf16[2048,128]{1,0:T(8,128)(2,1)S(1)}, bf16[2048,128]{1,0:T(8,128)(2,1)}, u32[]{:S(2)}) copy-start(bf16[2048,128]{1,0:T(8,128)(2,1)} %get-tuple-element.33.b_ref) | copy-start | bytes 1572868
  50.6 6.2 %copy-start.8 = (bf16[2048,128]{1,0:T(8,128)(2,1)S(1)}, bf16[2048,128]{1,0:T(8,128)(2,1)}, u32[]{:S(2)}) copy-start(bf16[2048,128]{1,0:T(8,128)(2,1)} %get-tuple-element.34.c_ref) | copy-start | bytes 1572868
  50.6 6.2 %copy-start.9 = (f32[16,32,128]{2,1,0:T(8,128)S(1)}, f32[16,32,128]{2,1,0:T(8,128)}, u32[]{:S(2)}) copy-start(f32[16,32,128]{2,1,0:T(8,128)} %get-tuple-element.35.rows_ref) | copy-start | bytes 786436
  50.6 6.2 %copy-start.10 = (f32[16,8,256]{2,1,0:T(8,128)S(1)}, f32[16,8,256]{2,1,0:T(8,128)}, u32[]{:S(2)}) copy-start(f32[16,8,256]{2,1,0:T(8,128)} %get-tuple-element.36.lanes_ref) | copy-start | bytes 393220
  50.7 6.2 %copy-start.11 = (f32[2048,256]{1,0:T(8,128)S(1)}, f32[2048,256]{1,0:T(8,128)}, u32[]{:S(2)}) copy-start(f32[2048,256]{1,0:T(8,128)} %get-tuple-element.44.d_ref) | copy-start | bytes 6291460
  50.7 6.2 %copy-start.12 = (f32[2048,256]{1,0:T(8,128)S(1)}, f32[2048,256]{1,0:T(8,128)}, u32[]{:S(2)}) copy-start(f32[2048,256]{1,0:T(8,128)} %get-tuple-element.43.s_ref) | copy-start | bytes 6291460
  52.1 13.1 %collective-permute-start.3 = (f32[2,128,256]{2,1,0:T(8,128)S(1)}, f32[2,128,256]{2,1,0:T(8,128)S(1)}, u32[]{:S(2)}, u32[]{:S(2)}) collective-permute-start(f32[2,128,256]{2,1,0:T(8,128)S(1)} %get-tuple-element.57), channel_id=1, source_target_pairs={{0,2},{1,3},{2,0},{3,1},{4,6},{5,7},{6,4},{7,5},{8,10},{9,11},{10,... | collective-permute-start | bytes 786440 | tf_op jit(solution)/shard_map/ppermute | solution.py:609
  53.7 14.9 %collective-permute-start.4 = (f32[2,128,256]{2,1,0:T(8,128)S(1)}, f32[2,128,256]{2,1,0:T(8,128)S(1)}, u32[]{:S(2)}, u32[]{:S(2)}) collective-permute-start(f32[2,128,256]{2,1,0:T(8,128)S(1)} %get-tuple-element.58), channel_id=1, source_target_pairs={{0,4},{1,5},{2,6},{3,7},{4,0},{5,1},{6,2},{7,3},{8,12},{9,13},{10,... | collective-permute-start | bytes 786440 | tf_op jit(solution)/shard_map/ppermute | solution.py:609
  56.4 14.8 %collective-permute-start.5 = (f32[2,128,256]{2,1,0:T(8,128)S(1)}, f32[2,128,256]{2,1,0:T(8,128)S(1)}, u32[]{:S(2)}, u32[]{:S(2)}) collective-permute-start(f32[2,128,256]{2,1,0:T(8,128)S(1)} %get-tuple-element.59), channel_id=1, source_target_pairs={{0,6},{1,7},{2,4},{3,5},{4,2},{5,3},{6,0},{7,1},{8,14},{9,15},{10,... | collective-permute-start | bytes 786440 | tf_op jit(solution)/shard_map/ppermute | solution.py:609

commit v4 on v3

--- a/solution.py
+++ b/solution.py
@@ -478,9 +478,13 @@
 
 
 def sum_kernel(kept_ref, out_ref, in_ref, *outs):
-    for m in range(4):
-        outs[m][0] = kept_ref[m, 0] + in_ref[m - 1] if m else kept_ref[m, 0]
-        outs[m][1] = kept_ref[m, 1] + out_ref[m]
+    second = lax.axis_index("head") % 2
+    own_ref, rest = outs[0], outs[1:]
+    own_ref[0] = kept_ref[0, 0]
+    own_ref[1] = kept_ref[0, 1] + out_ref[0]
+    for ref, m in zip(rest, (1 + 2 * second, 3 - 2 * second, 2)):
+        ref[0] = kept_ref[m, 0] + in_ref[m - 1]
+        ref[1] = kept_ref[m, 1] + out_ref[m]
 
 
 def in_vmem(name, kernel, shapes, *operands):
@@ -567,14 +571,16 @@
     )(x, y, b, c, rows, lanes, bound, s, d)
 
 
-def merge_kernel(own_ref, late_ref, near_ref, far_ref, side_ref, in_ref, out_ref):
-    group = lax.axis_index("head") // 4
+def merge_kernel(own_ref, late_ref, one_ref, two_ref, far_ref, in_ref, out_ref):
+    index = lax.axis_index("head")
+    group, second = index // 4, index % 2 == 1
     for t, ref in enumerate((in_ref, out_ref)):
-        own = own_ref[t] + near_ref[t]
+        one, two = one_ref[t], two_ref[t]
+        own = own_ref[t] + jnp.where(second, two, one)
         if t == 0:
             own = own + late_ref[...]
         ref[pl.ds(group, HALF, stride=2), :] = own.T
-        ref[pl.ds(1 - group, HALF, stride=2), :] = (far_ref[t] + side_ref[t]).T
+        ref[pl.ds(1 - group, HALF, stride=2), :] = (far_ref[t] + jnp.where(second, one, two)).T
 
 
 def local(inputs, log_decay, in_proj, out_proj, upstream):
@@ -605,8 +611,10 @@
         "keep", keep_kernel, [(4, 2, *block)], bound, edge, x, y, db_keep, dc_keep
     )
     parts = in_vmem("sum_cores", sum_kernel, [(2, *block)] * 4, kept, got_out, got_in)
+    hops = [(2, 6), (6, 2), (4, 4)]
     moved = [
-        lax.ppermute(parts[m], "head", [(i, i ^ (2 * m)) for i in range(8)]) for m in (1, 2, 3)
+        lax.ppermute(part, "head", [(i, i ^ hop[i % 2]) for i in range(8)])
+        for part, hop in zip(parts[1:], hops)
     ]
     grad_x, grad_log = last_pass(x, y, b, c, rows, lanes, bound, s, d)
     grad_in, grad_out = in_vmem(

time: 72.4 us -> 70.7 us (0.977); the launches traced: 72.1 us -> 69.6 us
  waiting for transfers between devices: 18.3 us -> 16.3 us
    ppermute x3, waiting for transfers between devices: 5.98 us -> 3.98 us  [local(): lax.ppermute(part, 'head', [(i, i ^ hop[i % 2]) for i in range(8)])]
  transfers between devices with their start and end apart: 8 -> 8, of which waited for: 5 -> 5; matrix products, arithmetic and copies ran while one was open for 0% -> 0% of each run, Pallas kernels for 34% -> 35%
where the time goes in v4:
time: 70.7 us; the launch traced here: 69.6 us
  Pallas kernels  31.2 us (44%)
  starting transfers between devices  21.2 us (30%)
  waiting for transfers between devices  16.3 us (23%)
  between operations  0.82 us (1%)
    all_to_all x1, starting transfers between devices, local(): got = lax.all_to_all(message, 'seq', 0, 0)  11.4 us
    pallas_call x1, Pallas kernels, last_pass(): pl.pallas_call(last_kernel, grid=(CHUNKS // PER5,), in_specs=chunk_specs(...  8.26 us
    pallas_call x1, Pallas kernels, ascend(): pl.pallas_call(ascend_kernel, grid=(CHUNKS // PER2,), in_specs=chunk_spec...  8.21 us
    pallas_call x1, Pallas kernels, descend(): pl.pallas_call(descend_kernel, grid=(steps,), in_specs=specs[:2] + specs[...  6.69 us
    all_to_all x1, waiting for transfers between devices, local(): got = lax.all_to_all(message, 'seq', 0, 0)  6.67 us
    all_to_all x1, waiting for transfers between devices, local(): bound = lax.all_to_all(scan_blocks(got), 'seq', 0, 0)  5.01 us
    all_to_all x1, starting transfers between devices, local(): bound = lax.all_to_all(scan_blocks(got), 'seq', 0, 0)  4.78 us
    pallas_call x1, Pallas kernels, first_pass(): pl.pallas_call(first_kernel, in_specs=[hbm] * 5, out_specs=[hbm] * 6, out...  4.72 us
  transfers between devices with their start and end apart: 8, of which 5 were waited for; matrix products, arithmetic and copies ran while one was open for 0% of the time, Pallas kernels for 35%

profile of v4, /device:TPU:32, one launch (start us, length us, event | category | flops | bytes accessed | tf_op | source)
XLA Modules:
  0.0 69.6 jit_solution(14975930582326999905)
XLA Ops:
  0.6 4.7 %own_states.1 = (f32[32,24,128]{2,1,0:T(8,128)}, f32[16,32,128]{2,1,0:T(8,128)}, f32[16,8,128]{2,1,0:T(8,128)}, f32[16,8,256]{2,1,0:T(8,128)}, bf16[2048,128]{1,0:T(8,128)(2,1)}, /*index=5*/bf16[2048,128]{1,0:T(8,128)(2,1)}) custom-call(bf16[256,2048]{1,0:T(8,128)(2,1)} %bitcast.21, bf16[256,2048]{1,0:T(8,128)(2,1)} %bitcast.15, bf16[4096,128]{1,0:T(8,128)(2,1)} %bitcast.27, ...), custom_call_target="tpu_custom_call" | custom-call | flops 800000000 | bytes 6000000 | tf_op jit(solution)/shard_map/own_states/pallas_call | solution.py:231
  5.4 11.4 %all-to-all-start = ((f32[32,24,128]{2,1,0:T(8,128)}), f32[32,24,128]{2,1,0:T(8,128)S(1)}, u32[]{:S(2)}, u32[]{:S(2)}) async-start(f32[32,24,128]{2,1,0:T(8,128)} %get-tuple-element.37), calls=%async_computation | async-start | bytes 786432 | tf_op jit(solution)/shard_map/all_to_all | solution.py:593
  16.7 8.2 %chunks_ascending.1 = (f32[128,2048]{1,0:T(8,128)}, f32[4,128,256]{2,1,0:T(8,128)}, f32[4,128,256]{2,1,0:T(8,128)}, f32[2048,256]{1,0:T(8,128)}) custom-call(bf16[256,2048]{1,0:T(8,128)(2,1)} %bitcast.22, bf16[256,2048]{1,0:T(8,128)(2,1)} %bitcast.16, bf16[2048,128]{1,0:T(8,128)(2,1)} %get-tuple-element.33.b_ref, bf16[2048,128]{1,0:T(8,128)(2,1)} %get-tuple-element.34.c_ref, ...), custom_call_target="tpu_custom_call" | custom-call | flops 3000000000 | bytes 8000000 | tf_op jit(solution)/shard_map/chunks_ascending/pallas_call | solution.py:380
  24.9 6.7 %all-to-all-done.got_ref = f32[32,24,128]{2,1,0:T(8,128)S(1)} async-done(((f32[32,24,128]{2,1,0:T(8,128)}), f32[32,24,128]{2,1,0:T(8,128)S(1)}, u32[]{:S(2)}, u32[]{:S(2)}) %all-to-all-start) | async-done | bytes 393248 | tf_op jit(solution)/shard_map/all_to_all | solution.py:593
  31.6 0.8 %scan_blocks.1 = f32[32,16,128]{2,1,0:T(8,128)} custom-call(f32[32,24,128]{2,1,0:T(8,128)S(1)} %all-to-all-done.got_ref), custom_call_target="tpu_custom_call" | custom-call | tf_op jit(solution)/shard_map/scan_blocks/pallas_call | solution.py:279
  32.4 4.8 %all-to-all-start.1 = ((f32[32,16,128]{2,1,0:T(8,128)}), f32[32,16,128]{2,1,0:T(8,128)S(1)}, u32[]{:S(2)}, u32[]{:S(2)}) async-start(f32[32,16,128]{2,1,0:T(8,128)} %scan_blocks.1), calls=%async_computation.1 | async-start | bytes 524288 | tf_op jit(solution)/shard_map/all_to_all | solution.py:596
  37.2 0.0 copy-start
  37.2 6.7 %chunks_descending.1 = (f32[4,128,256]{2,1,0:T(8,128)}, f32[4,128,256]{2,1,0:T(8,128)}, f32[2048,256]{1,0:T(8,128)}) custom-call(bf16[256,2048]{1,0:T(8,128)(2,1)} %bitcast.23, bf16[256,2048]{1,0:T(8,128)(2,1)} %bitcast.17, bf16[2048,128]{1,0:T(8,128)(2,1)} %get-tuple-element.34.c_ref, f32[16,32,128]{2,1,0:T(8,128)} %get-tuple-element.35.rows_ref, ...), custom_call_target="tpu_custom_call" | custom-call | flops 3000000000 | bytes 8000000 | tf_op jit(solution)/shard_map/chunks_descending/pallas_call | solution.py:426
  43.9 5.0 %all-to-all-done.1.bound_ref = f32[32,16,128]{2,1,0:T(8,128)S(1)} async-done(((f32[32,16,128]{2,1,0:T(8,128)}), f32[32,16,128]{2,1,0:T(8,128)S(1)}, u32[]{:S(2)}, u32[]{:S(2)}) %all-to-all-start.1) | async-done | bytes 262176 | tf_op jit(solution)/shard_map/all_to_all | solution.py:596
  48.9 0.0 copy-start.3
  49.0 0.0 copy-start.4
  49.0 0.4 out_send.1
  49.4 0.1 collective-permute-start
  49.5 0.4 in_send.1
  50.0 0.6 collective-permute-start.1
  50.5 0.1 collective-permute-start.2
  50.6 0.0 copy-done.4
  50.6 0.0 copy-start.9
  50.7 0.7 keep.1.kept_ref
  51.4 0.6 collective-permute-done.1.in_ref
  52.0 0.0 collective-permute-done.out_ref
  52.0 0.1 sum_cores.1
  52.1 1.6 %collective-permute-start.3 = (f32[2,128,256]{2,1,0:T(8,128)S(1)}, f32[2,128,256]{2,1,0:T(8,128)S(1)}, u32[]{:S(2)}, u32[]{:S(2)}) collective-permute-start(f32[2,128,256]{2,1,0:T(8,128)S(1)} %get-tuple-element.57), channel_id=1, source_target_pairs={{0,2},{1,7},{2,0},{3,5},{4,6},{5,3},{6,4},{7,1},{8,10},{9,15},{10,... | collective-permute-start | bytes 786440 | tf_op jit(solution)/shard_map/ppermute | solution.py:616
  53.7 2.1 %collective-permute-start.4 = (f32[2,128,256]{2,1,0:T(8,128)S(1)}, f32[2,128,256]{2,1,0:T(8,128)S(1)}, u32[]{:S(2)}, u32[]{:S(2)}) collective-permute-start(f32[2,128,256]{2,1,0:T(8,128)S(1)} %get-tuple-element.58), channel_id=1, source_target_pairs={{0,6},{1,3},{2,4},{3,1},{4,2},{5,7},{6,0},{7,5},{8,14},{9,11},{10,... | collective-permute-start | bytes 786440 | tf_op jit(solution)/shard_map/ppermute | solution.py:616
  55.7 0.6 collective-permute-start.5
  56.4 0.0 copy-done.7
  56.4 8.3 %inputs_and_decay.1 = (bf16[256,2048]{1,0:T(8,128)(2,1)}, f32[4,2048]{1,0:T(4,128)}) custom-call(bf16[256,2048]{1,0:T(8,128)(2,1)S(1)} %bitcast.26, bf16[256,2048]{1,0:T(8,128)(2,1)S(1)} %bitcast.20, bf16[2048,128]{1,0:T(8,128)(2,1)S(1)} %copy-done.7, bf16[2048,128]{1,0:T(8,128)(2,1)S(1)} %copy-done.8, f32[16,32,128]{2,1,0:T(8,128)S(1)} %copy-done.9, ...), custom_call_target="tpu_custom_call" | custom-call | flops 6000000000 | bytes 12000000 | tf_op jit(solution)/shard_map/inputs_and_decay/pallas_call | solution.py:551
  64.7 0.0 collective-permute-done.2.late_ref
  64.7 0.0 collective-permute-done.3.one_ref
  64.7 1.9 %collective-permute-done.4.two_ref = f32[2,128,256]{2,1,0:T(8,128)S(1)} collective-permute-done((f32[2,128,256]{2,1,0:T(8,128)S(1)}, f32[2,128,256]{2,1,0:T(8,128)S(1)}, u32[]{:S(2)}, u32[]{:S(2)}) %collective-permute-start.4) | collective-permute-done | bytes 262176 | tf_op jit(solution)/shard_map/ppermute | solution.py:616
  66.6 2.1 %collective-permute-done.5.far_ref = f32[2,128,256]{2,1,0:T(8,128)S(1)} collective-permute-done((f32[2,128,256]{2,1,0:T(8,128)S(1)}, f32[2,128,256]{2,1,0:T(8,128)S(1)}, u32[]{:S(2)}, u32[]{:S(2)}) %collective-permute-start.5) | collective-permute-done | bytes 262176 | tf_op jit(solution)/shard_map/ppermute | solution.py:616
  68.7 0.9 %merge.1 = (f32[512,128]{1,0:T(8,128)}, f32[512,128]{1,0:T(8,128)}) custom-call(f32[2,128,256]{2,1,0:T(8,128)S(1)} %get-tuple-element.55.own_ref, f32[128,256]{1,0:T(8,128)S(1)} %collective-permute-done.2.late_ref, f32[2,128,256]{2,1,0:T(8,128)S(1)} %collective-permute-done.3.one_ref, f32[2,128,256]{2,1,0:T(8,128)S(1)} %collective-permute-done.4.two_ref, ...), custom_call_target="tpu_custom_call" | custom-call | flops 500000000 | bytes 3000000 | tf_op jit(solution)/shard_map/merge/pallas_call | solution.py:492
  (20 shorter events, 0.0 us)
Async XLA Ops:
  5.4 26.3 %all-to-all-start = ((f32[32,24,128]{2,1,0:T(8,128)}), f32[32,24,128]{2,1,0:T(8,128)S(1)}, u32[]{:S(2)}, u32[]{:S(2)}) async-start(f32[32,24,128]{2,1,0:T(8,128)} %get-tuple-element.37), calls=%async_computation | async-start | bytes 786432 | tf_op jit(solution)/shard_map/all_to_all | solution.py:593
  32.4 16.5 %all-to-all-start.1 = ((f32[32,16,128]{2,1,0:T(8,128)}), f32[32,16,128]{2,1,0:T(8,128)S(1)}, u32[]{:S(2)}, u32[]{:S(2)}) async-start(f32[32,16,128]{2,1,0:T(8,128)} %scan_blocks.1), calls=%async_computation.1 | async-start | bytes 524288 | tf_op jit(solution)/shard_map/all_to_all | solution.py:596
  37.2 11.7 %copy-start = (bf16[2048,4,64]{0,2,1:T(8,128)(2,1)S(1)}, bf16[2048,4,64]{0,2,1:T(8,128)(2,1)}, u32[]{:S(2)}) copy-start(bf16[2048,4,64]{0,2,1:T(8,128)(2,1)} %param.9) | copy-start | bytes 3145732
  37.2 11.7 %copy-start.2 = (f32[16,8,128]{2,1,0:T(8,128)S(1)}, f32[16,8,128]{2,1,0:T(8,128)}, u32[]{:S(2)}) copy-start(f32[16,8,128]{2,1,0:T(8,128)} %get-tuple-element.47.edge_ref) | copy-start | bytes 196612
  37.2 11.7 %copy-start.5 = (f32[4,128,256]{2,1,0:T(8,128)S(1)}, f32[4,128,256]{2,1,0:T(8,128)}, u32[]{:S(2)}) copy-start(f32[4,128,256]{2,1,0:T(8,128)} %get-tuple-element.51.held_ref) | copy-start | bytes 1572868
  43.9 5.6 %copy-start.1 = (bf16[2048,4,64]{0,2,1:T(8,128)(2,1)S(1)}, bf16[2048,4,64]{0,2,1:T(8,128)(2,1)}, u32[]{:S(2)}) copy-start(bf16[2048,4,64]{0,2,1:T(8,128)(2,1)} %param.5) | copy-start | bytes 3145732
  43.9 5.6 %copy-start.6 = (f32[4,128,256]{2,1,0:T(8,128)S(1)}, f32[4,128,256]{2,1,0:T(8,128)}, u32[]{:S(2)}) copy-start(f32[4,128,256]{2,1,0:T(8,128)} %get-tuple-element.52.held_ref) | copy-start | bytes 1572868
  48.9 1.7 %copy-start.3 = (f32[4,128,256]{2,1,0:T(8,128)S(1)}, f32[4,128,256]{2,1,0:T(8,128)}, u32[]{:S(2)}) copy-start(f32[4,128,256]{2,1,0:T(8,128)} %get-tuple-element.54.out_ref) | copy-start | bytes 1572868
  49.0 1.7 %copy-start.4 = (f32[4,128,256]{2,1,0:T(8,128)S(1)}, f32[4,128,256]{2,1,0:T(8,128)}, u32[]{:S(2)}) copy-start(f32[4,128,256]{2,1,0:T(8,128)} %get-tuple-element.48.in_ref) | copy-start | bytes 1572868
  49.4 2.6 %collective-permute-start = (f32[4,128,256]{2,1,0:T(8,128)S(1)}, f32[4,128,256]{2,1,0:T(8,128)S(1)}, u32[]{:S(2)}, u32[]{:S(2)}) collective-permute-start(f32[4,128,256]{2,1,0:T(8,128)S(1)} %out_send.1), channel_id=1, source_target_pairs={{0,1},{1,0},{2,3},{3,2},{4,5},{5,4},{6,7},{7,6},{8,9},{9,8},{10,11... | collective-permute-start | bytes 1572872 | tf_op jit(solution)/shard_map/ppermute | solution.py:602
  50.0 2.0 %collective-permute-start.1 = (f32[3,128,256]{2,1,0:T(8,128)S(1)}, f32[3,128,256]{2,1,0:T(8,128)S(1)}, u32[]{:S(2)}, u32[]{:S(2)}) collective-permute-start(f32[3,128,256]{2,1,0:T(8,128)S(1)} %get-tuple-element.53), channel_id=1, source_target_pairs={{0,1},{1,0},{2,3},{3,2},{4,5},{5,4},{6,7},{7,6},{8,9},{9,8},{10,11... | collective-permute-start | bytes 1179656 | tf_op jit(solution)/shard_map/ppermute | solution.py:607
  50.5 14.2 %collective-permute-start.2 = (f32[128,256]{1,0:T(8,128)S(1)}, f32[128,256]{1,0:T(8,128)S(1)}, u32[]{:S(2)}, u32[]{:S(2)}) collective-permute-start(f32[128,256]{1,0:T(8,128)S(1)} %get-tuple-element.56), channel_id=1, source_target_pairs={{0,1},{1,0},{2,3},{3,2},{4,5},{5,4},{6,7},{7,6},{8,9},{9,8},{10,11... | collective-permute-start | bytes 393224 | tf_op jit(solution)/shard_map/ppermute | solution.py:608
  50.6 5.8 %copy-start.7 = (bf16[2048,128]{1,0:T(8,128)(2,1)S(1)}, bf16[2048,128]{1,0:T(8,128)(2,1)}, u32[]{:S(2)}) copy-start(bf16[2048,128]{1,0:T(8,128)(2,1)} %get-tuple-element.33.b_ref) | copy-start | bytes 1572868
  50.6 5.8 %copy-start.8 = (bf16[2048,128]{1,0:T(8,128)(2,1)S(1)}, bf16[2048,128]{1,0:T(8,128)(2,1)}, u32[]{:S(2)}) copy-start(bf16[2048,128]{1,0:T(8,128)(2,1)} %get-tuple-element.34.c_ref) | copy-start | bytes 1572868
  50.6 5.8 %copy-start.9 = (f32[16,32,128]{2,1,0:T(8,128)S(1)}, f32[16,32,128]{2,1,0:T(8,128)}, u32[]{:S(2)}) copy-start(f32[16,32,128]{2,1,0:T(8,128)} %get-tuple-element.35.rows_ref) | copy-start | bytes 786436
  50.6 5.7 %copy-start.10 = (f32[16,8,256]{2,1,0:T(8,128)S(1)}, f32[16,8,256]{2,1,0:T(8,128)}, u32[]{:S(2)}) copy-start(f32[16,8,256]{2,1,0:T(8,128)} %get-tuple-element.36.lanes_ref) | copy-start | bytes 393220
  50.7 5.7 %copy-start.11 = (f32[2048,256]{1,0:T(8,128)S(1)}, f32[2048,256]{1,0:T(8,128)}, u32[]{:S(2)}) copy-start(f32[2048,256]{1,0:T(8,128)} %get-tuple-element.44.d_ref) | copy-start | bytes 6291460
  50.7 5.7 %copy-start.12 = (f32[2048,256]{1,0:T(8,128)S(1)}, f32[2048,256]{1,0:T(8,128)}, u32[]{:S(2)}) copy-start(f32[2048,256]{1,0:T(8,128)} %get-tuple-element.43.s_ref) | copy-start | bytes 6291460
  52.1 12.6 %collective-permute-start.3 = (f32[2,128,256]{2,1,0:T(8,128)S(1)}, f32[2,128,256]{2,1,0:T(8,128)S(1)}, u32[]{:S(2)}, u32[]{:S(2)}) collective-permute-start(f32[2,128,256]{2,1,0:T(8,128)S(1)} %get-tuple-element.57), channel_id=1, source_target_pairs={{0,2},{1,7},{2,0},{3,5},{4,6},{5,3},{6,4},{7,1},{8,10},{9,15},{10,... | collective-permute-start | bytes 786440 | tf_op jit(solution)/shard_map/ppermute | solution.py:616
  53.7 12.9 %collective-permute-start.4 = (f32[2,128,256]{2,1,0:T(8,128)S(1)}, f32[2,128,256]{2,1,0:T(8,128)S(1)}, u32[]{:S(2)}, u32[]{:S(2)}) collective-permute-start(f32[2,128,256]{2,1,0:T(8,128)S(1)} %get-tuple-element.58), channel_id=1, source_target_pairs={{0,6},{1,3},{2,4},{3,1},{4,2},{5,7},{6,0},{7,5},{8,14},{9,11},{10,... | collective-permute-start | bytes 786440 | tf_op jit(solution)/shard_map/ppermute | solution.py:616
  55.7 12.9 %collective-permute-start.5 = (f32[2,128,256]{2,1,0:T(8,128)S(1)}, f32[2,128,256]{2,1,0:T(8,128)S(1)}, u32[]{:S(2)}, u32[]{:S(2)}) collective-permute-start(f32[2,128,256]{2,1,0:T(8,128)S(1)} %get-tuple-element.59), channel_id=1, source_target_pairs={{0,4},{1,5},{2,6},{3,7},{4,0},{5,1},{6,2},{7,3},{8,12},{9,13},{10,... | collective-permute-start | bytes 786440 | tf_op jit(solution)/shard_map/ppermute | solution.py:616

commit v5 on v4

--- a/solution.py
+++ b/solution.py
@@ -605,7 +605,6 @@
         "in_send", send_in_kernel, [(3, *block), block], bound, edge, x, db_send
     )
     got_in = lax.ppermute(sent_in, "head", pair)
-    late = lax.ppermute(sent_own, "head", pair)
     dc_keep, sent_in = lax.optimization_barrier((dc_keep, sent_in))
     (kept,) = in_vmem(
         "keep", keep_kernel, [(4, 2, *block)], bound, edge, x, y, db_keep, dc_keep
@@ -617,6 +616,8 @@
         for part, hop in zip(parts[1:], hops)
     ]
     grad_x, grad_log = last_pass(x, y, b, c, rows, lanes, bound, s, d)
+    sent_own, grad_log = lax.optimization_barrier((sent_own, grad_log))
+    late = lax.ppermute(sent_own, "head", pair)
     grad_in, grad_out = in_vmem(
         "merge", merge_kernel, [(2 * HALF, STATE)] * 2, parts[0], late, *moved
     )

time: 70.7 us -> 70.7 us (level)
    ppermute x3, waiting for transfers between devices: 3.98 us -> 2.63 us  [local(): lax.ppermute(part, 'head', [(i, i ^ hop[i % 2]) for i in range(8)])]
    ppermute x1, waiting for transfers between devices: 0.01 us -> 1.35 us  [local(): late = lax.ppermute(sent_own, 'head', pair)]
  transfers between devices with their start and end apart: 8 -> 8, of which waited for: 5 -> 6; matrix products, arithmetic and copies ran while one was open for 0% -> 0% of each run, Pallas kernels for 35% -> 35%
where the time goes in v5:
time: 70.7 us; the launch traced here: 69.6 us
  Pallas kernels  31.2 us (44%)
  starting transfers between devices  21.1 us (30%)
  waiting for transfers between devices  16.4 us (23%)
  between operations  0.82 us (1%)
    all_to_all x1, starting transfers between devices, local(): got = lax.all_to_all(message, 'seq', 0, 0)  11.4 us
    pallas_call x1, Pallas kernels, last_pass(): pl.pallas_call(last_kernel, grid=(CHUNKS // PER5,), in_specs=chunk_specs(...  8.26 us
    pallas_call x1, Pallas kernels, ascend(): pl.pallas_call(ascend_kernel, grid=(CHUNKS // PER2,), in_specs=chunk_spec...  8.21 us
    pallas_call x1, Pallas kernels, descend(): pl.pallas_call(descend_kernel, grid=(steps,), in_specs=specs[:2] + specs[...  6.69 us
    all_to_all x1, waiting for transfers between devices, local(): got = lax.all_to_all(message, 'seq', 0, 0)  6.67 us
    all_to_all x1, waiting for transfers between devices, local(): bound = lax.all_to_all(scan_blocks(got), 'seq', 0, 0)  5.01 us
    all_to_all x1, starting transfers between devices, local(): bound = lax.all_to_all(scan_blocks(got), 'seq', 0, 0)  4.78 us
    pallas_call x1, Pallas kernels, first_pass(): pl.pallas_call(first_kernel, in_specs=[hbm] * 5, out_specs=[hbm] * 6, out...  4.72 us
  transfers between devices with their start and end apart: 8, of which 6 were waited for; matrix products, arithmetic and copies ran while one was open for 0% of the time, Pallas kernels for 35%

profile of v5, /device:TPU:32, one launch (start us, length us, event | category | flops | bytes accessed | tf_op | source)
XLA Modules:
  0.0 69.6 jit_solution(11833514996397186849)
XLA Ops:
  0.6 4.7 %own_states.1 = (f32[32,24,128]{2,1,0:T(8,128)}, f32[16,32,128]{2,1,0:T(8,128)}, f32[16,8,128]{2,1,0:T(8,128)}, f32[16,8,256]{2,1,0:T(8,128)}, bf16[2048,128]{1,0:T(8,128)(2,1)}, /*index=5*/bf16[2048,128]{1,0:T(8,128)(2,1)}) custom-call(bf16[256,2048]{1,0:T(8,128)(2,1)} %bitcast.21, bf16[256,2048]{1,0:T(8,128)(2,1)} %bitcast.15, bf16[4096,128]{1,0:T(8,128)(2,1)} %bitcast.27, ...), custom_call_target="tpu_custom_call" | custom-call | flops 800000000 | bytes 6000000 | tf_op jit(solution)/shard_map/own_states/pallas_call | solution.py:231
  5.4 11.4 %all-to-all-start = ((f32[32,24,128]{2,1,0:T(8,128)}), f32[32,24,128]{2,1,0:T(8,128)S(1)}, u32[]{:S(2)}, u32[]{:S(2)}) async-start(f32[32,24,128]{2,1,0:T(8,128)} %get-tuple-element.39), calls=%async_computation | async-start | bytes 786432 | tf_op jit(solution)/shard_map/all_to_all | solution.py:593
  16.7 8.2 %chunks_ascending.1 = (f32[128,2048]{1,0:T(8,128)}, f32[4,128,256]{2,1,0:T(8,128)}, f32[4,128,256]{2,1,0:T(8,128)}, f32[2048,256]{1,0:T(8,128)}) custom-call(bf16[256,2048]{1,0:T(8,128)(2,1)} %bitcast.22, bf16[256,2048]{1,0:T(8,128)(2,1)} %bitcast.16, bf16[2048,128]{1,0:T(8,128)(2,1)} %get-tuple-element.35.b_ref, bf16[2048,128]{1,0:T(8,128)(2,1)} %get-tuple-element.36.c_ref, ...), custom_call_target="tpu_custom_call" | custom-call | flops 3000000000 | bytes 8000000 | tf_op jit(solution)/shard_map/chunks_ascending/pallas_call | solution.py:380
  24.9 6.7 %all-to-all-done.got_ref = f32[32,24,128]{2,1,0:T(8,128)S(1)} async-done(((f32[32,24,128]{2,1,0:T(8,128)}), f32[32,24,128]{2,1,0:T(8,128)S(1)}, u32[]{:S(2)}, u32[]{:S(2)}) %all-to-all-start) | async-done | bytes 393248 | tf_op jit(solution)/shard_map/all_to_all | solution.py:593
  31.6 0.8 %scan_blocks.1 = f32[32,16,128]{2,1,0:T(8,128)} custom-call(f32[32,24,128]{2,1,0:T(8,128)S(1)} %all-to-all-done.got_ref), custom_call_target="tpu_custom_call" | custom-call | tf_op jit(solution)/shard_map/scan_blocks/pallas_call | solution.py:279
  32.4 4.8 %all-to-all-start.1 = ((f32[32,16,128]{2,1,0:T(8,128)}), f32[32,16,128]{2,1,0:T(8,128)S(1)}, u32[]{:S(2)}, u32[]{:S(2)}) async-start(f32[32,16,128]{2,1,0:T(8,128)} %scan_blocks.1), calls=%async_computation.1 | async-start | bytes 524288 | tf_op jit(solution)/shard_map/all_to_all | solution.py:596
  37.2 0.0 copy-start
  37.2 6.7 %chunks_descending.1 = (f32[4,128,256]{2,1,0:T(8,128)}, f32[4,128,256]{2,1,0:T(8,128)}, f32[2048,256]{1,0:T(8,128)}) custom-call(bf16[256,2048]{1,0:T(8,128)(2,1)} %bitcast.23, bf16[256,2048]{1,0:T(8,128)(2,1)} %bitcast.17, bf16[2048,128]{1,0:T(8,128)(2,1)} %get-tuple-element.36.c_ref, f32[16,32,128]{2,1,0:T(8,128)} %get-tuple-element.37.rows_ref, ...), custom_call_target="tpu_custom_call" | custom-call | flops 3000000000 | bytes 8000000 | tf_op jit(solution)/shard_map/chunks_descending/pallas_call | solution.py:426
  43.9 5.0 %all-to-all-done.1.bound_ref = f32[32,16,128]{2,1,0:T(8,128)S(1)} async-done(((f32[32,16,128]{2,1,0:T(8,128)}), f32[32,16,128]{2,1,0:T(8,128)S(1)}, u32[]{:S(2)}, u32[]{:S(2)}) %all-to-all-start.1) | async-done | bytes 262176 | tf_op jit(solution)/shard_map/all_to_all | solution.py:596
  48.9 0.0 copy-start.3
  49.0 0.0 copy-start.5
  49.0 0.4 out_send.1
  49.4 0.1 collective-permute-start
  49.5 0.4 in_send.1
  50.0 0.6 collective-permute-start.1
  50.5 0.0 copy-start.9
  50.5 0.0 copy-start.10
  50.6 0.0 copy-start.11
  50.6 0.7 keep.1.kept_ref
  51.3 0.7 %collective-permute-done.1.in_ref = f32[3,128,256]{2,1,0:T(8,128)S(1)} collective-permute-done((f32[3,128,256]{2,1,0:T(8,128)S(1)}, f32[3,128,256]{2,1,0:T(8,128)S(1)}, u32[]{:S(2)}, u32[]{:S(2)}) %collective-permute-start.1) | collective-permute-done | bytes 393248 | tf_op jit(solution)/shard_map/ppermute | solution.py:607
  52.0 0.0 collective-permute-done.out_ref
  52.0 0.1 sum_cores.1
  52.1 1.6 %collective-permute-start.3 = (f32[2,128,256]{2,1,0:T(8,128)S(1)}, f32[2,128,256]{2,1,0:T(8,128)S(1)}, u32[]{:S(2)}, u32[]{:S(2)}) collective-permute-start(f32[2,128,256]{2,1,0:T(8,128)S(1)} %get-tuple-element.61), channel_id=1, source_target_pairs={{0,2},{1,7},{2,0},{3,5},{4,6},{5,3},{6,4},{7,1},{8,10},{9,15},{10,... | collective-permute-start | bytes 786440 | tf_op jit(solution)/shard_map/ppermute | solution.py:615
  53.7 2.1 %collective-permute-start.4 = (f32[2,128,256]{2,1,0:T(8,128)S(1)}, f32[2,128,256]{2,1,0:T(8,128)S(1)}, u32[]{:S(2)}, u32[]{:S(2)}) collective-permute-start(f32[2,128,256]{2,1,0:T(8,128)S(1)} %get-tuple-element.62), channel_id=1, source_target_pairs={{0,6},{1,3},{2,4},{3,1},{4,2},{5,7},{6,0},{7,5},{8,14},{9,11},{10,... | collective-permute-start | bytes 786440 | tf_op jit(solution)/shard_map/ppermute | solution.py:615
  55.7 0.6 collective-permute-start.5
  56.4 8.3 %inputs_and_decay.1 = (bf16[256,2048]{1,0:T(8,128)(2,1)}, f32[4,2048]{1,0:T(4,128)}) custom-call(bf16[256,2048]{1,0:T(8,128)(2,1)S(1)} %bitcast.26, bf16[256,2048]{1,0:T(8,128)(2,1)S(1)} %bitcast.20, bf16[2048,128]{1,0:T(8,128)(2,1)S(1)} %copy-done.7, bf16[2048,128]{1,0:T(8,128)(2,1)S(1)} %copy-done.8, f32[16,32,128]{2,1,0:T(8,128)S(1)} %copy-done.9, ...), custom_call_target="tpu_custom_call" | custom-call | flops 6000000000 | bytes 12000000 | tf_op jit(solution)/shard_map/inputs_and_decay/pallas_call | solution.py:551
  64.7 0.0 collective-permute-start.2
  64.7 1.3 %collective-permute-done.2.late_ref = f32[128,256]{1,0:T(8,128)S(1)} collective-permute-done((f32[128,256]{1,0:T(8,128)S(1)}, f32[128,256]{1,0:T(8,128)S(1)}, u32[]{:S(2)}, u32[]{:S(2)}) %collective-permute-start.2) | collective-permute-done | bytes 131104 | tf_op jit(solution)/shard_map/ppermute | solution.py:620
  66.0 0.0 collective-permute-done.3.one_ref
  66.0 0.5 collective-permute-done.4.two_ref
  66.6 2.1 %collective-permute-done.5.far_ref = f32[2,128,256]{2,1,0:T(8,128)S(1)} collective-permute-done((f32[2,128,256]{2,1,0:T(8,128)S(1)}, f32[2,128,256]{2,1,0:T(8,128)S(1)}, u32[]{:S(2)}, u32[]{:S(2)}) %collective-permute-start.5) | collective-permute-done | bytes 262176 | tf_op jit(solution)/shard_map/ppermute | solution.py:615
  68.7 0.9 %merge.1 = (f32[512,128]{1,0:T(8,128)}, f32[512,128]{1,0:T(8,128)}) custom-call(f32[2,128,256]{2,1,0:T(8,128)S(1)} %get-tuple-element.59.own_ref, f32[128,256]{1,0:T(8,128)S(1)} %collective-permute-done.2.late_ref, f32[2,128,256]{2,1,0:T(8,128)S(1)} %collective-permute-done.3.one_ref, f32[2,128,256]{2,1,0:T(8,128)S(1)} %collective-permute-done.4.two_ref, ...), custom_call_target="tpu_custom_call" | custom-call | flops 500000000 | bytes 3000000 | tf_op jit(solution)/shard_map/merge/pallas_call | solution.py:492
  (20 shorter events, 0.0 us)
Async XLA Ops:
  5.4 26.3 %all-to-all-start = ((f32[32,24,128]{2,1,0:T(8,128)}), f32[32,24,128]{2,1,0:T(8,128)S(1)}, u32[]{:S(2)}, u32[]{:S(2)}) async-start(f32[32,24,128]{2,1,0:T(8,128)} %get-tuple-element.39), calls=%async_computation | async-start | bytes 786432 | tf_op jit(solution)/shard_map/all_to_all | solution.py:593
  32.4 16.5 %all-to-all-start.1 = ((f32[32,16,128]{2,1,0:T(8,128)}), f32[32,16,128]{2,1,0:T(8,128)S(1)}, u32[]{:S(2)}, u32[]{:S(2)}) async-start(f32[32,16,128]{2,1,0:T(8,128)} %scan_blocks.1), calls=%async_computation.1 | async-start | bytes 524288 | tf_op jit(solution)/shard_map/all_to_all | solution.py:596
  37.2 11.7 %copy-start = (bf16[2048,4,64]{0,2,1:T(8,128)(2,1)S(1)}, bf16[2048,4,64]{0,2,1:T(8,128)(2,1)}, u32[]{:S(2)}) copy-start(bf16[2048,4,64]{0,2,1:T(8,128)(2,1)} %param.9) | copy-start | bytes 3145732
  37.2 11.7 %copy-start.2 = (f32[16,8,128]{2,1,0:T(8,128)S(1)}, f32[16,8,128]{2,1,0:T(8,128)}, u32[]{:S(2)}) copy-start(f32[16,8,128]{2,1,0:T(8,128)} %get-tuple-element.48.edge_ref) | copy-start | bytes 196612
  37.2 11.7 %copy-start.4 = (f32[4,128,256]{2,1,0:T(8,128)S(1)}, f32[4,128,256]{2,1,0:T(8,128)}, u32[]{:S(2)}) copy-start(f32[4,128,256]{2,1,0:T(8,128)} %get-tuple-element.50.held_ref) | copy-start | bytes 1572868
  43.9 5.6 %copy-start.1 = (bf16[2048,4,64]{0,2,1:T(8,128)(2,1)S(1)}, bf16[2048,4,64]{0,2,1:T(8,128)(2,1)}, u32[]{:S(2)}) copy-start(bf16[2048,4,64]{0,2,1:T(8,128)(2,1)} %param.5) | copy-start | bytes 3145732
  43.9 5.6 %copy-start.6 = (f32[4,128,256]{2,1,0:T(8,128)S(1)}, f32[4,128,256]{2,1,0:T(8,128)}, u32[]{:S(2)}) copy-start(f32[4,128,256]{2,1,0:T(8,128)} %get-tuple-element.51.held_ref) | copy-start | bytes 1572868
  48.9 1.6 %copy-start.3 = (f32[4,128,256]{2,1,0:T(8,128)S(1)}, f32[4,128,256]{2,1,0:T(8,128)}, u32[]{:S(2)}) copy-start(f32[4,128,256]{2,1,0:T(8,128)} %get-tuple-element.58.out_ref) | copy-start | bytes 1572868
  49.0 1.6 %copy-start.5 = (f32[4,128,256]{2,1,0:T(8,128)S(1)}, f32[4,128,256]{2,1,0:T(8,128)}, u32[]{:S(2)}) copy-start(f32[4,128,256]{2,1,0:T(8,128)} %get-tuple-element.55.in_ref) | copy-start | bytes 1572868
  49.4 2.6 %collective-permute-start = (f32[4,128,256]{2,1,0:T(8,128)S(1)}, f32[4,128,256]{2,1,0:T(8,128)S(1)}, u32[]{:S(2)}, u32[]{:S(2)}) collective-permute-start(f32[4,128,256]{2,1,0:T(8,128)S(1)} %out_send.1), channel_id=1, source_target_pairs={{0,1},{1,0},{2,3},{3,2},{4,5},{5,4},{6,7},{7,6},{8,9},{9,8},{10,11... | collective-permute-start | bytes 1572872 | tf_op jit(solution)/shard_map/ppermute | solution.py:602
  50.0 2.0 %collective-permute-start.1 = (f32[3,128,256]{2,1,0:T(8,128)S(1)}, f32[3,128,256]{2,1,0:T(8,128)S(1)}, u32[]{:S(2)}, u32[]{:S(2)}) collective-permute-start(f32[3,128,256]{2,1,0:T(8,128)S(1)} %get-tuple-element.57), channel_id=1, source_target_pairs={{0,1},{1,0},{2,3},{3,2},{4,5},{5,4},{6,7},{7,6},{8,9},{9,8},{10,11... | collective-permute-start | bytes 1179656 | tf_op jit(solution)/shard_map/ppermute | solution.py:607
  50.5 5.9 %copy-start.7 = (bf16[2048,128]{1,0:T(8,128)(2,1)S(1)}, bf16[2048,128]{1,0:T(8,128)(2,1)}, u32[]{:S(2)}) copy-start(bf16[2048,128]{1,0:T(8,128)(2,1)} %get-tuple-element.35.b_ref) | copy-start | bytes 1572868
  50.5 5.9 %copy-start.8 = (bf16[2048,128]{1,0:T(8,128)(2,1)S(1)}, bf16[2048,128]{1,0:T(8,128)(2,1)}, u32[]{:S(2)}) copy-start(bf16[2048,128]{1,0:T(8,128)(2,1)} %get-tuple-element.36.c_ref) | copy-start | bytes 1572868
  50.5 5.9 %copy-start.9 = (f32[16,32,128]{2,1,0:T(8,128)S(1)}, f32[16,32,128]{2,1,0:T(8,128)}, u32[]{:S(2)}) copy-start(f32[16,32,128]{2,1,0:T(8,128)} %get-tuple-element.37.rows_ref) | copy-start | bytes 786436
  50.5 5.8 %copy-start.10 = (f32[16,8,256]{2,1,0:T(8,128)S(1)}, f32[16,8,256]{2,1,0:T(8,128)}, u32[]{:S(2)}) copy-start(f32[16,8,256]{2,1,0:T(8,128)} %get-tuple-element.38.lanes_ref) | copy-start | bytes 393220
  50.6 5.8 %copy-start.11 = (f32[2048,256]{1,0:T(8,128)S(1)}, f32[2048,256]{1,0:T(8,128)}, u32[]{:S(2)}) copy-start(f32[2048,256]{1,0:T(8,128)} %get-tuple-element.46.d_ref) | copy-start | bytes 6291460
  50.6 5.8 %copy-start.12 = (f32[2048,256]{1,0:T(8,128)S(1)}, f32[2048,256]{1,0:T(8,128)}, u32[]{:S(2)}) copy-start(f32[2048,256]{1,0:T(8,128)} %get-tuple-element.45.s_ref) | copy-start | bytes 6291460
  52.1 14.0 %collective-permute-start.3 = (f32[2,128,256]{2,1,0:T(8,128)S(1)}, f32[2,128,256]{2,1,0:T(8,128)S(1)}, u32[]{:S(2)}, u32[]{:S(2)}) collective-permute-start(f32[2,128,256]{2,1,0:T(8,128)S(1)} %get-tuple-element.61), channel_id=1, source_target_pairs={{0,2},{1,7},{2,0},{3,5},{4,6},{5,3},{6,4},{7,1},{8,10},{9,15},{10,... | collective-permute-start | bytes 786440 | tf_op jit(solution)/shard_map/ppermute | solution.py:615
  53.7 12.9 %collective-permute-start.4 = (f32[2,128,256]{2,1,0:T(8,128)S(1)}, f32[2,128,256]{2,1,0:T(8,128)S(1)}, u32[]{:S(2)}, u32[]{:S(2)}) collective-permute-start(f32[2,128,256]{2,1,0:T(8,128)S(1)} %get-tuple-element.62), channel_id=1, source_target_pairs={{0,6},{1,3},{2,4},{3,1},{4,2},{5,7},{6,0},{7,5},{8,14},{9,11},{10,... | collective-permute-start | bytes 786440 | tf_op jit(solution)/shard_map/ppermute | solution.py:615
  55.7 12.9 %collective-permute-start.5 = (f32[2,128,256]{2,1,0:T(8,128)S(1)}, f32[2,128,256]{2,1,0:T(8,128)S(1)}, u32[]{:S(2)}, u32[]{:S(2)}) collective-permute-start(f32[2,128,256]{2,1,0:T(8,128)S(1)} %get-tuple-element.63), channel_id=1, source_target_pairs={{0,4},{1,5},{2,6},{3,7},{4,0},{5,1},{6,2},{7,3},{8,12},{9,13},{10,... | collective-permute-start | bytes 786440 | tf_op jit(solution)/shard_map/ppermute | solution.py:615
  64.7 1.3 %collective-permute-start.2 = (f32[128,256]{1,0:T(8,128)S(1)}, f32[128,256]{1,0:T(8,128)S(1)}, u32[]{:S(2)}, u32[]{:S(2)}) collective-permute-start(f32[128,256]{1,0:T(8,128)S(1)} %get-tuple-element.60), channel_id=1, source_target_pairs={{0,1},{1,0},{2,3},{3,2},{4,5},{5,4},{6,7},{7,6},{8,9},{9,8},{10,11... | collective-permute-start | bytes 393224 | tf_op jit(solution)/shard_map/ppermute | solution.py:620

commit v6 on v4

--- a/solution.py
+++ b/solution.py
@@ -457,9 +457,12 @@
         yield i, held[to] + (first[:STATE] + (first[STATE:] + dot_nn(edge[0], near_lo)))
 
 
-def send_out_kernel(bound_ref, edge_ref, y_ref, held_ref, out_ref):
+def send_out_kernel(bound_ref, edge_ref, y_ref, held_ref, far_ref, own_ref):
     for i, block in blocks_of(1, 0, 0, bound_ref, edge_ref, y_ref, held_ref):
-        out_ref[i] = block
+        if i == 0:
+            own_ref[...] = block
+        else:
+            far_ref[i - 1] = block
 
 
 def send_in_kernel(bound_ref, edge_ref, x_ref, held_ref, far_ref, own_ref):
@@ -481,10 +484,10 @@
     second = lax.axis_index("head") % 2
     own_ref, rest = outs[0], outs[1:]
     own_ref[0] = kept_ref[0, 0]
-    own_ref[1] = kept_ref[0, 1] + out_ref[0]
+    own_ref[1] = kept_ref[0, 1]
     for ref, m in zip(rest, (1 + 2 * second, 3 - 2 * second, 2)):
         ref[0] = kept_ref[m, 0] + in_ref[m - 1]
-        ref[1] = kept_ref[m, 1] + out_ref[m]
+        ref[1] = kept_ref[m, 1] + out_ref[m - 1]
 
 
 def in_vmem(name, kernel, shapes, *operands):
@@ -571,14 +574,13 @@
     )(x, y, b, c, rows, lanes, bound, s, d)
 
 
-def merge_kernel(own_ref, late_ref, one_ref, two_ref, far_ref, in_ref, out_ref):
+def merge_kernel(own_ref, late_in_ref, late_out_ref, one_ref, two_ref, far_ref, in_ref, out_ref):
     index = lax.axis_index("head")
     group, second = index // 4, index % 2 == 1
     for t, ref in enumerate((in_ref, out_ref)):
         one, two = one_ref[t], two_ref[t]
         own = own_ref[t] + jnp.where(second, two, one)
-        if t == 0:
-            own = own + late_ref[...]
+        own = own + (late_out_ref if t else late_in_ref)[...]
         ref[pl.ds(group, HALF, stride=2), :] = own.T
         ref[pl.ds(1 - group, HALF, stride=2), :] = (far_ref[t] + jnp.where(second, one, two)).T
 
@@ -598,14 +600,15 @@
     bound, d = lax.optimization_barrier((bound, d))
     pair = [(i, i ^ 1) for i in range(8)]
     block = (STATE, HALF)
-    (sent_out,) = in_vmem("out_send", send_out_kernel, [(4, *block)], bound, edge, y, dc_send)
+    sent_out, own_out = in_vmem(
+        "out_send", send_out_kernel, [(3, *block), block], bound, edge, y, dc_send
+    )
     got_out = lax.ppermute(sent_out, "head", pair)
     db_send, sent_out = lax.optimization_barrier((db_send, sent_out))
     sent_in, sent_own = in_vmem(
         "in_send", send_in_kernel, [(3, *block), block], bound, edge, x, db_send
     )
     got_in = lax.ppermute(sent_in, "head", pair)
-    late = lax.ppermute(sent_own, "head", pair)
     dc_keep, sent_in = lax.optimization_barrier((dc_keep, sent_in))
     (kept,) = in_vmem(
         "keep", keep_kernel, [(4, 2, *block)], bound, edge, x, y, db_keep, dc_keep
@@ -617,8 +620,10 @@
         for part, hop in zip(parts[1:], hops)
     ]
     grad_x, grad_log = last_pass(x, y, b, c, rows, lanes, bound, s, d)
+    sent_own, own_out, grad_log = lax.optimization_barrier((sent_own, own_out, grad_log))
+    late = [lax.ppermute(part, "head", pair) for part in (sent_own, own_out)]
     grad_in, grad_out = in_vmem(
-        "merge", merge_kernel, [(2 * HALF, STATE)] * 2, parts[0], late, *moved
+        "merge", merge_kernel, [(2 * HALF, STATE)] * 2, parts[0], *late, *moved
     )
     return (
         jnp.transpose(grad_x.reshape(HEADS_HERE, WIDTH, TOK), (2, 0, 1)),

time: 70.7 us -> 72.8 us (1.030)
  local copies, waits for them, and re-layouts: 0.06 us -> 2.13 us
    unnamed x26, local copies, waits for them, and re-layouts: 0.06 us -> 2.13 us
    ppermute x3, waiting for transfers between devices: 3.98 us -> 2.32 us  [local(): lax.ppermute(part, 'head', [(i, i ^ hop[i % 2]) for i in range(8)])]
    ppermute x1 -> x2, waiting for transfers between devices: 0.01 us -> 1.02 us  [local(): late = [lax.ppermute(part, 'head', pair) for part in (sent_own, own_out)]]
  transfers between devices with their start and end apart: 8 -> 9, of which waited for: 5 -> 8; matrix products, arithmetic and copies ran while one was open for 0% -> 0% of each run, Pallas kernels for 35% -> 33%
where the time goes in v6:
time: 72.8 us; the launch traced here: 71.8 us
  Pallas kernels  31.3 us (43%)
  starting transfers between devices  21.5 us (30%)
  waiting for transfers between devices  16 us (22%)
  local copies, waits for them, and re-layouts  2.13 us (3%)
  between operations  0.8 us (1%)
    all_to_all x1, starting transfers between devices, local(): got = lax.all_to_all(message, 'seq', 0, 0)  11.4 us
    pallas_call x1, Pallas kernels, last_pass(): pl.pallas_call(last_kernel, grid=(CHUNKS // PER5,), in_specs=chunk_specs(...  8.26 us
    pallas_call x1, Pallas kernels, ascend(): pl.pallas_call(ascend_kernel, grid=(CHUNKS // PER2,), in_specs=chunk_spec...  8.2 us
    pallas_call x1, Pallas kernels, descend(): pl.pallas_call(descend_kernel, grid=(steps,), in_specs=specs[:2] + specs[...  6.73 us
    all_to_all x1, waiting for transfers between devices, local(): got = lax.all_to_all(message, 'seq', 0, 0)  6.68 us
    all_to_all x1, waiting for transfers between devices, local(): bound = lax.all_to_all(scan_blocks(got), 'seq', 0, 0)  4.97 us
    all_to_all x1, starting transfers between devices, local(): bound = lax.all_to_all(scan_blocks(got), 'seq', 0, 0)  4.78 us
    pallas_call x1, Pallas kernels, first_pass(): pl.pallas_call(first_kernel, in_specs=[hbm] * 5, out_specs=[hbm] * 6, out...  4.74 us
  transfers between devices with their start and end apart: 9, of which 8 were waited for; matrix products, arithmetic and copies ran while one was open for 0% of the time, Pallas kernels for 33%

profile of v6, /device:TPU:32, one launch (start us, length us, event | category | flops | bytes accessed | tf_op | source)
XLA Modules:
  0.0 71.8 jit_solution(8795150815764365991)
XLA Ops:
  0.6 4.7 %own_states.1 = (f32[32,24,128]{2,1,0:T(8,128)}, f32[16,32,128]{2,1,0:T(8,128)}, f32[16,8,128]{2,1,0:T(8,128)}, f32[16,8,256]{2,1,0:T(8,128)}, bf16[2048,128]{1,0:T(8,128)(2,1)}, /*index=5*/bf16[2048,128]{1,0:T(8,128)(2,1)}) custom-call(bf16[256,2048]{1,0:T(8,128)(2,1)} %bitcast.15, bf16[256,2048]{1,0:T(8,128)(2,1)} %bitcast.21, bf16[4096,128]{1,0:T(8,128)(2,1)} %bitcast.27, ...), custom_call_target="tpu_custom_call" | custom-call | flops 800000000 | bytes 6000000 | tf_op jit(solution)/shard_map/own_states/pallas_call | solution.py:231
  5.4 11.4 %all-to-all-start = ((f32[32,24,128]{2,1,0:T(8,128)}), f32[32,24,128]{2,1,0:T(8,128)S(1)}, u32[]{:S(2)}, u32[]{:S(2)}) async-start(f32[32,24,128]{2,1,0:T(8,128)} %get-tuple-element.42), calls=%async_computation | async-start | bytes 786432 | tf_op jit(solution)/shard_map/all_to_all | solution.py:595
  16.8 8.2 %chunks_ascending.1 = (f32[128,2048]{1,0:T(8,128)}, f32[4,128,256]{2,1,0:T(8,128)}, f32[4,128,256]{2,1,0:T(8,128)}, f32[2048,256]{1,0:T(8,128)}) custom-call(bf16[256,2048]{1,0:T(8,128)(2,1)} %bitcast.16, bf16[256,2048]{1,0:T(8,128)(2,1)} %bitcast.22, bf16[2048,128]{1,0:T(8,128)(2,1)} %get-tuple-element.38.b_ref, bf16[2048,128]{1,0:T(8,128)(2,1)} %get-tuple-element.39.c_ref, ...), custom_call_target="tpu_custom_call" | custom-call | flops 3000000000 | bytes 8000000 | tf_op jit(solution)/shard_map/chunks_ascending/pallas_call | solution.py:380
  25.0 6.7 %all-to-all-done.got_ref = f32[32,24,128]{2,1,0:T(8,128)S(1)} async-done(((f32[32,24,128]{2,1,0:T(8,128)}), f32[32,24,128]{2,1,0:T(8,128)S(1)}, u32[]{:S(2)}, u32[]{:S(2)}) %all-to-all-start) | async-done | bytes 393248 | tf_op jit(solution)/shard_map/all_to_all | solution.py:595
  31.6 0.8 %scan_blocks.1 = f32[32,16,128]{2,1,0:T(8,128)} custom-call(f32[32,24,128]{2,1,0:T(8,128)S(1)} %all-to-all-done.got_ref), custom_call_target="tpu_custom_call" | custom-call | tf_op jit(solution)/shard_map/scan_blocks/pallas_call | solution.py:279
  32.4 4.8 %all-to-all-start.1 = ((f32[32,16,128]{2,1,0:T(8,128)}), f32[32,16,128]{2,1,0:T(8,128)S(1)}, u32[]{:S(2)}, u32[]{:S(2)}) async-start(f32[32,16,128]{2,1,0:T(8,128)} %scan_blocks.1), calls=%async_computation.1 | async-start | bytes 524288 | tf_op jit(solution)/shard_map/all_to_all | solution.py:598
  37.2 0.0 copy-start.1
  37.2 0.0 copy-start
  37.2 6.7 %chunks_descending.1 = (f32[4,128,256]{2,1,0:T(8,128)}, f32[4,128,256]{2,1,0:T(8,128)}, f32[2048,256]{1,0:T(8,128)}) custom-call(bf16[256,2048]{1,0:T(8,128)(2,1)} %bitcast.17, bf16[256,2048]{1,0:T(8,128)(2,1)} %bitcast.23, bf16[2048,128]{1,0:T(8,128)(2,1)} %get-tuple-element.39.c_ref, f32[16,32,128]{2,1,0:T(8,128)} %get-tuple-element.40.rows_ref, ...), custom_call_target="tpu_custom_call" | custom-call | flops 3000000000 | bytes 8000000 | tf_op jit(solution)/shard_map/chunks_descending/pallas_call | solution.py:426
  44.0 5.0 %all-to-all-done.1.bound_ref = f32[32,16,128]{2,1,0:T(8,128)S(1)} async-done(((f32[32,16,128]{2,1,0:T(8,128)}), f32[32,16,128]{2,1,0:T(8,128)S(1)}, u32[]{:S(2)}, u32[]{:S(2)}) %all-to-all-start.1) | async-done | bytes 262176 | tf_op jit(solution)/shard_map/all_to_all | solution.py:598
  49.0 1.0 %copy-done.5 = f32[4,128,256]{2,1,0:T(8,128)S(1)} copy-done((f32[4,128,256]{2,1,0:T(8,128)S(1)}, f32[4,128,256]{2,1,0:T(8,128)}, u32[]{:S(2)}) %copy-start.5) | copy-done | bytes 524312
  50.0 0.4 out_send.1
  50.4 1.0 %copy-done.6 = f32[4,128,256]{2,1,0:T(8,128)S(1)} copy-done((f32[4,128,256]{2,1,0:T(8,128)S(1)}, f32[4,128,256]{2,1,0:T(8,128)}, u32[]{:S(2)}) %copy-start.6) | copy-done | bytes 524312
  51.5 0.4 in_send.1
  51.9 0.1 collective-permute-start.1
  52.0 0.5 collective-permute-start
  52.5 0.0 copy-start.9
  52.6 0.7 keep.1.kept_ref
  53.2 0.5 collective-permute-done.1.in_ref
  53.7 0.6 collective-permute-done.out_ref
  54.3 0.1 sum_cores.1
  54.4 1.6 %collective-permute-start.4 = (f32[2,128,256]{2,1,0:T(8,128)S(1)}, f32[2,128,256]{2,1,0:T(8,128)S(1)}, u32[]{:S(2)}, u32[]{:S(2)}) collective-permute-start(f32[2,128,256]{2,1,0:T(8,128)S(1)} %get-tuple-element.67), channel_id=1, source_target_pairs={{0,2},{1,7},{2,0},{3,5},{4,6},{5,3},{6,4},{7,1},{8,10},{9,15},{10,... | collective-permute-start | bytes 786440 | tf_op jit(solution)/shard_map/ppermute | solution.py:619
  56.0 2.1 %collective-permute-start.5 = (f32[2,128,256]{2,1,0:T(8,128)S(1)}, f32[2,128,256]{2,1,0:T(8,128)S(1)}, u32[]{:S(2)}, u32[]{:S(2)}) collective-permute-start(f32[2,128,256]{2,1,0:T(8,128)S(1)} %get-tuple-element.68), channel_id=1, source_target_pairs={{0,6},{1,3},{2,4},{3,1},{4,2},{5,7},{6,0},{7,5},{8,14},{9,11},{10,... | collective-permute-start | bytes 786440 | tf_op jit(solution)/shard_map/ppermute | solution.py:619
  58.1 0.6 collective-permute-start.6
  58.7 8.3 %inputs_and_decay.1 = (bf16[256,2048]{1,0:T(8,128)(2,1)}, f32[4,2048]{1,0:T(4,128)}) custom-call(bf16[256,2048]{1,0:T(8,128)(2,1)S(1)} %bitcast.20, bf16[256,2048]{1,0:T(8,128)(2,1)S(1)} %bitcast.26, bf16[2048,128]{1,0:T(8,128)(2,1)S(1)} %copy-done.7, bf16[2048,128]{1,0:T(8,128)(2,1)S(1)} %copy-done.8, f32[16,32,128]{2,1,0:T(8,128)S(1)} %copy-done.9, ...), custom_call_target="tpu_custom_call" | custom-call | flops 6000000000 | bytes 12000000 | tf_op jit(solution)/shard_map/inputs_and_decay/pallas_call | solution.py:554
  67.0 0.0 collective-permute-start.2
  67.0 0.5 collective-permute-start.3
  67.5 0.8 %collective-permute-done.2.late_in_ref = f32[128,256]{1,0:T(8,128)S(1)} collective-permute-done((f32[128,256]{1,0:T(8,128)S(1)}, f32[128,256]{1,0:T(8,128)S(1)}, u32[]{:S(2)}, u32[]{:S(2)}) %collective-permute-start.2) | collective-permute-done | bytes 131104 | tf_op jit(solution)/shard_map/ppermute | solution.py:624
  68.3 0.2 collective-permute-done.3.late_out_ref
  68.5 0.2 collective-permute-done.5.two_ref
  68.7 2.1 %collective-permute-done.6.far_ref = f32[2,128,256]{2,1,0:T(8,128)S(1)} collective-permute-done((f32[2,128,256]{2,1,0:T(8,128)S(1)}, f32[2,128,256]{2,1,0:T(8,128)S(1)}, u32[]{:S(2)}, u32[]{:S(2)}) %collective-permute-start.6) | collective-permute-done | bytes 262176 | tf_op jit(solution)/shard_map/ppermute | solution.py:619
  70.8 0.9 %merge.1 = (f32[512,128]{1,0:T(8,128)}, f32[512,128]{1,0:T(8,128)}) custom-call(f32[2,128,256]{2,1,0:T(8,128)S(1)} %get-tuple-element.64.own_ref, f32[128,256]{1,0:T(8,128)S(1)} %collective-permute-done.2.late_in_ref, f32[128,256]{1,0:T(8,128)S(1)} %collective-permute-done.3.late_out_ref, f32[2,128,256]{2,1,0:T(8,128)S(1)} %collective-permute-done.4.one_ref, ...), custom_call_target="tpu_custom_call" | custom-call | flops 500000000 | bytes 3000000 | tf_op jit(solution)/shard_map/merge/pallas_call | solution.py:495
  (22 shorter events, 0.0 us)
Async XLA Ops:
  5.4 26.2 %all-to-all-start = ((f32[32,24,128]{2,1,0:T(8,128)}), f32[32,24,128]{2,1,0:T(8,128)S(1)}, u32[]{:S(2)}, u32[]{:S(2)}) async-start(f32[32,24,128]{2,1,0:T(8,128)} %get-tuple-element.42), calls=%async_computation | async-start | bytes 786432 | tf_op jit(solution)/shard_map/all_to_all | solution.py:595
  32.4 16.5 %all-to-all-start.1 = ((f32[32,16,128]{2,1,0:T(8,128)}), f32[32,16,128]{2,1,0:T(8,128)S(1)}, u32[]{:S(2)}, u32[]{:S(2)}) async-start(f32[32,16,128]{2,1,0:T(8,128)} %scan_blocks.1), calls=%async_computation.1 | async-start | bytes 524288 | tf_op jit(solution)/shard_map/all_to_all | solution.py:598
  37.2 11.7 %copy-start.1 = (bf16[2048,4,64]{0,2,1:T(8,128)(2,1)S(1)}, bf16[2048,4,64]{0,2,1:T(8,128)(2,1)}, u32[]{:S(2)}) copy-start(bf16[2048,4,64]{0,2,1:T(8,128)(2,1)} %param.9) | copy-start | bytes 3145732
  37.2 11.7 %copy-start.2 = (f32[16,8,128]{2,1,0:T(8,128)S(1)}, f32[16,8,128]{2,1,0:T(8,128)}, u32[]{:S(2)}) copy-start(f32[16,8,128]{2,1,0:T(8,128)} %get-tuple-element.51.edge_ref) | copy-start | bytes 196612
  37.2 13.2 %copy-start = (bf16[2048,4,64]{0,2,1:T(8,128)(2,1)S(1)}, bf16[2048,4,64]{0,2,1:T(8,128)(2,1)}, u32[]{:S(2)}) copy-start(bf16[2048,4,64]{0,2,1:T(8,128)(2,1)} %param.5) | copy-start | bytes 3145732
  44.0 8.5 %copy-start.3 = (f32[4,128,256]{2,1,0:T(8,128)S(1)}, f32[4,128,256]{2,1,0:T(8,128)}, u32[]{:S(2)}) copy-start(f32[4,128,256]{2,1,0:T(8,128)} %get-tuple-element.63.out_ref) | copy-start | bytes 1572868
  44.0 8.5 %copy-start.4 = (f32[4,128,256]{2,1,0:T(8,128)S(1)}, f32[4,128,256]{2,1,0:T(8,128)}, u32[]{:S(2)}) copy-start(f32[4,128,256]{2,1,0:T(8,128)} %get-tuple-element.60.in_ref) | copy-start | bytes 1572868
  48.9 1.0 %copy-start.5 = (f32[4,128,256]{2,1,0:T(8,128)S(1)}, f32[4,128,256]{2,1,0:T(8,128)}, u32[]{:S(2)}) copy-start(f32[4,128,256]{2,1,0:T(8,128)} %get-tuple-element.53.held_ref) | copy-start | bytes 1572868
  50.4 1.0 %copy-start.6 = (f32[4,128,256]{2,1,0:T(8,128)S(1)}, f32[4,128,256]{2,1,0:T(8,128)}, u32[]{:S(2)}) copy-start(f32[4,128,256]{2,1,0:T(8,128)} %get-tuple-element.55.held_ref) | copy-start | bytes 1572868
  51.9 1.8 %collective-permute-start.1 = (f32[3,128,256]{2,1,0:T(8,128)S(1)}, f32[3,128,256]{2,1,0:T(8,128)S(1)}, u32[]{:S(2)}, u32[]{:S(2)}) collective-permute-start(f32[3,128,256]{2,1,0:T(8,128)S(1)} %get-tuple-element.62), channel_id=1, source_target_pairs={{0,1},{1,0},{2,3},{3,2},{4,5},{5,4},{6,7},{7,6},{8,9},{9,8},{10,11... | collective-permute-start | bytes 1179656 | tf_op jit(solution)/shard_map/ppermute | solution.py:611
  52.0 2.3 %collective-permute-start = (f32[3,128,256]{2,1,0:T(8,128)S(1)}, f32[3,128,256]{2,1,0:T(8,128)S(1)}, u32[]{:S(2)}, u32[]{:S(2)}) collective-permute-start(f32[3,128,256]{2,1,0:T(8,128)S(1)} %get-tuple-element.54), channel_id=1, source_target_pairs={{0,1},{1,0},{2,3},{3,2},{4,5},{5,4},{6,7},{7,6},{8,9},{9,8},{10,11... | collective-permute-start | bytes 1179656 | tf_op jit(solution)/shard_map/ppermute | solution.py:606
  52.5 6.2 %copy-start.7 = (bf16[2048,128]{1,0:T(8,128)(2,1)S(1)}, bf16[2048,128]{1,0:T(8,128)(2,1)}, u32[]{:S(2)}) copy-start(bf16[2048,128]{1,0:T(8,128)(2,1)} %get-tuple-element.38.b_ref) | copy-start | bytes 1572868
  52.5 6.2 %copy-start.8 = (bf16[2048,128]{1,0:T(8,128)(2,1)S(1)}, bf16[2048,128]{1,0:T(8,128)(2,1)}, u32[]{:S(2)}) copy-start(bf16[2048,128]{1,0:T(8,128)(2,1)} %get-tuple-element.39.c_ref) | copy-start | bytes 1572868
  52.5 6.2 %copy-start.9 = (f32[16,32,128]{2,1,0:T(8,128)S(1)}, f32[16,32,128]{2,1,0:T(8,128)}, u32[]{:S(2)}) copy-start(f32[16,32,128]{2,1,0:T(8,128)} %get-tuple-element.40.rows_ref) | copy-start | bytes 786436
  52.5 6.2 %copy-start.10 = (f32[16,8,256]{2,1,0:T(8,128)S(1)}, f32[16,8,256]{2,1,0:T(8,128)}, u32[]{:S(2)}) copy-start(f32[16,8,256]{2,1,0:T(8,128)} %get-tuple-element.41.lanes_ref) | copy-start | bytes 393220
  52.5 6.1 %copy-start.11 = (f32[2048,256]{1,0:T(8,128)S(1)}, f32[2048,256]{1,0:T(8,128)}, u32[]{:S(2)}) copy-start(f32[2048,256]{1,0:T(8,128)} %get-tuple-element.49.d_ref) | copy-start | bytes 6291460
  52.5 6.1 %copy-start.12 = (f32[2048,256]{1,0:T(8,128)S(1)}, f32[2048,256]{1,0:T(8,128)}, u32[]{:S(2)}) copy-start(f32[2048,256]{1,0:T(8,128)} %get-tuple-element.48.s_ref) | copy-start | bytes 6291460
  54.4 14.1 %collective-permute-start.4 = (f32[2,128,256]{2,1,0:T(8,128)S(1)}, f32[2,128,256]{2,1,0:T(8,128)S(1)}, u32[]{:S(2)}, u32[]{:S(2)}) collective-permute-start(f32[2,128,256]{2,1,0:T(8,128)S(1)} %get-tuple-element.67), channel_id=1, source_target_pairs={{0,2},{1,7},{2,0},{3,5},{4,6},{5,3},{6,4},{7,1},{8,10},{9,15},{10,... | collective-permute-start | bytes 786440 | tf_op jit(solution)/shard_map/ppermute | solution.py:619
  56.0 12.8 %collective-permute-start.5 = (f32[2,128,256]{2,1,0:T(8,128)S(1)}, f32[2,128,256]{2,1,0:T(8,128)S(1)}, u32[]{:S(2)}, u32[]{:S(2)}) collective-permute-start(f32[2,128,256]{2,1,0:T(8,128)S(1)} %get-tuple-element.68), channel_id=1, source_target_pairs={{0,6},{1,3},{2,4},{3,1},{4,2},{5,7},{6,0},{7,5},{8,14},{9,11},{10,... | collective-permute-start | bytes 786440 | tf_op jit(solution)/shard_map/ppermute | solution.py:619
  58.1 12.7 %collective-permute-start.6 = (f32[2,128,256]{2,1,0:T(8,128)S(1)}, f32[2,128,256]{2,1,0:T(8,128)S(1)}, u32[]{:S(2)}, u32[]{:S(2)}) collective-permute-start(f32[2,128,256]{2,1,0:T(8,128)S(1)} %get-tuple-element.69), channel_id=1, source_target_pairs={{0,4},{1,5},{2,6},{3,7},{4,0},{5,1},{6,2},{7,3},{8,12},{9,13},{10,... | collective-permute-start | bytes 786440 | tf_op jit(solution)/shard_map/ppermute | solution.py:619
  67.0 1.3 %collective-permute-start.2 = (f32[128,256]{1,0:T(8,128)S(1)}, f32[128,256]{1,0:T(8,128)S(1)}, u32[]{:S(2)}, u32[]{:S(2)}) collective-permute-start(f32[128,256]{1,0:T(8,128)S(1)} %get-tuple-element.65), channel_id=1, source_target_pairs={{0,1},{1,0},{2,3},{3,2},{4,5},{5,4},{6,7},{7,6},{8,9},{9,8},{10,11... | collective-permute-start | bytes 393224 | tf_op jit(solution)/shard_map/ppermute | solution.py:624
  67.0 1.5 %collective-permute-start.3 = (f32[128,256]{1,0:T(8,128)S(1)}, f32[128,256]{1,0:T(8,128)S(1)}, u32[]{:S(2)}, u32[]{:S(2)}) collective-permute-start(f32[128,256]{1,0:T(8,128)S(1)} %get-tuple-element.66), channel_id=1, source_target_pairs={{0,1},{1,0},{2,3},{3,2},{4,5},{5,4},{6,7},{7,6},{8,9},{9,8},{10,11... | collective-permute-start | bytes 393224 | tf_op jit(solution)/shard_map/ppermute | solution.py:624
